TPU v7x, 512 devices: a whole 4x4x16 slice. The times are simulated.
512 devices in a mesh: dp: 32 (over z, core), mp: 16 (over x, y).
Axes of the slice: x: 4, y: 4, z: 16, core: 2. Of those that a mesh axis runs over, the one named last changes fastest.
Arguments:
- acts: bfloat16 [65536, 8192], P('dp', 'mp'), may hold values from -54 to 54, as said below
- grads_out: bfloat16 [65536, 8192], P('dp', 'mp'), may hold values from -54 to 54, as said below
- panel_owner: int32 [32], replicated, may hold values from 0 to 31, each once
Outputs:
- update: float32 [16, 512, 512], P(None, 'dp', 'mp')
Inputs may be any that keep to these rules, and one draw needn't show every extreme that they name: acts: every entry finite. grads_out: every entry finite. `panel_owner`: a permutation of the panels.
All inputs are finite; a program needn't handle non-finite values.
Results may differ from a plain program's by a relative error of at most 0.0003.
Values sent between devices are 32-bit elements; how exact they have to be, the bound alone decides.
No kernel may reach another device: no remote copies, remote signals or barrier semaphores. Data moves between devices by JAX's collectives and lax.ppermute only.
A program may use at most 64 MiB of HBM per device.

v0:
```python
import jax
import jax.numpy as jnp
from jax import lax
from jax.sharding import PartitionSpec as P


def batched(left, right):
    return jnp.einsum("kij,kjl->kil", left, right, precision=lax.Precision.HIGHEST)


def reorder(gathered, inverse, width):
    ordered = gathered[inverse]
    moved = jnp.moveaxis(ordered, 0, -3)
    return moved.reshape(moved.shape[:-3] + (width, width))


def per_device(acts, grads_out, panel_owner):
    width = acts.shape[1]
    count_dp = lax.axis_size("dp")
    rows = width // count_dp
    my_panel = panel_owner[lax.axis_index("dp")]
    inverse = (
        jnp.zeros((count_dp,), jnp.int32).at[panel_owner].set(jnp.arange(count_dp, dtype=jnp.int32))
    )
    part_grad = jnp.einsum("tb,tc->bc", acts, grads_out, preferred_element_type=jnp.float32)
    part_low = part_grad.astype(jnp.bfloat16)
    left_part = jnp.einsum("ik,jk->ij", part_low, part_low, preferred_element_type=jnp.float32)
    right_part = jnp.einsum("ki,kj->ij", part_low, part_low, preferred_element_type=jnp.float32)
    stacked = jnp.stack(
        [
            left_part.reshape(count_dp, rows, width),
            right_part.reshape(count_dp, rows, width),
            part_grad.reshape(count_dp, rows, width),
        ],
        axis=1,
    )
    owned = lax.psum_scatter(stacked[panel_owner], "dp", scatter_dimension=0, tiled=True)[0]
    factor_rows = owned[:2]
    grad_rows = owned[2]

    def assemble(panel_pair):
        gathered = lax.all_gather(panel_pair[None], "dp", axis=0, tiled=True)
        return reorder(gathered, inverse, width)

    row_ids = jnp.arange(rows, dtype=jnp.int32)[:, None] + my_panel * rows
    col_ids = jnp.arange(width, dtype=jnp.int32)[None, :]
    eye_rows = (row_ids == col_ids).astype(jnp.float32)[None]
    squares = jnp.sum(factor_rows * factor_rows, axis=(1, 2))
    norm_f = jnp.sqrt(lax.psum(squares, "dp") + 1e-06)
    iter_m = factor_rows / norm_f[:, None, None]
    iter_z = (5.0 * eye_rows - iter_m) / 4.0
    whole_z = assemble(iter_z)
    iter_x = norm_f[:, None, None] ** (-0.25) * iter_z
    square_rows = batched(iter_z, whole_z)
    whole_square = assemble(square_rows)
    fourth_rows = batched(square_rows, whole_square)
    whole_fourth = assemble(fourth_rows)
    iter_m = batched(iter_m, whole_fourth)
    iter_z = (5.0 * eye_rows - iter_m) / 4.0
    whole_z = assemble(iter_z)
    iter_x = batched(iter_x, whole_z)
    whole_grad = reorder(lax.all_gather(grad_rows[None], "dp", axis=0, tiled=True), inverse, width)
    whole_right = reorder(lax.all_gather(iter_x[1][None], "dp", axis=0, tiled=True), inverse, width)
    mixed_rows = jnp.matmul(iter_x[0], whole_grad, precision=lax.Precision.HIGHEST)
    precond_rows = jnp.matmul(mixed_rows, whole_right, precision=lax.Precision.HIGHEST)
    total_sq = lax.psum(jnp.sum(precond_rows * precond_rows), "dp")
    scale_rms = jnp.sqrt(total_sq / (width * width) + 1e-06)
    scaled = precond_rows / scale_rms
    return lax.all_to_all(scaled[None], "mp", split_axis=2, concat_axis=0, tiled=True)


def solution(mesh):
    return jax.shard_map(
        per_device,
        mesh=mesh,
        in_specs=(P("dp", "mp"), P("dp", "mp"), P()),
        out_specs=P(None, "dp", "mp"),
        check_vma=False,
    )
```

profile of v0, /device:TPU:1, one launch (start us, length us, event | category | flops | bytes accessed | tf_op | source)
XLA Modules:
  0.0 698.2 jit_solution(17170587361085150991)
XLA Ops:
  6.5 1.6 copy-done
  8.1 2.9 fusion.21
  11.0 0.5 fusion.3
  11.5 0.5 fusion.1
  12.0 2.0 pad_maximum_fusion
  14.0 4.3 gather_fusion
  18.3 0.0 all-gather.11.cloned.1.call-start
  18.3 0.6 dynamic_slice.3
  19.6 113.2 %reduce-scatter.2.cloned.1.call-done = f32[1,3,16,512]{3,2,1,0:T(8,128)} async-done(((f32[32,3,16,512]{3,2,1,0:T(8,128)}), f32[1,3,16,512]{3,2,1,0:T(8,128)}) %reduce-scatter.2.cloned.1.call-update) | async-done | bytes 98320 | tf_op jit(solution)/shard_map/reduce_scatter | solution.py:37
  132.7 0.9 fusion.5
  133.7 0.1 fusion.17
  133.8 48.7 %psum.14 = f32[2]{0:T(128)S(1)} all-reduce(f32[2]{0:T(128)S(1)} %fusion.5), channel_id=1, replica_groups=mesh['dp'=32,'mp'=16] {'dp'}, use_global_device_ids=true, to_apply=%region_2.0 | all-reduce | flops 2 | bytes 16 | tf_op jit(solution)/shard_map/psum | solution.py:49
  182.5 1.6 subtract_multiply_fusion
  184.1 0.7 scatter_custom_fusion
  184.9 71.6 %all-gather.11.cloned.1.call-done = f32[32,2,16,512]{3,2,1,0:T(8,128)} async-done(((f32[1,2,16,512]{3,2,1,0:T(8,128)}), f32[32,2,16,512]{3,2,1,0:T(8,128)}) %all-gather.11.cloned.1.call-update) | async-done | bytes 2097168 | tf_op jit(solution)/shard_map/all_gather | solution.py:42
  256.4 3.6 gather_fusion.1
  260.0 1.9 copy.18
  261.9 1.8 fusion.6
  263.7 68.8 %all-gather.15.cloned.1.call-done = f32[64,16,512]{2,1,0:T(8,128)} async-done(((f32[2,16,512]{2,1,0:T(8,128)}), f32[64,16,512]{2,1,0:T(8,128)}) %all-gather.15.cloned.1.call-update) | async-done | bytes 2097168 | tf_op jit(solution)/shard_map/all_gather | solution.py:42
  332.5 3.6 gather_fusion.2
  336.1 1.9 copy.19
  338.0 1.7 fusion.22
  339.8 0.0 all-gather.19.cloned.1.call-start
  339.8 68.8 %all-gather.17.cloned.1.call-done = f32[64,16,512]{2,1,0:T(8,128)} async-done(((f32[2,16,512]{2,1,0:T(8,128)}), f32[64,16,512]{2,1,0:T(8,128)}) %all-gather.17.cloned.1.call-update) | async-done | bytes 2097168 | tf_op jit(solution)/shard_map/all_gather | solution.py:42
  408.6 3.6 gather_fusion.3
  412.2 1.8 copy.20
  414.0 1.7 fusion
  415.9 0.6 slice.40
  416.5 68.1 %all-gather.19.cloned.1.call-done = f32[64,16,512]{2,1,0:T(8,128)} async-done(((f32[2,16,512]{2,1,0:T(8,128)}), f32[64,16,512]{2,1,0:T(8,128)}) %all-gather.19.cloned.1.call-update) | async-done | bytes 2097168 | tf_op jit(solution)/shard_map/all_gather | solution.py:42
  484.7 3.6 gather_fusion.4
  488.2 1.8 copy.21
  490.1 1.1 fusion.8
  491.2 0.6 slice.41
  491.9 62.6 %all-gather.21.cloned.1.call-done = f32[32,1,16,512]{3,2,1,0:T(8,128)} async-done(((f32[1,1,16,512]{3,2,1,0:T(8,128)}), f32[32,1,16,512]{3,2,1,0:T(8,128)}) %all-gather.21.cloned.1.call-update) | async-done | bytes 1048592 | tf_op jit(solution)/shard_map/all_gather | solution.py:62
  554.4 1.8 gather_fusion.5
  556.3 0.6 fusion.12
  556.9 67.7 %all-gather.13.cloned.1.call-done = f32[32,16,512]{2,1,0:T(8,128)} async-done(((f32[1,16,512]{2,1,0:T(8,128)}), f32[32,16,512]{2,1,0:T(8,128)}) %all-gather.13.cloned.1.call-update) | async-done | bytes 1048592 | tf_op jit(solution)/shard_map/all_gather | solution.py:63
  624.6 1.8 gather_fusion.6
  626.5 1.2 multiply_reduce_fusion
  627.7 46.0 %psum.15 = f32[]{:T(128)} all-reduce(f32[]{:T(128)} %get-tuple-element.7), channel_id=1, replica_groups=mesh['dp'=32,'mp'=16] {'dp'}, use_global_device_ids=true, to_apply=%region_5.0 | all-reduce | flops 1 | bytes 8 | tf_op jit(solution)/shard_map/psum | solution.py:66
  674.4 0.1 copy.22
  674.6 0.5 broadcast.99
  675.1 1.3 reduce
  676.4 0.1 reshape.135
  676.5 12.8 %all_to_all.18 = f32[16,1,512]{2,1,0:T(1,128)S(1)} all-to-all(f32[16,1,512]{2,1,0:T(1,128)S(1)} %reshape.135), channel_id=1, replica_groups=mesh['dp'=32,'mp'=16] {'mp'}, dimensions={0} | all-to-all | bytes 65536 | tf_op jit(solution)/shard_map/all_to_all | solution.py:69
  689.3 0.7 reduce.1
  690.1 0.5 reshape.136
  690.6 0.8 copy.23
  (27 shorter events, 0.4 us)
Async XLA Ops:
  6.5 1.6 copy-start
  6.5 126.2 %reduce-scatter.2.cloned.1.call-start = ((), (), s32[]{:S(2)}) async-start(), calls=%async_computation.2 | async-start | bytes 3244032 | tf_op jit(solution)/shard_map/reduce_scatter | solution.py:37
  11.0 1.0 copy-start.3
  18.3 238.2 %all-gather.11.cloned.1.call-start = ((), (), s32[]{:S(2)}) async-start(), calls=%async_computation.3 | async-start | bytes 2162688 | tf_op jit(solution)/shard_map/all_gather | solution.py:42
  184.1 148.4 %all-gather.15.cloned.1.call-start = ((), (), s32[]{:S(2)}) async-start(), calls=%async_computation.5 | async-start | bytes 2162688 | tf_op jit(solution)/shard_map/all_gather | solution.py:42
  260.0 1.9 copy-start.1
  263.7 144.9 %all-gather.17.cloned.1.call-start = ((), (), s32[]{:S(2)}) async-start(), calls=%async_computation.6 | async-start | bytes 2162688 | tf_op jit(solution)/shard_map/all_gather | solution.py:42
  336.1 1.9 copy-start.2
  339.8 144.9 %all-gather.19.cloned.1.call-start = ((), (), s32[]{:S(2)}) async-start(), calls=%async_computation.7 | async-start | bytes 2162688 | tf_op jit(solution)/shard_map/all_gather | solution.py:42
  415.8 138.6 %all-gather.21.cloned.1.call-start = ((), (), s32[]{:S(2)}) async-start(), calls=%async_computation.8 | async-start | bytes 1081344 | tf_op jit(solution)/shard_map/all_gather | solution.py:62
  416.5 208.1 %all-gather.13.cloned.1.call-start = ((), (), s32[]{:S(2)}) async-start(), calls=%async_computation.4 | async-start | bytes 1081344 | tf_op jit(solution)/shard_map/all_gather | solution.py:63
Sparse Core Ops, SparseCore 0:
  18.4 114.3 reduce-scatter.1
  184.2 72.1 all-gather.10
  263.8 68.6 all-gather.14
  339.9 68.6 all-gather.16
  415.9 68.6 all-gather.18
  486.8 67.5 all-gather.20
  556.8 67.8 all-gather.12
where the time goes:
time: 701 us; the launch traced here: 698 us
  waiting for transfers between devices  521 us (74%)
  blocking collectives  108 us (15%)
  local copies, waits for them, and re-layouts  35.8 us (5%)
  between operations  15 us (2%)
  matrix products  12 us (2%)
    all_gather x4, waiting for transfers between devices, assemble(): gathered = lax.all_gather(panel_pair[None], 'dp', axis=0, tiled=True)  277 us
    reduce_scatter x1, waiting for transfers between devices, per_device(): lax.psum_scatter(stacked[panel_owner], 'dp', scatter_dimension=0, tiled=T...  113 us
    all_gather x1, waiting for transfers between devices, per_device(): lax.all_gather(iter_x[1][None], 'dp', axis=0, tiled=True)  67.7 us
    all_gather x1, waiting for transfers between devices, per_device(): lax.all_gather(grad_rows[None], 'dp', axis=0, tiled=True)  62.6 us
    psum x1, blocking collectives, per_device(): norm_f = jnp.sqrt(lax.psum(squares, 'dp') + 1e-06)  48.7 us
    psum x1, blocking collectives, per_device(): total_sq = lax.psum(jnp.sum(precond_rows * precond_rows), 'dp')  46 us
    gather x6, local copies, waits for them, and re-layouts, reorder(): ordered = gathered[inverse]  18 us
  transfers between devices with their start and end apart: 7, of which 7 were waited for; matrix products, arithmetic and copies ran while one was open for 2% of the time, Pallas kernels for 0%

commit v1 on v0

v1 whole, which is shorter than its diff:
```python
import functools

import jax
import jax.numpy as jnp
import numpy as np
from jax import lax
from jax.experimental import pallas as pl
from jax.experimental.pallas import tpu as pltpu
from jax.sharding import PartitionSpec as P

Z = 16
W = 512
B = 128
GROWS = 128
FROWS = 160
OFF = ((0, 1), (0, 2), (0, 3), (1, 2), (1, 3), (2, 3))
VMEM_LIMIT = 40 * 1024 * 1024


def partner1(v):
    return v ^ 1


def partner2(v):
    return (((v + 1) % Z) ^ 1) - 1 if ((v + 1) % Z) ^ 1 else Z - 1


def partner3(v):
    return v + 3 if v % 4 == 0 else v - 3 if v % 4 == 3 else (v + 3) % Z if v % 4 == 2 else (v - 3) % Z


def partner4(v):
    return (v + 5) % Z if v % 2 else (v - 5) % Z


EIGHTH = {3: 0, 8: 0, 0: 1, 11: 1, 7: 2, 12: 2, 4: 3, 15: 3, 9: 4, 14: 4, 1: 5, 6: 5, 5: 6, 10: 6, 2: 7, 13: 7}


def local_order(v):
    four = lambda u: [EIGHTH[u], EIGHTH[partner3(u)], EIGHTH[partner2(u)], EIGHTH[partner3(partner2(u))]]
    return four(v) + four(partner1(v))


def position(z, core):
    return z if core == 0 else (-z) % Z


def table():
    rows = np.zeros((2 * Z, 16), np.int32)
    for z in range(Z):
        for core in range(2):
            for slot, c in enumerate((core, 1 - core)):
                order = local_order(position(z, c))
                assert sorted(order) == list(range(8))
                for k, e in enumerate(order):
                    rows[2 * z + core, 8 * slot + e] = k
    return rows.reshape(-1)


def ring_pairs(partner):
    pairs = []
    for z in range(Z):
        for core in range(2):
            pairs.append((2 * z + core, 2 * position(partner(position(z, core)), core) + core))
    return pairs


CORE_PAIRS = [(i, i ^ 1) for i in range(2 * Z)]
PAIRS = [ring_pairs(p) for p in (partner1, partner2, partner3, partner4)]


def split(x):
    high = x.astype(jnp.bfloat16)
    low = (x - high.astype(jnp.float32)).astype(jnp.bfloat16)
    return high, low


def dot(a, b, dims=((1,), (0,))):
    return lax.dot_general(a, b, (dims, ((), ())), preferred_element_type=jnp.float32)


def product(a, b):
    (ah, al), (bh, bl) = a, b
    return dot(ah, bh) + (dot(ah, bl) + dot(al, bh))


def rows_of(index, size):
    return pl.ds(pl.multiple_of(index * size, size), size)


def pack_grad(tab, grad, own, send):
    dp = lax.axis_index("dp")

    def put(dst, half, slot):
        for e in range(8):
            r, c = half * 256 + (e // 4) * B, (e % 4) * B
            dst[rows_of(tab[dp * 16 + slot * 8 + e], GROWS), :] = grad[r : r + B, c : c + B]

    @pl.when(dp % 2 == 0)
    def _():
        put(own, 0, 0)
        put(send, 1, 1)

    @pl.when(dp % 2 == 1)
    def _():
        put(own, 1, 0)
        put(send, 0, 1)


def pack_factors(tab, grad, own, send, left, right):
    dp = lax.axis_index("dp")
    low = grad[...].astype(jnp.bfloat16)
    left[...] = dot(low, low, ((1,), (1,)))
    right[...] = dot(low, low, ((0,), (0,)))

    def put(dst, src, slot):
        for e in range(8):
            i, j = OFF[e] if e < 6 else (e - 6, e - 6)
            base = pl.multiple_of(tab[dp * 16 + slot * 8 + e] * FROWS, 32)
            dst[pl.ds(base, B), :] = src[i * B : (i + 1) * B, j * B : (j + 1) * B]
            d = 2 + e // 4
            r = d * B + (e % 4) * 32
            dst[pl.ds(pl.multiple_of(base + B, 32), 32), :] = src[r : r + 32, d * B : (d + 1) * B]

    @pl.when(dp % 2 == 0)
    def _():
        put(own, left, 0)
        put(send, right, 1)

    @pl.when(dp % 2 == 1)
    def _():
        put(own, right, 0)
        put(send, left, 1)


def root(tab, near, far, out, packed, factor):
    dp = lax.axis_index("dp")
    packed[: 4 * FROWS, :] = near[...]
    packed[4 * FROWS :, :] = far[...]
    for e in range(8):
        base = pl.multiple_of(tab[dp * 16 + e] * FROWS, 32)
        block = packed[pl.ds(base, B), :]
        i, j = OFF[e] if e < 6 else (e - 6, e - 6)
        factor[i * B : (i + 1) * B, j * B : (j + 1) * B] = block
        if i != j:
            factor[j * B : (j + 1) * B, i * B : (i + 1) * B] = block.T
        d = 2 + e // 4
        r = d * B + (e % 4) * 32
        factor[r : r + 32, d * B : (d + 1) * B] = packed[pl.ds(pl.multiple_of(base + B, 32), 32), :]
    f = factor[...]
    norm = jnp.sqrt(jnp.sum(f * f, keepdims=True) + 1e-06)
    m1 = f / norm
    s1 = split(m1)
    m2 = product(s1, s1)
    s2 = split(m2)
    m3 = product(s2, s1)
    c = 1.0 / 4096.0
    high = (250.0 * c) * m1 - (25.0 * c) * m2 + c * m3
    low = (-5.0 / 16.0 - 3125.0 * c) * m1 + (3125.0 * c) * m2 - (1250.0 * c) * m3
    diagonal = lax.broadcasted_iota(jnp.int32, (W, W), 0) == lax.broadcasted_iota(jnp.int32, (W, W), 1)
    low = low + jnp.where(diagonal, 25.0 / 16.0, 0.0)
    x = low + product(split(m3), split(high))
    out[...] = x * lax.rsqrt(jnp.sqrt(norm))


def finish(tab, owner, x_own, x_other, g_near, g_far, h_near, h_far, out, grad, precond):
    dp = lax.axis_index("dp")
    core = dp % 2

    def take(near, far, half, slot):
        for e in range(8):
            k = tab[dp * 16 + slot * 8 + e]
            r, c = half * 256 + (e // 4) * B, (e % 4) * B

            @pl.when(k < 4)
            def _():
                grad[r : r + B, c : c + B] = near[rows_of(k, GROWS), :]

            @pl.when(k >= 4)
            def _():
                grad[r : r + B, c : c + B] = far[rows_of(k - 4, GROWS), :]

    @pl.when(core == 0)
    def _():
        take(g_near, g_far, 0, 0)
        take(h_near, h_far, 1, 1)

    @pl.when(core == 1)
    def _():
        take(g_near, g_far, 1, 0)
        take(h_near, h_far, 0, 1)

    left = jnp.where(core == 0, x_own[...], x_other[...])
    right = jnp.where(core == 0, x_other[...], x_own[...])
    mixed = product(split(left), split(grad[...]))
    value = product(split(mixed), split(right))
    precond[...] = value
    scale = jnp.sqrt(jnp.sum(value * value, keepdims=True) / (W * W) + 1e-06)
    out[...] = precond[rows_of(owner[dp], 16), :] / scale


def call(kernel, outs, scratch, *args):
    smem = [isinstance(a, tuple) for a in args]
    return pl.pallas_call(
        kernel,
        out_shape=[jax.ShapeDtypeStruct(s, jnp.float32) for s in outs],
        in_specs=[pl.BlockSpec(memory_space=pltpu.SMEM if s else pltpu.VMEM) for s in smem],
        out_specs=[pl.BlockSpec(memory_space=pltpu.VMEM) for _ in outs],
        scratch_shapes=[pltpu.VMEM(s, jnp.float32) for s in scratch],
        compiler_params=pltpu.CompilerParams(vmem_limit_bytes=VMEM_LIMIT),
    )(*[a[0] if s else a for a, s in zip(args, smem)])


def move(x, step):
    return lax.ppermute(x, "dp", CORE_PAIRS if step == 0 else PAIRS[step - 1])


def halve(own, received):
    half = own.shape[0] // 2
    return own[:half] + received[:half], own[half:] + received[half:]


def total(own, send):
    received = move(send, 0)
    for step in (1, 2, 3):
        keep, give = halve(own, received)
        own, received = keep, move(give, step)
    own = own + received
    own = own + move(own, 4)
    own = jnp.concatenate([own, move(own, 3)])
    own = jnp.concatenate([own, move(own, 2)])
    return own, move(own, 1)


def per_device(acts, grads_out, panel_owner):
    tab = jnp.asarray(table())
    part_grad = jnp.einsum("tb,tc->bc", acts, grads_out, preferred_element_type=jnp.float32)
    g_own, g_send = call(pack_grad, [(8 * GROWS, B)] * 2, [], (tab,), part_grad)
    f_own, f_send = call(pack_factors, [(8 * FROWS, B)] * 2, [(W, W)] * 2, (tab,), part_grad)
    f_near, f_far = total(f_own, f_send)
    g_near, g_far = total(g_own, g_send)
    (x_own,) = call(root, [(W, W)], [(8 * FROWS, B), (W, W)], (tab,), f_near, f_far)
    h_near, h_far = move(g_near, 0), move(g_far, 0)
    x_other = move(x_own, 0)
    (panel,) = call(
        finish, [(16, W)], [(W, W)] * 2, (tab,), (panel_owner,), x_own, x_other, g_near, g_far, h_near, h_far
    )
    return lax.all_to_all(panel[None], "mp", split_axis=2, concat_axis=0, tiled=True)


def solution(mesh):
    return jax.shard_map(
        per_device,
        mesh=mesh,
        in_specs=(P("dp", "mp"), P("dp", "mp"), P()),
        out_specs=P(None, "dp", "mp"),
        check_vma=False,
    )
```

time: 701 us -> 153 us (0.22)
  waiting for transfers between devices: 521 us -> 37 us
  blocking collectives: 108 us -> 13.2 us
  starting transfers between devices: 0.25 us -> 83.6 us
  local copies, waits for them, and re-layouts: 35.8 us -> 3.66 us
  between operations: 15 us -> 0.37 us
  matrix products: 12 us -> 2.86 us
  Pallas kernels: 0 us -> 9.02 us
    all_gather x6 -> x0, waiting for transfers between devices: 408 us -> none  [the longest x4 277 us: assemble(): gathered = lax.all_gather(panel_pair[None], 'dp', axis=0, tiled=True)]
    reduce_scatter x1 -> x0, waiting for transfers between devices: 113 us -> none  [per_device(): lax.psum_scatter(stacked[panel_owner], 'dp', scatter_dimension=0, tiled=T...]
    psum x2 -> x0, blocking collectives: 94.8 us -> none  [the longest x1 48.7 us: per_device(): norm_f = jnp.sqrt(lax.psum(squares, 'dp') + 1e-06)]
    ppermute x0 -> x19, starting transfers between devices: none -> 83.6 us  [move(): return lax.ppermute(x, 'dp', CORE_PAIRS if step == 0 else PAIRS[step - 1])]
    ppermute x0 -> x19, waiting for transfers between devices: none -> 37 us  [move(): return lax.ppermute(x, 'dp', CORE_PAIRS if step == 0 else PAIRS[step - 1])]
    gather x7 -> x0, local copies, waits for them, and re-layouts: 22.3 us -> none  [the longest x6 18 us: reorder(): ordered = gathered[inverse]]
    dot_general x8 -> x0, matrix products: 9.14 us -> none  [the longest x4 6.36 us: batched(): jnp.einsum('kij,kjl->kil', left, right, precision=lax.Precision.HIGHEST)]
    pallas_call x0 -> x4, Pallas kernels: none -> 9.02 us  [call(): pl.pallas_call(kernel, out_shape=[jax.ShapeDtypeStruct(s, jnp.float32) fo...]
  transfers between devices with their start and end apart: 7 -> 19, of which waited for: 7 -> 11; matrix products, arithmetic and copies ran while one was open for 2% -> 0% of each run, Pallas kernels for 0% -> 3%
where the time goes in v1:
time: 153 us; the launch traced here: 152 us
  starting transfers between devices  83.6 us (55%)
  waiting for transfers between devices  37 us (24%)
  blocking collectives  13.2 us (9%)
  Pallas kernels  9.02 us (6%)
  local copies, waits for them, and re-layouts  3.66 us (2%)
  matrix products  2.86 us (2%)
  other arithmetic  2.34 us (2%)
    ppermute x19, starting transfers between devices, move(): return lax.ppermute(x, 'dp', CORE_PAIRS if step == 0 else PAIRS[step - 1])  83.6 us
    ppermute x19, waiting for transfers between devices, move(): return lax.ppermute(x, 'dp', CORE_PAIRS if step == 0 else PAIRS[step - 1])  37 us
    all_to_all x1, blocking collectives, per_device(): lax.all_to_all(panel[None], 'mp', split_axis=2, concat_axis=0, tiled=True)  13.2 us
    pallas_call x4, Pallas kernels, call(): pl.pallas_call(kernel, out_shape=[jax.ShapeDtypeStruct(s, jnp.float32) fo...  9.02 us
  transfers between devices with their start and end apart: 19, of which 11 were waited for; matrix products, arithmetic and copies ran while one was open for 0% of the time, Pallas kernels for 3%

profile of v1, /device:TPU:1, one launch (start us, length us, event | category | flops | bytes accessed | tf_op | source)
XLA Modules:
  0.0 152.0 jit_solution(13139411832839925628)
XLA Ops:
  0.0 1.6 %copy-done = bf16[2048,512]{1,0:T(8,128)(2,1)S(1)} copy-done((bf16[2048,512]{1,0:T(8,128)(2,1)S(1)}, bf16[2048,512]{1,0:T(8,128)(2,1)}, u32[]{:S(2)}) %copy-start) | copy-done | bytes 2097176
  1.6 2.9 %fusion.2.grad = f32[512,512]{1,0:T(8,128)S(1)} fusion(bf16[2048,512]{1,0:T(8,128)(2,1)S(1)} %copy-done, bf16[2048,512]{1,0:T(8,128)(2,1)} %param.5), kind=kOutput, calls=%fused_computation.18 | convolution fusion | flops 1073741824 | bytes 5242880 | tf_op jit(solution)/shard_map/tb,tc->bc/dot_general | solution.py:237
  4.5 1.4 shard_map.46
  5.9 8.8 %collective-permute-start = (f32[1280,128]{1,0:T(8,128)S(1)}, f32[1280,128]{1,0:T(8,128)S(1)}, u32[]{:S(2)}, u32[]{:S(2)}) collective-permute-start(f32[1280,128]{1,0:T(8,128)S(1)} %get-tuple-element.10), channel_id=1, source_target_pairs={{0,16},{16,0},{32,48},{48,32},{64,80},{80,64},{96,112},{112,96},{1... | collective-permute-start | bytes 1966088 | tf_op jit(solution)/shard_map/ppermute | solution.py:215
  14.7 1.7 %collective-permute-done = f32[1280,128]{1,0:T(8,128)S(1)} collective-permute-done((f32[1280,128]{1,0:T(8,128)S(1)}, f32[1280,128]{1,0:T(8,128)S(1)}, u32[]{:S(2)}, u32[]{:S(2)}) %collective-permute-start) | collective-permute-done | bytes 655392 | tf_op jit(solution)/shard_map/ppermute | solution.py:215
  16.4 0.1 slice_add_fusion.1
  16.5 5.7 %collective-permute-start.1 = (f32[640,128]{1,0:T(8,128)S(1)}, f32[640,128]{1,0:T(8,128)S(1)}, u32[]{:S(2)}, u32[]{:S(2)}) collective-permute-start(f32[640,128]{1,0:T(8,128)S(1)} %get-tuple-element.14), channel_id=1, source_target_pairs={{0,32},{16,496},{32,0},{48,80},{64,96},{80,48},{96,64},{112,144},{... | collective-permute-start | bytes 983048 | tf_op jit(solution)/shard_map/ppermute | solution.py:215
  22.2 4.4 %collective-permute-done.1 = f32[640,128]{1,0:T(8,128)S(1)} collective-permute-done((f32[640,128]{1,0:T(8,128)S(1)}, f32[640,128]{1,0:T(8,128)S(1)}, u32[]{:S(2)}, u32[]{:S(2)}) %collective-permute-start.1) | collective-permute-done | bytes 327712 | tf_op jit(solution)/shard_map/ppermute | solution.py:215
  26.7 1.9 %collective-permute-start.2 = (f32[320,128]{1,0:T(8,128)S(1)}, f32[320,128]{1,0:T(8,128)S(1)}, u32[]{:S(2)}, u32[]{:S(2)}) collective-permute-start(f32[320,128]{1,0:T(8,128)S(1)} %get-tuple-element.18), channel_id=1, source_target_pairs={{0,480},{16,48},{32,64},{48,16},{64,32},{80,112},{96,128},{112,80}... | collective-permute-start | bytes 491528 | tf_op jit(solution)/shard_map/ppermute | solution.py:215
  28.6 0.7 shard_map.48
  29.3 5.2 %collective-permute-start.9 = (f32[1024,128]{1,0:T(8,128)S(1)}, f32[1024,128]{1,0:T(8,128)S(1)}, u32[]{:S(2)}, u32[]{:S(2)}) collective-permute-start(f32[1024,128]{1,0:T(8,128)S(1)} %get-tuple-element.12), channel_id=1, source_target_pairs={{0,16},{16,0},{32,48},{48,32},{64,80},{80,64},{96,112},{112,96},{1... | collective-permute-start | bytes 1572872 | tf_op jit(solution)/shard_map/ppermute | solution.py:215
  34.5 3.5 %collective-permute-start.3 = (f32[160,128]{1,0:T(8,128)S(1)}, f32[160,128]{1,0:T(8,128)S(1)}, u32[]{:S(2)}, u32[]{:S(2)}) collective-permute-start(f32[160,128]{1,0:T(8,128)S(1)} %slice_add_fusion.8), channel_id=1, source_target_pairs={{0,96},{16,432},{32,448},{48,144},{64,160},{80,496},{96,0},{112,20... | collective-permute-start | bytes 245768 | tf_op jit(solution)/shard_map/ppermute | solution.py:215
  38.0 4.7 %collective-permute-done.3 = f32[160,128]{1,0:T(8,128)S(1)} collective-permute-done((f32[160,128]{1,0:T(8,128)S(1)}, f32[160,128]{1,0:T(8,128)S(1)}, u32[]{:S(2)}, u32[]{:S(2)}) %collective-permute-start.3) | collective-permute-done | bytes 81952 | tf_op jit(solution)/shard_map/ppermute | solution.py:215
  42.7 3.3 %collective-permute-start.4 = (f32[160,128]{1,0:T(8,128)S(1)}, f32[160,128]{1,0:T(8,128)S(1)}, u32[]{:S(2)}, u32[]{:S(2)}) collective-permute-start(f32[160,128]{1,0:T(8,128)S(1)} %fusion), channel_id=1, source_target_pairs={{0,352},{16,176},{32,192},{48,400},{64,416},{80,240},{96,256},{112... | collective-permute-start | bytes 245768 | tf_op jit(solution)/shard_map/ppermute | solution.py:215
  46.0 0.1 slice_add_fusion.3
  46.1 5.0 %collective-permute-start.10 = (f32[512,128]{1,0:T(8,128)S(1)}, f32[512,128]{1,0:T(8,128)S(1)}, u32[]{:S(2)}, u32[]{:S(2)}) collective-permute-start(f32[512,128]{1,0:T(8,128)S(1)} %get-tuple-element.16), channel_id=1, source_target_pairs={{0,32},{16,496},{32,0},{48,80},{64,96},{80,48},{96,64},{112,144},{... | collective-permute-start | bytes 786440 | tf_op jit(solution)/shard_map/ppermute | solution.py:215
  51.1 2.9 %collective-permute-done.4 = f32[160,128]{1,0:T(8,128)S(1)} collective-permute-done((f32[160,128]{1,0:T(8,128)S(1)}, f32[160,128]{1,0:T(8,128)S(1)}, u32[]{:S(2)}, u32[]{:S(2)}) %collective-permute-start.4) | collective-permute-done | bytes 81952 | tf_op jit(solution)/shard_map/ppermute | solution.py:215
  54.0 2.4 %collective-permute-start.5 = (f32[160,128]{1,0:T(8,128)S(1)}, f32[160,128]{1,0:T(8,128)S(1)}, u32[]{:S(2)}, u32[]{:S(2)}) collective-permute-start(f32[160,128]{1,0:T(8,128)S(1)} %add.55), channel_id=1, source_target_pairs={{0,96},{16,432},{32,448},{48,144},{64,160},{80,496},{96,0},{112,20... | collective-permute-start | bytes 245768 | tf_op jit(solution)/shard_map/ppermute | solution.py:215
  56.5 6.6 %collective-permute-done.5 = f32[160,128]{1,0:T(8,128)S(1)} collective-permute-done((f32[160,128]{1,0:T(8,128)S(1)}, f32[160,128]{1,0:T(8,128)S(1)}, u32[]{:S(2)}, u32[]{:S(2)}) %collective-permute-start.5) | collective-permute-done | bytes 81952 | tf_op jit(solution)/shard_map/ppermute | solution.py:215
  63.1 1.9 %collective-permute-start.6 = (f32[320,128]{1,0:T(8,128)S(1)}, f32[320,128]{1,0:T(8,128)S(1)}, u32[]{:S(2)}, u32[]{:S(2)}) collective-permute-start(f32[320,128]{1,0:T(8,128)S(1)} %pad_maximum_fusion.2), channel_id=1, source_target_pairs={{0,480},{16,48},{32,64},{48,16},{64,32},{80,112},{96,128},{112,80}... | collective-permute-start | bytes 491528 | tf_op jit(solution)/shard_map/ppermute | solution.py:215
  65.0 0.0 collective-permute-done.10
  65.1 0.0 copy-start.2
  65.1 3.4 %collective-permute-start.11 = (f32[256,128]{1,0:T(8,128)S(1)}, f32[256,128]{1,0:T(8,128)S(1)}, u32[]{:S(2)}, u32[]{:S(2)}) collective-permute-start(f32[256,128]{1,0:T(8,128)S(1)} %get-tuple-element.20), channel_id=1, source_target_pairs={{0,480},{16,48},{32,64},{48,16},{64,32},{80,112},{96,128},{112,80}... | collective-permute-start | bytes 393224 | tf_op jit(solution)/shard_map/ppermute | solution.py:215
  68.5 0.7 collective-permute-done.6
  69.2 2.2 %collective-permute-start.7 = (f32[640,128]{1,0:T(8,128)S(1)}, f32[640,128]{1,0:T(8,128)S(1)}, u32[]{:S(2)}, u32[]{:S(2)}) collective-permute-start(f32[640,128]{1,0:T(8,128)S(1)} %pad_maximum_fusion.near), channel_id=1, source_target_pairs={{0,32},{16,496},{32,0},{48,80},{64,96},{80,48},{96,64},{112,144},{... | collective-permute-start | bytes 983048 | tf_op jit(solution)/shard_map/ppermute | solution.py:215
  71.4 4.1 %collective-permute-start.12 = (f32[128,128]{1,0:T(8,128)S(1)}, f32[128,128]{1,0:T(8,128)S(1)}, u32[]{:S(2)}, u32[]{:S(2)}) collective-permute-start(f32[128,128]{1,0:T(8,128)S(1)} %slice_add_fusion.10), channel_id=1, source_target_pairs={{0,96},{16,432},{32,448},{48,144},{64,160},{80,496},{96,0},{112,20... | collective-permute-start | bytes 196616 | tf_op jit(solution)/shard_map/ppermute | solution.py:215
  75.5 4.4 %collective-permute-done.7.far = f32[640,128]{1,0:T(8,128)S(1)} collective-permute-done((f32[640,128]{1,0:T(8,128)S(1)}, f32[640,128]{1,0:T(8,128)S(1)}, u32[]{:S(2)}, u32[]{:S(2)}) %collective-permute-start.7) | collective-permute-done | bytes 327712 | tf_op jit(solution)/shard_map/ppermute | solution.py:215
  79.9 4.0 %shard_map.47.x_own = f32[512,512]{1,0:T(8,128)S(1)} custom-call(s32[512]{0:T(512)S(1)} %copy-done.1, f32[640,128]{1,0:T(8,128)S(1)} %pad_maximum_fusion.near, f32[640,128]{1,0:T(8,128)S(1)} %collective-permute-done.7.far), custom_call_target="tpu_custom_call" | custom-call | tf_op jit(solution)/shard_map/pallas_call | solution.py:204
  83.8 5.8 %collective-permute-start.8 = (f32[512,512]{1,0:T(8,128)S(1)}, f32[512,512]{1,0:T(8,128)S(1)}, u32[]{:S(2)}, u32[]{:S(2)}) collective-permute-start(f32[512,512]{1,0:T(8,128)S(1)} %shard_map.47.x_own), channel_id=1, source_target_pairs={{0,16},{16,0},{32,48},{48,32},{64,80},{80,64},{96,112},{112,96},{1... | collective-permute-start | bytes 3145736 | tf_op jit(solution)/shard_map/ppermute | solution.py:215
  89.7 4.6 %collective-permute-start.13 = (f32[128,128]{1,0:T(8,128)S(1)}, f32[128,128]{1,0:T(8,128)S(1)}, u32[]{:S(2)}, u32[]{:S(2)}) collective-permute-start(f32[128,128]{1,0:T(8,128)S(1)} %fusion.1), channel_id=1, source_target_pairs={{0,352},{16,176},{32,192},{48,400},{64,416},{80,240},{96,256},{112... | collective-permute-start | bytes 196616 | tf_op jit(solution)/shard_map/ppermute | solution.py:215
  94.3 6.0 %collective-permute-done.13 = f32[128,128]{1,0:T(8,128)S(1)} collective-permute-done((f32[128,128]{1,0:T(8,128)S(1)}, f32[128,128]{1,0:T(8,128)S(1)}, u32[]{:S(2)}, u32[]{:S(2)}) %collective-permute-start.13) | collective-permute-done | bytes 65568 | tf_op jit(solution)/shard_map/ppermute | solution.py:215
  100.3 5.9 %collective-permute-start.14 = (f32[128,128]{1,0:T(8,128)S(1)}, f32[128,128]{1,0:T(8,128)S(1)}, u32[]{:S(2)}, u32[]{:S(2)}) collective-permute-start(f32[128,128]{1,0:T(8,128)S(1)} %add.63), channel_id=1, source_target_pairs={{0,96},{16,432},{32,448},{48,144},{64,160},{80,496},{96,0},{112,20... | collective-permute-start | bytes 196616 | tf_op jit(solution)/shard_map/ppermute | solution.py:215
  106.2 2.1 %collective-permute-done.14 = f32[128,128]{1,0:T(8,128)S(1)} collective-permute-done((f32[128,128]{1,0:T(8,128)S(1)}, f32[128,128]{1,0:T(8,128)S(1)}, u32[]{:S(2)}, u32[]{:S(2)}) %collective-permute-start.14) | collective-permute-done | bytes 65568 | tf_op jit(solution)/shard_map/ppermute | solution.py:215
  108.3 5.0 %collective-permute-start.15 = (f32[256,128]{1,0:T(8,128)S(1)}, f32[256,128]{1,0:T(8,128)S(1)}, u32[]{:S(2)}, u32[]{:S(2)}) collective-permute-start(f32[256,128]{1,0:T(8,128)S(1)} %pad_maximum_fusion.3), channel_id=1, source_target_pairs={{0,480},{16,48},{32,64},{48,16},{64,32},{80,112},{96,128},{112,80}... | collective-permute-start | bytes 393224 | tf_op jit(solution)/shard_map/ppermute | solution.py:215
  113.3 2.3 %collective-permute-done.15 = f32[256,128]{1,0:T(8,128)S(1)} collective-permute-done((f32[256,128]{1,0:T(8,128)S(1)}, f32[256,128]{1,0:T(8,128)S(1)}, u32[]{:S(2)}, u32[]{:S(2)}) %collective-permute-start.15) | collective-permute-done | bytes 131104 | tf_op jit(solution)/shard_map/ppermute | solution.py:215
  115.7 4.1 %collective-permute-start.16 = (f32[512,128]{1,0:T(8,128)S(1)}, f32[512,128]{1,0:T(8,128)S(1)}, u32[]{:S(2)}, u32[]{:S(2)}) collective-permute-start(f32[512,128]{1,0:T(8,128)S(1)} %pad_maximum_fusion.1.g_near), channel_id=1, source_target_pairs={{0,32},{16,496},{32,0},{48,80},{64,96},{80,48},{96,64},{112,144},{... | collective-permute-start | bytes 786440 | tf_op jit(solution)/shard_map/ppermute | solution.py:215
  119.7 5.8 %collective-permute-start.17 = (f32[512,128]{1,0:T(8,128)S(1)}, f32[512,128]{1,0:T(8,128)S(1)}, u32[]{:S(2)}, u32[]{:S(2)}) collective-permute-start(f32[512,128]{1,0:T(8,128)S(1)} %pad_maximum_fusion.1.g_near), channel_id=1, source_target_pairs={{0,16},{16,0},{32,48},{48,32},{64,80},{80,64},{96,112},{112,96},{1... | collective-permute-start | bytes 786440 | tf_op jit(solution)/shard_map/ppermute | solution.py:215
  125.5 5.0 %collective-permute-start.18 = (f32[512,128]{1,0:T(8,128)S(1)}, f32[512,128]{1,0:T(8,128)S(1)}, u32[]{:S(2)}, u32[]{:S(2)}) collective-permute-start(f32[512,128]{1,0:T(8,128)S(1)} %collective-permute-done.16.g_far), channel_id=1, source_target_pairs={{0,16},{16,0},{32,48},{48,32},{64,80},{80,64},{96,112},{112,96},{1... | collective-permute-start | bytes 786440 | tf_op jit(solution)/shard_map/ppermute | solution.py:215
  130.6 1.1 collective-permute-done.18.h_far
  131.7 3.0 %shard_map.49 = f32[16,512]{1,0:T(8,128)S(1)} custom-call(s32[512]{0:T(512)S(1)} %copy-done.1, s32[32]{0:T(128)S(1)} %copy-done.2, f32[512,512]{1,0:T(8,128)S(1)} %shard_map.47.x_own, f32[512,512]{1,0:T(8,128)S(1)} %collective-permute-done.8.x_other, f32[512,128]{1,0:T(8,128)S(1)} %pad_maximum_fusion.1.g_near, f32[512,128]{1,0:T(8,128)S(1)} %collective-permute-done.16.g_far, ...), custom_call_target="tpu_custom_call" | custom-call | tf_op jit(solution)/shard_map/pallas_call | solution.py:204
  134.7 0.1 copy.6
  134.8 0.5 broadcast
  135.4 1.3 reduce
  136.7 0.1 reshape
  136.8 13.2 %all_to_all.18 = f32[16,1,512]{2,1,0:T(1,128)S(1)} all-to-all(f32[16,1,512]{2,1,0:T(1,128)S(1)} %reshape), channel_id=1, replica_groups=mesh['dp'=32,'mp'=16] {'mp'}, dimensions={0} | all-to-all | bytes 65536 | tf_op jit(solution)/shard_map/all_to_all | solution.py:248
  150.0 0.7 reduce.1
  150.8 0.5 reshape.1
  151.3 0.8 copy.7
  (23 shorter events, 0.2 us)
Async XLA Ops:
  0.0 1.6 %copy-start = (bf16[2048,512]{1,0:T(8,128)(2,1)S(1)}, bf16[2048,512]{1,0:T(8,128)(2,1)}, u32[]{:S(2)}) copy-start(bf16[2048,512]{1,0:T(8,128)(2,1)} %param.4) | copy-start | bytes 6291460
  0.0 4.5 %copy-start.1 = (s32[512]{0:T(512)S(1)}, s32[512]{0:T(512)}, u32[]{:S(2)}) copy-start(s32[512]{0:T(512)} %constant.2.clone.tab) | copy-start | bytes 6148
  5.9 10.5 %collective-permute-start = (f32[1280,128]{1,0:T(8,128)S(1)}, f32[1280,128]{1,0:T(8,128)S(1)}, u32[]{:S(2)}, u32[]{:S(2)}) collective-permute-start(f32[1280,128]{1,0:T(8,128)S(1)} %get-tuple-element.10), channel_id=1, source_target_pairs={{0,16},{16,0},{32,48},{48,32},{64,80},{80,64},{96,112},{112,96},{1... | collective-permute-start | bytes 1966088 | tf_op jit(solution)/shard_map/ppermute | solution.py:215
  16.5 10.2 %collective-permute-start.1 = (f32[640,128]{1,0:T(8,128)S(1)}, f32[640,128]{1,0:T(8,128)S(1)}, u32[]{:S(2)}, u32[]{:S(2)}) collective-permute-start(f32[640,128]{1,0:T(8,128)S(1)} %get-tuple-element.14), channel_id=1, source_target_pairs={{0,32},{16,496},{32,0},{48,80},{64,96},{80,48},{96,64},{112,144},{... | collective-permute-start | bytes 983048 | tf_op jit(solution)/shard_map/ppermute | solution.py:215
  26.7 7.8 %collective-permute-start.2 = (f32[320,128]{1,0:T(8,128)S(1)}, f32[320,128]{1,0:T(8,128)S(1)}, u32[]{:S(2)}, u32[]{:S(2)}) collective-permute-start(f32[320,128]{1,0:T(8,128)S(1)} %get-tuple-element.18), channel_id=1, source_target_pairs={{0,480},{16,48},{32,64},{48,16},{64,32},{80,112},{96,128},{112,80}... | collective-permute-start | bytes 491528 | tf_op jit(solution)/shard_map/ppermute | solution.py:215
  29.3 16.7 %collective-permute-start.9 = (f32[1024,128]{1,0:T(8,128)S(1)}, f32[1024,128]{1,0:T(8,128)S(1)}, u32[]{:S(2)}, u32[]{:S(2)}) collective-permute-start(f32[1024,128]{1,0:T(8,128)S(1)} %get-tuple-element.12), channel_id=1, source_target_pairs={{0,16},{16,0},{32,48},{48,32},{64,80},{80,64},{96,112},{112,96},{1... | collective-permute-start | bytes 1572872 | tf_op jit(solution)/shard_map/ppermute | solution.py:215
  34.5 8.2 %collective-permute-start.3 = (f32[160,128]{1,0:T(8,128)S(1)}, f32[160,128]{1,0:T(8,128)S(1)}, u32[]{:S(2)}, u32[]{:S(2)}) collective-permute-start(f32[160,128]{1,0:T(8,128)S(1)} %slice_add_fusion.8), channel_id=1, source_target_pairs={{0,96},{16,432},{32,448},{48,144},{64,160},{80,496},{96,0},{112,20... | collective-permute-start | bytes 245768 | tf_op jit(solution)/shard_map/ppermute | solution.py:215
  42.7 11.3 %collective-permute-start.4 = (f32[160,128]{1,0:T(8,128)S(1)}, f32[160,128]{1,0:T(8,128)S(1)}, u32[]{:S(2)}, u32[]{:S(2)}) collective-permute-start(f32[160,128]{1,0:T(8,128)S(1)} %fusion), channel_id=1, source_target_pairs={{0,352},{16,176},{32,192},{48,400},{64,416},{80,240},{96,256},{112... | collective-permute-start | bytes 245768 | tf_op jit(solution)/shard_map/ppermute | solution.py:215
  46.1 19.0 %collective-permute-start.10 = (f32[512,128]{1,0:T(8,128)S(1)}, f32[512,128]{1,0:T(8,128)S(1)}, u32[]{:S(2)}, u32[]{:S(2)}) collective-permute-start(f32[512,128]{1,0:T(8,128)S(1)} %get-tuple-element.16), channel_id=1, source_target_pairs={{0,32},{16,496},{32,0},{48,80},{64,96},{80,48},{96,64},{112,144},{... | collective-permute-start | bytes 786440 | tf_op jit(solution)/shard_map/ppermute | solution.py:215
  54.0 9.1 %collective-permute-start.5 = (f32[160,128]{1,0:T(8,128)S(1)}, f32[160,128]{1,0:T(8,128)S(1)}, u32[]{:S(2)}, u32[]{:S(2)}) collective-permute-start(f32[160,128]{1,0:T(8,128)S(1)} %add.55), channel_id=1, source_target_pairs={{0,96},{16,432},{32,448},{48,144},{64,160},{80,496},{96,0},{112,20... | collective-permute-start | bytes 245768 | tf_op jit(solution)/shard_map/ppermute | solution.py:215
  63.1 6.1 %collective-permute-start.6 = (f32[320,128]{1,0:T(8,128)S(1)}, f32[320,128]{1,0:T(8,128)S(1)}, u32[]{:S(2)}, u32[]{:S(2)}) collective-permute-start(f32[320,128]{1,0:T(8,128)S(1)} %pad_maximum_fusion.2), channel_id=1, source_target_pairs={{0,480},{16,48},{32,64},{48,16},{64,32},{80,112},{96,128},{112,80}... | collective-permute-start | bytes 491528 | tf_op jit(solution)/shard_map/ppermute | solution.py:215
  65.1 66.6 %copy-start.2 = (s32[32]{0:T(128)S(1)}, s32[32]{0:T(128)}, u32[]{:S(2)}) copy-start(s32[32]{0:T(128)} %owner.1) | copy-start | bytes 388
  65.1 6.3 %collective-permute-start.11 = (f32[256,128]{1,0:T(8,128)S(1)}, f32[256,128]{1,0:T(8,128)S(1)}, u32[]{:S(2)}, u32[]{:S(2)}) collective-permute-start(f32[256,128]{1,0:T(8,128)S(1)} %get-tuple-element.20), channel_id=1, source_target_pairs={{0,480},{16,48},{32,64},{48,16},{64,32},{80,112},{96,128},{112,80}... | collective-permute-start | bytes 393224 | tf_op jit(solution)/shard_map/ppermute | solution.py:215
  69.2 10.7 %collective-permute-start.7 = (f32[640,128]{1,0:T(8,128)S(1)}, f32[640,128]{1,0:T(8,128)S(1)}, u32[]{:S(2)}, u32[]{:S(2)}) collective-permute-start(f32[640,128]{1,0:T(8,128)S(1)} %pad_maximum_fusion.near), channel_id=1, source_target_pairs={{0,32},{16,496},{32,0},{48,80},{64,96},{80,48},{96,64},{112,144},{... | collective-permute-start | bytes 983048 | tf_op jit(solution)/shard_map/ppermute | solution.py:215
  71.4 18.2 %collective-permute-start.12 = (f32[128,128]{1,0:T(8,128)S(1)}, f32[128,128]{1,0:T(8,128)S(1)}, u32[]{:S(2)}, u32[]{:S(2)}) collective-permute-start(f32[128,128]{1,0:T(8,128)S(1)} %slice_add_fusion.10), channel_id=1, source_target_pairs={{0,96},{16,432},{32,448},{48,144},{64,160},{80,496},{96,0},{112,20... | collective-permute-start | bytes 196616 | tf_op jit(solution)/shard_map/ppermute | solution.py:215
  83.8 47.9 %collective-permute-start.8 = (f32[512,512]{1,0:T(8,128)S(1)}, f32[512,512]{1,0:T(8,128)S(1)}, u32[]{:S(2)}, u32[]{:S(2)}) collective-permute-start(f32[512,512]{1,0:T(8,128)S(1)} %shard_map.47.x_own), channel_id=1, source_target_pairs={{0,16},{16,0},{32,48},{48,32},{64,80},{80,64},{96,112},{112,96},{1... | collective-permute-start | bytes 3145736 | tf_op jit(solution)/shard_map/ppermute | solution.py:215
  89.7 10.6 %collective-permute-start.13 = (f32[128,128]{1,0:T(8,128)S(1)}, f32[128,128]{1,0:T(8,128)S(1)}, u32[]{:S(2)}, u32[]{:S(2)}) collective-permute-start(f32[128,128]{1,0:T(8,128)S(1)} %fusion.1), channel_id=1, source_target_pairs={{0,352},{16,176},{32,192},{48,400},{64,416},{80,240},{96,256},{112... | collective-permute-start | bytes 196616 | tf_op jit(solution)/shard_map/ppermute | solution.py:215
  100.3 8.0 %collective-permute-start.14 = (f32[128,128]{1,0:T(8,128)S(1)}, f32[128,128]{1,0:T(8,128)S(1)}, u32[]{:S(2)}, u32[]{:S(2)}) collective-permute-start(f32[128,128]{1,0:T(8,128)S(1)} %add.63), channel_id=1, source_target_pairs={{0,96},{16,432},{32,448},{48,144},{64,160},{80,496},{96,0},{112,20... | collective-permute-start | bytes 196616 | tf_op jit(solution)/shard_map/ppermute | solution.py:215
  108.3 7.3 %collective-permute-start.15 = (f32[256,128]{1,0:T(8,128)S(1)}, f32[256,128]{1,0:T(8,128)S(1)}, u32[]{:S(2)}, u32[]{:S(2)}) collective-permute-start(f32[256,128]{1,0:T(8,128)S(1)} %pad_maximum_fusion.3), channel_id=1, source_target_pairs={{0,480},{16,48},{32,64},{48,16},{64,32},{80,112},{96,128},{112,80}... | collective-permute-start | bytes 393224 | tf_op jit(solution)/shard_map/ppermute | solution.py:215
  115.7 9.9 %collective-permute-start.16 = (f32[512,128]{1,0:T(8,128)S(1)}, f32[512,128]{1,0:T(8,128)S(1)}, u32[]{:S(2)}, u32[]{:S(2)}) collective-permute-start(f32[512,128]{1,0:T(8,128)S(1)} %pad_maximum_fusion.1.g_near), channel_id=1, source_target_pairs={{0,32},{16,496},{32,0},{48,80},{64,96},{80,48},{96,64},{112,144},{... | collective-permute-start | bytes 786440 | tf_op jit(solution)/shard_map/ppermute | solution.py:215
  119.7 10.8 %collective-permute-start.17 = (f32[512,128]{1,0:T(8,128)S(1)}, f32[512,128]{1,0:T(8,128)S(1)}, u32[]{:S(2)}, u32[]{:S(2)}) collective-permute-start(f32[512,128]{1,0:T(8,128)S(1)} %pad_maximum_fusion.1.g_near), channel_id=1, source_target_pairs={{0,16},{16,0},{32,48},{48,32},{64,80},{80,64},{96,112},{112,96},{1... | collective-permute-start | bytes 786440 | tf_op jit(solution)/shard_map/ppermute | solution.py:215
  125.5 6.2 %collective-permute-start.18 = (f32[512,128]{1,0:T(8,128)S(1)}, f32[512,128]{1,0:T(8,128)S(1)}, u32[]{:S(2)}, u32[]{:S(2)}) collective-permute-start(f32[512,128]{1,0:T(8,128)S(1)} %collective-permute-done.16.g_far), channel_id=1, source_target_pairs={{0,16},{16,0},{32,48},{48,32},{64,80},{80,64},{96,112},{112,96},{1... | collective-permute-start | bytes 786440 | tf_op jit(solution)/shard_map/ppermute | solution.py:215

commit v2 on v1

v2 whole, which is shorter than its diff:
```python
import functools

import jax
import jax.numpy as jnp
from jax import lax
from jax.experimental import pallas as pl
from jax.experimental.pallas import tpu as pltpu
from jax.sharding import PartitionSpec as P

Z = 16
W = 512
B = 128
ROWS = 144
OFF = ((0, 1), (0, 2), (0, 3), (1, 2), (1, 3), (2, 3))
JOIN_FLOPS = 4_000_000_000
ADD_FLOPS = 0
ROOT_FLOPS = 0

MIX_FLOPS = 5_000_000_000
TOKENS = 512
FRONT_LIMIT = 51 * 1024 * 1024
VMEM_LIMIT = 40 * 1024 * 1024


def partner1(v):
    return v ^ 1


def partner2(v):
    return (((v + 1) % Z) ^ 1) - 1 if ((v + 1) % Z) ^ 1 else Z - 1


def partner3(v):
    return v + 3 if v % 4 == 0 else v - 3 if v % 4 == 3 else (v + 3) % Z if v % 4 == 2 else (v - 3) % Z


def partner4(v):
    return (v + 5) % Z if v % 2 else (v - 5) % Z


EIGHTH = {3: 0, 8: 0, 0: 1, 11: 1, 7: 2, 12: 2, 4: 3, 15: 3, 9: 4, 14: 4, 1: 5, 6: 5, 5: 6, 10: 6, 2: 7, 13: 7}


def local_order(v):
    four = lambda u: [EIGHTH[u], EIGHTH[partner3(u)], EIGHTH[partner2(u)], EIGHTH[partner3(partner2(u))]]
    return four(v) + four(partner1(v))


def position(z, core):
    return z if core == 0 else (-z) % Z


def order_code(v):
    order = local_order(v)
    return sum(order.index(e) << (3 * e) for e in range(8))


CODES = [order_code(v) for v in range(Z)]


def places(own):
    dp = lax.axis_index("dp")
    z, core = dp // 2, dp % 2
    v = jnp.where((core == 0) == own, z, (Z - z) % Z)
    code = jnp.int32(CODES[0])
    for u in range(1, Z):
        code = jnp.where(v == u, CODES[u], code)
    return [(code >> (3 * e)) & 7 for e in range(8)]


def ring_pairs(partner):
    pairs = []
    for z in range(Z):
        for core in range(2):
            pairs.append((2 * z + core, 2 * position(partner(position(z, core)), core) + core))
    return pairs


CORE_PAIRS = [(i, i ^ 1) for i in range(2 * Z)]
PAIRS = [ring_pairs(p) for p in (partner1, partner2, partner3, partner4)]


def split(x):
    high = x.astype(jnp.bfloat16)
    low = (x - high.astype(jnp.float32)).astype(jnp.bfloat16)
    return high, low


def dot(a, b, dims=((1,), (0,))):
    return lax.dot_general(a, b, (dims, ((), ())), preferred_element_type=jnp.float32)


def product(a, b):
    (ah, al), (bh, bl) = a, b
    return dot(ah, bh) + (dot(ah, bl) + dot(al, bh))


def rows_of(index, size):
    return pl.ds(pl.multiple_of(index * ROWS, 16), size)


def put_gradient(grad, dst, half, place):
    for e in range(8):
        r, c = half * 256 + (e // 4) * B, (e % 4) * B
        dst[rows_of(place[e], B), :] = grad[r : r + B, c : c + B]
        dst[pl.ds(pl.multiple_of(place[e] * ROWS + B, 16), ROWS - B), :] = jnp.zeros((ROWS - B, B), jnp.float32)


def eighth_parts(e):
    if e < 6:
        return [(OFF[e][0] * B, OFF[e][1] * B, B)]
    return [((2 * e - 12) * B, (2 * e - 12) * B, 64), ((2 * e - 11) * B, (2 * e - 11) * B, 64)]


def left_lanes(rows):
    return lax.broadcasted_iota(jnp.int32, (rows, B), 1) < 64


def put_factor(src, dst, place, corners):
    for pair in range(2):
        lower = [src[d * B + 64 : (d + 1) * B, d * B : (d + 1) * B] for d in (2 * pair, 2 * pair + 1)]
        corners[pair * 64 : (pair + 1) * 64, :] = jnp.where(left_lanes(64), pltpu.roll(lower[0], 64, 1), lower[1])
    for e in range(8):
        base = place[e] * ROWS
        at = 0
        for r, c, n in eighth_parts(e):
            dst[pl.ds(pl.multiple_of(base + at, 16), n), :] = src[r : r + n, c : c + B]
            at += n
        dst[pl.ds(pl.multiple_of(base + at, 16), 16), :] = corners[16 * e : 16 * e + 16, :]


def front(acts, grads_out, f_own, f_send, g_own, g_send, a_vmem, g_vmem, grad, left, right, corners, sems):
    copies = []
    for i in range(acts.shape[0] // TOKENS):
        rows = pl.ds(i * TOKENS, TOKENS)
        pair = [
            pltpu.make_async_copy(src.at[rows], dst.at[rows], sems.at[i, n])
            for n, (src, dst) in enumerate(((acts, a_vmem), (grads_out, g_vmem)))
        ]
        for copy in pair:
            copy.start()
        copies.append(pair)
    place, other = places(True), places(False)
    core = lax.axis_index("dp") % 2
    for i, pair in enumerate(copies):
        for copy in pair:
            copy.wait()
        rows = slice(i * TOKENS, (i + 1) * TOKENS)
        part = dot(a_vmem[rows, :], g_vmem[rows, :], ((0,), (0,)))
        grad[...] = part if i == 0 else grad[...] + part
    low = grad[...].astype(jnp.bfloat16)
    left[...] = dot(low, low, ((1,), (1,)))
    right[...] = dot(low, low, ((0,), (0,)))

    @pl.when(core == 0)
    def _():
        put_factor(left, f_own, place, corners)
        put_factor(right, f_send, other, corners)
        put_gradient(grad, g_own, 0, place)
        put_gradient(grad, g_send, 1, other)

    @pl.when(core == 1)
    def _():
        put_factor(right, f_own, place, corners)
        put_factor(left, f_send, other, corners)
        put_gradient(grad, g_own, 1, place)
        put_gradient(grad, g_send, 0, other)


def root(near, far, after, out, packed, factor, corners):
    place = places(True)
    packed[: 4 * ROWS, :] = near[...]
    packed[4 * ROWS :, :] = far[...]
    for e in range(8):
        base = place[e] * ROWS
        at = 0
        for r, c, n in eighth_parts(e):
            block = packed[pl.ds(pl.multiple_of(base + at, 16), n), :]
            factor[r : r + n, c : c + B] = block
            if r != c:
                factor[c : c + B, r : r + n] = block.T
            at += n
        corners[16 * e : 16 * e + 16, :] = packed[pl.ds(pl.multiple_of(base + at, 16), 16), :]
    for d in range(4):
        upper = factor[d * B : d * B + 64, d * B : (d + 1) * B]
        turned = jnp.concatenate([upper, jnp.zeros_like(upper)]).T
        corner = corners[(d // 2) * 64 : (d // 2 + 1) * 64, :]
        if d % 2 == 0:
            corner = pltpu.roll(corner, 64, 1)
        factor[d * B + 64 : (d + 1) * B, d * B : (d + 1) * B] = jnp.where(left_lanes(64), turned[64:, :], corner)
    f = factor[...]
    norm = jnp.sqrt(jnp.sum(f * f, keepdims=True) + 1e-06)
    m1 = f / norm
    s1 = split(m1)
    m2 = product(s1, s1)
    s2 = split(m2)
    m3 = product(s2, s1)
    c = 1.0 / 4096.0
    high = (250.0 * c) * m1 - (25.0 * c) * m2 + c * m3
    low = (-5.0 / 16.0 - 3125.0 * c) * m1 + (3125.0 * c) * m2 - (1250.0 * c) * m3
    diagonal = lax.broadcasted_iota(jnp.int32, (W, W), 0) == lax.broadcasted_iota(jnp.int32, (W, W), 1)
    low = low + jnp.where(diagonal, 25.0 / 16.0, 0.0)
    x = low + product(split(m3), split(high))
    out[...] = x * lax.rsqrt(jnp.sqrt(norm))


def mix(x, g_near, g_far, h_near, h_far, out, grad):
    core = lax.axis_index("dp") % 2
    place, other = places(True), places(False)

    def take(near, far, half, place):
        for e in range(8):
            k = place[e]
            r, c = half * 256 + (e // 4) * B, (e % 4) * B

            @pl.when(k < 4)
            def _():
                grad[r : r + B, c : c + B] = near[rows_of(k, B), :]

            @pl.when(k >= 4)
            def _():
                grad[r : r + B, c : c + B] = far[rows_of(k - 4, B), :]

    @pl.when(core == 0)
    def _():
        take(g_near, g_far, 0, place)
        take(h_near, h_far, 1, other)
        out[...] = product(split(x[...]), split(grad[...]))

    @pl.when(core == 1)
    def _():
        take(g_near, g_far, 1, place)
        take(h_near, h_far, 0, other)
        out[...] = product(split(grad[...]), split(x[...]))


def finish(owner, mixed, x, out, precond):
    dp = lax.axis_index("dp")

    @pl.when(dp % 2 == 0)
    def _():
        precond[...] = product(split(mixed[...]), split(x[...]))

    @pl.when(dp % 2 == 1)
    def _():
        precond[...] = product(split(x[...]), split(mixed[...]))

    value = precond[...]
    scale = jnp.sqrt(jnp.sum(value * value, keepdims=True) / (W * W) + 1e-06)
    panel = precond[pl.ds(pl.multiple_of(owner[dp] * 16, 16), 16), :] / scale
    lane = lax.broadcasted_iota(jnp.int32, (8, B), 1)
    for m in range(16):
        tile = panel[:, (m // 4) * B : (m // 4 + 1) * B]
        shift = -32 * (m % 4) % B
        upper = pltpu.roll(tile[:8], shift, 1) if shift else tile[:8]
        lower = pltpu.roll(tile[8:], (shift + 32) % B, 1) if (shift + 32) % B else tile[8:]
        out[m] = jnp.where(lane < 32, upper, jnp.where(lane < 64, lower, 0.0))


def unfold(tiles, out):
    out[:, :8, :] = tiles[:, :, :32]
    out[:, 8:, :] = tiles[:, :, 32:64]


def call(kernel, outs, scratch, *args, cost=None):
    places = {tuple: pltpu.SMEM, list: pl.ANY}
    estimate = {} if cost is None else dict(cost_estimate=pl.CostEstimate(flops=cost, transcendentals=0, bytes_accessed=1))
    return pl.pallas_call(
        kernel,
        out_shape=[jax.ShapeDtypeStruct(s, jnp.float32) for s in outs],
        in_specs=[pl.BlockSpec(memory_space=places.get(type(a), pltpu.VMEM)) for a in args],
        out_specs=[pl.BlockSpec(memory_space=pltpu.VMEM) for _ in outs],
        scratch_shapes=[pltpu.VMEM(s, jnp.float32) for s in scratch],
        compiler_params=pltpu.CompilerParams(vmem_limit_bytes=VMEM_LIMIT),
        **estimate,
    )(*[a[0] if type(a) in places else a for a in args])


def move(x, step):
    return lax.ppermute(x, "dp", CORE_PAIRS if step == 0 else PAIRS[step - 1])


def halve(own, received, after):
    half = own.shape[0] // 2

    def kernel(own, received, after, keep, give):
        give[...] = own[half:, :] + received[half:, :]
        keep[...] = own[:half, :] + received[:half, :]

    return call(kernel, [(half, B)] * 2, [], own, received, [after], cost=ADD_FLOPS)


def add(own, received, after):
    def kernel(own, received, after, out):
        out[...] = own[...] + received[...]

    return call(kernel, [own.shape], [], own, received, [after], cost=ADD_FLOPS)[0]


def join(near, far, after):
    half = near.shape[0]

    def kernel(near, far, after, out):
        out[:half, :] = near[...]
        out[half:, :] = far[...]

    return call(kernel, [(2 * half, B)], [], near, far, [after], cost=JOIN_FLOPS)[0]


def totals(first, second):
    (a, a_send), (b, b_send) = first, second
    def move_a(x, step):
        with jax.named_scope("factors"):
            return move(x, step)

    def move_b(x, step):
        with jax.named_scope("grad"):
            return move(x, step)

    a_in, b_in = move_a(a_send, 0), move_b(b_send, 0)
    for step in (1, 2, 3):
        a, a_give = halve(a, a_in, b)
        a_in = move_a(a_give, step)
        b, b_give = halve(b, b_in, a)
        b_in = move_b(b_give, step)
    for step in (4, 3):
        a = add(a, a_in, b)
        a_in = move_a(a, step)
        b = add(b, b_in, a)
        b_in = move_b(b, step)
    for step in (2, 1):
        a = join(a, a_in, b)
        a_in = move_a(a, step)
        b = join(b, b_in, a)
        b_in = move_b(b, step)
    return (a, a_in), (b, b_in)


def per_device(acts, grads_out, panel_owner):
    whole = (8 * ROWS, B)
    f_own, f_send, g_own, g_send = pl.pallas_call(
        front,
        out_shape=[jax.ShapeDtypeStruct(whole, jnp.float32)] * 4,
        in_specs=[pl.BlockSpec(memory_space=pltpu.HBM)] * 2,
        out_specs=[pl.BlockSpec(memory_space=pltpu.VMEM)] * 4,
        scratch_shapes=[pltpu.VMEM(acts.shape, acts.dtype)] * 2
        + [pltpu.VMEM((W, W), jnp.float32)] * 3
        + [pltpu.VMEM((B, B), jnp.float32), pltpu.SemaphoreType.DMA((acts.shape[0] // TOKENS, 2))],
        compiler_params=pltpu.CompilerParams(vmem_limit_bytes=FRONT_LIMIT),
    )(acts, grads_out)
    (f_near, f_far), (g_near, g_far) = totals((f_own, f_send), (g_own, g_send))
    with jax.named_scope("grad"):
        h_near, h_far = move(g_near, 0), move(g_far, 0)
    after = g_near
    (x_own,) = call(root, [(W, W)], [whole, (W, W), (B, B)], f_near, f_far, [after], cost=ROOT_FLOPS)
    with jax.named_scope("root"):
        x_other = move(x_own, 0)
    (mixed,) = call(mix, [(W, W)], [(W, W)], x_own, g_near, g_far, h_near, h_far, cost=MIX_FLOPS)
    (tiles,) = call(finish, [(16, 8, B)], [(W, W)], (panel_owner,), mixed, x_other)
    tiles = lax.all_to_all(tiles, "mp", split_axis=0, concat_axis=0, tiled=True)
    return call(unfold, [(16, 16, 32)], [], tiles)[0]


def solution(mesh):
    return jax.shard_map(
        per_device,
        mesh=mesh,
        in_specs=(P("dp", "mp"), P("dp", "mp"), P()),
        out_specs=P(None, "dp", "mp"),
        check_vma=False,
    )
```

time: 153 us -> 112 us (0.73)
  waiting for transfers between devices: 37 us -> 12.2 us
  starting transfers between devices: 83.6 us -> 74.3 us
  local copies, waits for them, and re-layouts: 3.66 us -> 0.01 us
  matrix products: 2.86 us -> 0 us
  Pallas kernels: 9.02 us -> 11.5 us
  other arithmetic: 2.34 us -> 0 us
    ppermute x19, waiting for transfers between devices: 37 us -> 12.2 us  [move(): return lax.ppermute(x, 'dp', CORE_PAIRS if step == 0 else PAIRS[step - 1])]
    ppermute x19, starting transfers between devices: 83.6 us -> 74.3 us  [move(): return lax.ppermute(x, 'dp', CORE_PAIRS if step == 0 else PAIRS[step - 1])]
    pallas_call x0 -> x1, Pallas kernels: none -> 3.63 us  [per_device(): pl.pallas_call(front, out_shape=[jax.ShapeDtypeStruct(whole, jnp.float32)...]
    dot_general x1 -> x0, matrix products: 2.86 us -> none  [per_device(): jnp.einsum('tb,tc->bc', acts, grads_out, preferred_element_type=jnp.float32)]
    unnamed x9 -> x2, local copies, waits for them, and re-layouts: 2.75 us -> 0.01 us
    pallas_call x4 -> x18, Pallas kernels: 9.02 us -> 7.82 us  [call(): pl.pallas_call(kernel, out_shape=[jax.ShapeDtypeStruct(s, jnp.float32) fo...]
  transfers between devices with their start and end apart: 19 -> 19, of which waited for: 11 -> 7; matrix products, arithmetic and copies ran while one was open for 0% -> 0% of each run, Pallas kernels for 3% -> 5%
where the time goes in v2:
time: 112 us; the launch traced here: 111 us
  starting transfers between devices  74.3 us (66%)
  blocking collectives  12.7 us (11%)
  waiting for transfers between devices  12.2 us (11%)
  Pallas kernels  11.5 us (10%)
    ppermute x19, starting transfers between devices, move(): return lax.ppermute(x, 'dp', CORE_PAIRS if step == 0 else PAIRS[step - 1])  74.3 us
    all_to_all x1, blocking collectives, per_device(): tiles = lax.all_to_all(tiles, 'mp', split_axis=0, concat_axis=0, tiled=True)  12.7 us
    ppermute x19, waiting for transfers between devices, move(): return lax.ppermute(x, 'dp', CORE_PAIRS if step == 0 else PAIRS[step - 1])  12.2 us
    pallas_call x18, Pallas kernels, call(): pl.pallas_call(kernel, out_shape=[jax.ShapeDtypeStruct(s, jnp.float32) fo...  7.82 us
    pallas_call x1, Pallas kernels, per_device(): pl.pallas_call(front, out_shape=[jax.ShapeDtypeStruct(whole, jnp.float32)...  3.63 us
  transfers between devices with their start and end apart: 19, of which 7 were waited for; matrix products, arithmetic and copies ran while one was open for 0% of the time, Pallas kernels for 5%

profile of v2, /device:TPU:1, one launch (start us, length us, event | category | flops | bytes accessed | tf_op | source)
XLA Modules:
  0.0 111.1 jit_solution(14388112095726335846)
XLA Ops:
  0.0 3.6 %shard_map.37 = (f32[1152,128]{1,0:T(8,128)S(1)}, f32[1152,128]{1,0:T(8,128)S(1)}, f32[1152,128]{1,0:T(8,128)S(1)}, f32[1152,128]{1,0:T(8,128)S(1)}) custom-call(bf16[2048,512]{1,0:T(8,128)(2,1)} %acts.1, bf16[2048,512]{1,0:T(8,128)(2,1)} %grads_out.1), custom_call_target="tpu_custom_call" | custom-call | tf_op jit(solution)/shard_map/pallas_call | solution.py:341
  3.6 8.8 %collective-permute-start = (f32[1152,128]{1,0:T(8,128)S(1)}, f32[1152,128]{1,0:T(8,128)S(1)}, u32[]{:S(2)}, u32[]{:S(2)}) collective-permute-start(f32[1152,128]{1,0:T(8,128)S(1)} %get-tuple-element.22), channel_id=1, source_target_pairs={{0,16},{16,0},{32,48},{48,32},{64,80},{80,64},{96,112},{112,96},{1... | collective-permute-start | bytes 1769480 | tf_op jit(solution)/shard_map/factors/ppermute | solution.py:280
  12.4 1.9 %collective-permute-start.2 = (f32[1152,128]{1,0:T(8,128)S(1)}, f32[1152,128]{1,0:T(8,128)S(1)}, u32[]{:S(2)}, u32[]{:S(2)}) collective-permute-start(f32[1152,128]{1,0:T(8,128)S(1)} %get-tuple-element.26), channel_id=1, source_target_pairs={{0,16},{16,0},{32,48},{48,32},{64,80},{80,64},{96,112},{112,96},{1... | collective-permute-start | bytes 1769480 | tf_op jit(solution)/shard_map/grad/ppermute | solution.py:280
  14.4 0.0 collective-permute-done.received
  14.4 0.1 shard_map.38
  14.5 5.7 %collective-permute-start.1 = (f32[576,128]{1,0:T(8,128)S(1)}, f32[576,128]{1,0:T(8,128)S(1)}, u32[]{:S(2)}, u32[]{:S(2)}) collective-permute-start(f32[576,128]{1,0:T(8,128)S(1)} %get-tuple-element.25), channel_id=1, source_target_pairs={{0,32},{16,496},{32,0},{48,80},{64,96},{80,48},{96,64},{112,144},{... | collective-permute-start | bytes 884744 | tf_op jit(solution)/shard_map/factors/ppermute | solution.py:280
  20.2 0.0 collective-permute-done.2.received
  20.2 0.1 shard_map.39
  20.3 1.9 %collective-permute-start.4 = (f32[576,128]{1,0:T(8,128)S(1)}, f32[576,128]{1,0:T(8,128)S(1)}, u32[]{:S(2)}, u32[]{:S(2)}) collective-permute-start(f32[576,128]{1,0:T(8,128)S(1)} %get-tuple-element.30), channel_id=1, source_target_pairs={{0,32},{16,496},{32,0},{48,80},{64,96},{80,48},{96,64},{112,144},{... | collective-permute-start | bytes 884744 | tf_op jit(solution)/shard_map/grad/ppermute | solution.py:280
  22.2 2.1 %collective-permute-done.1.received = f32[576,128]{1,0:T(8,128)S(1)} collective-permute-done((f32[576,128]{1,0:T(8,128)S(1)}, f32[576,128]{1,0:T(8,128)S(1)}, u32[]{:S(2)}, u32[]{:S(2)}) %collective-permute-start.1) | collective-permute-done | bytes 294944 | tf_op jit(solution)/shard_map/factors/ppermute | solution.py:280
  24.3 1.9 %collective-permute-start.3 = (f32[288,128]{1,0:T(8,128)S(1)}, f32[288,128]{1,0:T(8,128)S(1)}, u32[]{:S(2)}, u32[]{:S(2)}) collective-permute-start(f32[288,128]{1,0:T(8,128)S(1)} %get-tuple-element.29), channel_id=1, source_target_pairs={{0,480},{16,48},{32,64},{48,16},{64,32},{80,112},{96,128},{112,80}... | collective-permute-start | bytes 442376 | tf_op jit(solution)/shard_map/factors/ppermute | solution.py:280
  26.3 2.7 %collective-permute-done.4.received = f32[576,128]{1,0:T(8,128)S(1)} collective-permute-done((f32[576,128]{1,0:T(8,128)S(1)}, f32[576,128]{1,0:T(8,128)S(1)}, u32[]{:S(2)}, u32[]{:S(2)}) %collective-permute-start.4) | collective-permute-done | bytes 294944 | tf_op jit(solution)/shard_map/grad/ppermute | solution.py:280
  29.0 1.9 %collective-permute-start.6 = (f32[288,128]{1,0:T(8,128)S(1)}, f32[288,128]{1,0:T(8,128)S(1)}, u32[]{:S(2)}, u32[]{:S(2)}) collective-permute-start(f32[288,128]{1,0:T(8,128)S(1)} %get-tuple-element.34), channel_id=1, source_target_pairs={{0,480},{16,48},{32,64},{48,16},{64,32},{80,112},{96,128},{112,80}... | collective-permute-start | bytes 442376 | tf_op jit(solution)/shard_map/grad/ppermute | solution.py:280
  30.9 0.0 collective-permute-done.3.received
  31.0 5.5 %collective-permute-start.5 = (f32[144,128]{1,0:T(8,128)S(1)}, f32[144,128]{1,0:T(8,128)S(1)}, u32[]{:S(2)}, u32[]{:S(2)}) collective-permute-start(f32[144,128]{1,0:T(8,128)S(1)} %get-tuple-element.33), channel_id=1, source_target_pairs={{0,96},{16,432},{32,448},{48,144},{64,160},{80,496},{96,0},{112,20... | collective-permute-start | bytes 221192 | tf_op jit(solution)/shard_map/factors/ppermute | solution.py:280
  36.4 0.0 collective-permute-done.6.received
  36.5 2.8 %collective-permute-start.8 = (f32[144,128]{1,0:T(8,128)S(1)}, f32[144,128]{1,0:T(8,128)S(1)}, u32[]{:S(2)}, u32[]{:S(2)}) collective-permute-start(f32[144,128]{1,0:T(8,128)S(1)} %get-tuple-element.36), channel_id=1, source_target_pairs={{0,96},{16,432},{32,448},{48,144},{64,160},{80,496},{96,0},{112,20... | collective-permute-start | bytes 221192 | tf_op jit(solution)/shard_map/grad/ppermute | solution.py:280
  39.3 0.0 collective-permute-done.5.received
  39.3 5.2 %collective-permute-start.7 = (f32[144,128]{1,0:T(8,128)S(1)}, f32[144,128]{1,0:T(8,128)S(1)}, u32[]{:S(2)}, u32[]{:S(2)}) collective-permute-start(f32[144,128]{1,0:T(8,128)S(1)} %shard_map.44.after.own), channel_id=1, source_target_pairs={{0,352},{16,176},{32,192},{48,400},{64,416},{80,240},{96,256},{112... | collective-permute-start | bytes 221192 | tf_op jit(solution)/shard_map/factors/ppermute | solution.py:280
  44.5 0.0 collective-permute-done.8.received
  44.6 5.0 %collective-permute-start.10 = (f32[144,128]{1,0:T(8,128)S(1)}, f32[144,128]{1,0:T(8,128)S(1)}, u32[]{:S(2)}, u32[]{:S(2)}) collective-permute-start(f32[144,128]{1,0:T(8,128)S(1)} %shard_map.45.after.own), channel_id=1, source_target_pairs={{0,352},{16,176},{32,192},{48,400},{64,416},{80,240},{96,256},{112... | collective-permute-start | bytes 221192 | tf_op jit(solution)/shard_map/grad/ppermute | solution.py:280
  49.6 0.1 collective-permute-done.7.received
  49.7 7.5 %collective-permute-start.9 = (f32[144,128]{1,0:T(8,128)S(1)}, f32[144,128]{1,0:T(8,128)S(1)}, u32[]{:S(2)}, u32[]{:S(2)}) collective-permute-start(f32[144,128]{1,0:T(8,128)S(1)} %shard_map.46.after.near), channel_id=1, source_target_pairs={{0,96},{16,432},{32,448},{48,144},{64,160},{80,496},{96,0},{112,20... | collective-permute-start | bytes 221192 | tf_op jit(solution)/shard_map/factors/ppermute | solution.py:280
  57.2 0.0 collective-permute-done.10.received
  57.3 4.6 %collective-permute-start.12 = (f32[144,128]{1,0:T(8,128)S(1)}, f32[144,128]{1,0:T(8,128)S(1)}, u32[]{:S(2)}, u32[]{:S(2)}) collective-permute-start(f32[144,128]{1,0:T(8,128)S(1)} %shard_map.47.after.near), channel_id=1, source_target_pairs={{0,96},{16,432},{32,448},{48,144},{64,160},{80,496},{96,0},{112,20... | collective-permute-start | bytes 221192 | tf_op jit(solution)/shard_map/grad/ppermute | solution.py:280
  61.9 0.0 collective-permute-done.9.far
  61.9 1.9 %collective-permute-start.11 = (f32[288,128]{1,0:T(8,128)S(1)}, f32[288,128]{1,0:T(8,128)S(1)}, u32[]{:S(2)}, u32[]{:S(2)}) collective-permute-start(f32[288,128]{1,0:T(8,128)S(1)} %shard_map.48.after.near), channel_id=1, source_target_pairs={{0,480},{16,48},{32,64},{48,16},{64,32},{80,112},{96,128},{112,80}... | collective-permute-start | bytes 442376 | tf_op jit(solution)/shard_map/factors/ppermute | solution.py:280
  63.8 2.9 %collective-permute-done.12.far = f32[144,128]{1,0:T(8,128)S(1)} collective-permute-done((f32[144,128]{1,0:T(8,128)S(1)}, f32[144,128]{1,0:T(8,128)S(1)}, u32[]{:S(2)}, u32[]{:S(2)}) %collective-permute-start.12) | collective-permute-done | bytes 73760 | tf_op jit(solution)/shard_map/grad/ppermute | solution.py:280
  66.7 1.9 %collective-permute-start.14 = (f32[288,128]{1,0:T(8,128)S(1)}, f32[288,128]{1,0:T(8,128)S(1)}, u32[]{:S(2)}, u32[]{:S(2)}) collective-permute-start(f32[288,128]{1,0:T(8,128)S(1)} %shard_map.49.after.near), channel_id=1, source_target_pairs={{0,480},{16,48},{32,64},{48,16},{64,32},{80,112},{96,128},{112,80}... | collective-permute-start | bytes 442376 | tf_op jit(solution)/shard_map/grad/ppermute | solution.py:280
  68.6 0.0 collective-permute-done.11.far
  68.7 3.2 %collective-permute-start.13 = (f32[576,128]{1,0:T(8,128)S(1)}, f32[576,128]{1,0:T(8,128)S(1)}, u32[]{:S(2)}, u32[]{:S(2)}) collective-permute-start(f32[576,128]{1,0:T(8,128)S(1)} %shard_map.50.after.near), channel_id=1, source_target_pairs={{0,32},{16,496},{32,0},{48,80},{64,96},{80,48},{96,64},{112,144},{... | collective-permute-start | bytes 884744 | tf_op jit(solution)/shard_map/factors/ppermute | solution.py:280
  71.9 1.0 collective-permute-done.14.far
  72.9 2.3 %collective-permute-start.15 = (f32[576,128]{1,0:T(8,128)S(1)}, f32[576,128]{1,0:T(8,128)S(1)}, u32[]{:S(2)}, u32[]{:S(2)}) collective-permute-start(f32[576,128]{1,0:T(8,128)S(1)} %shard_map.51.after.g_near), channel_id=1, source_target_pairs={{0,32},{16,496},{32,0},{48,80},{64,96},{80,48},{96,64},{112,144},{... | collective-permute-start | bytes 884744 | tf_op jit(solution)/shard_map/grad/ppermute | solution.py:280
  75.2 2.1 %collective-permute-done.13.far = f32[576,128]{1,0:T(8,128)S(1)} collective-permute-done((f32[576,128]{1,0:T(8,128)S(1)}, f32[576,128]{1,0:T(8,128)S(1)}, u32[]{:S(2)}, u32[]{:S(2)}) %collective-permute-start.13) | collective-permute-done | bytes 294944 | tf_op jit(solution)/shard_map/factors/ppermute | solution.py:280
  77.4 3.5 %shard_map.52.x = f32[512,512]{1,0:T(8,128)S(1)} custom-call(f32[576,128]{1,0:T(8,128)S(1)} %shard_map.50.after.near, f32[576,128]{1,0:T(8,128)S(1)} %collective-permute-done.13.far, f32[576,128]{1,0:T(8,128)S(1)} %shard_map.51.after.g_near), custom_call_target="tpu_custom_call" | custom-call | bytes 1 | tf_op jit(solution)/shard_map/pallas_call | solution.py:268
  80.9 0.0 copy-start
  80.9 7.9 %collective-permute-start.18 = (f32[512,512]{1,0:T(8,128)S(1)}, f32[512,512]{1,0:T(8,128)S(1)}, u32[]{:S(2)}, u32[]{:S(2)}) collective-permute-start(f32[512,512]{1,0:T(8,128)S(1)} %shard_map.52.x), channel_id=1, source_target_pairs={{0,16},{16,0},{32,48},{48,32},{64,80},{80,64},{96,112},{112,96},{1... | collective-permute-start | bytes 3145736 | tf_op jit(solution)/shard_map/root/ppermute | solution.py:280
  88.7 1.9 %collective-permute-start.16 = (f32[576,128]{1,0:T(8,128)S(1)}, f32[576,128]{1,0:T(8,128)S(1)}, u32[]{:S(2)}, u32[]{:S(2)}) collective-permute-start(f32[576,128]{1,0:T(8,128)S(1)} %shard_map.51.after.g_near), channel_id=1, source_target_pairs={{0,16},{16,0},{32,48},{48,32},{64,80},{80,64},{96,112},{112,96},{1... | collective-permute-start | bytes 884744 | tf_op jit(solution)/shard_map/grad/ppermute | solution.py:280
  90.7 0.0 collective-permute-done.15.g_far
  90.7 2.4 %collective-permute-start.17 = (f32[576,128]{1,0:T(8,128)S(1)}, f32[576,128]{1,0:T(8,128)S(1)}, u32[]{:S(2)}, u32[]{:S(2)}) collective-permute-start(f32[576,128]{1,0:T(8,128)S(1)} %collective-permute-done.15.g_far), channel_id=1, source_target_pairs={{0,16},{16,0},{32,48},{48,32},{64,80},{80,64},{96,112},{112,96},{1... | collective-permute-start | bytes 884744 | tf_op jit(solution)/shard_map/grad/ppermute | solution.py:280
  93.1 0.0 collective-permute-done.16.h_near
  93.1 1.2 %collective-permute-done.17.h_far = f32[576,128]{1,0:T(8,128)S(1)} collective-permute-done((f32[576,128]{1,0:T(8,128)S(1)}, f32[576,128]{1,0:T(8,128)S(1)}, u32[]{:S(2)}, u32[]{:S(2)}) %collective-permute-start.17) | collective-permute-done | bytes 294944 | tf_op jit(solution)/shard_map/grad/ppermute | solution.py:280
  94.3 1.2 %shard_map.53.mixed = f32[512,512]{1,0:T(8,128)S(1)} custom-call(f32[512,512]{1,0:T(8,128)S(1)} %shard_map.52.x, f32[576,128]{1,0:T(8,128)S(1)} %shard_map.51.after.g_near, f32[576,128]{1,0:T(8,128)S(1)} %collective-permute-done.15.g_far, f32[576,128]{1,0:T(8,128)S(1)} %collective-permute-done.16.h_near, f32[576,128]{1,0:T(8,128)S(1)} %collective-permute-done.17.h_far), custom_call_target="tpu_custom_call" | custom-call | flops 5000000000 | bytes 1 | tf_op jit(solution)/shard_map/pallas_call | solution.py:268
  95.5 0.0 collective-permute-done.18.x
  95.5 0.0 copy-done
  95.5 2.0 %shard_map.54 = f32[16,8,128]{2,1,0:T(8,128)S(1)} custom-call(s32[32]{0:T(128)S(1)} %copy-done, f32[512,512]{1,0:T(8,128)S(1)} %shard_map.53.mixed, f32[512,512]{1,0:T(8,128)S(1)} %collective-permute-done.18.x), custom_call_target="tpu_custom_call" | custom-call | tf_op jit(solution)/shard_map/pallas_call | solution.py:268
  97.6 12.7 %all_to_all.5.tiles = f32[16,8,128]{2,1,0:T(8,128)S(1)} all-to-all(f32[16,8,128]{2,1,0:T(8,128)S(1)} %shard_map.54), channel_id=1, replica_groups=mesh['dp'=32,'mp'=16] {'mp'}, dimensions={0} | all-to-all | bytes 131072 | tf_op jit(solution)/shard_map/all_to_all | solution.py:360
  110.3 0.7 shard_map.55
  (12 shorter events, 0.2 us)
Async XLA Ops:
  3.6 10.7 %collective-permute-start = (f32[1152,128]{1,0:T(8,128)S(1)}, f32[1152,128]{1,0:T(8,128)S(1)}, u32[]{:S(2)}, u32[]{:S(2)}) collective-permute-start(f32[1152,128]{1,0:T(8,128)S(1)} %get-tuple-element.22), channel_id=1, source_target_pairs={{0,16},{16,0},{32,48},{48,32},{64,80},{80,64},{96,112},{112,96},{1... | collective-permute-start | bytes 1769480 | tf_op jit(solution)/shard_map/factors/ppermute | solution.py:280
  12.4 7.8 %collective-permute-start.2 = (f32[1152,128]{1,0:T(8,128)S(1)}, f32[1152,128]{1,0:T(8,128)S(1)}, u32[]{:S(2)}, u32[]{:S(2)}) collective-permute-start(f32[1152,128]{1,0:T(8,128)S(1)} %get-tuple-element.26), channel_id=1, source_target_pairs={{0,16},{16,0},{32,48},{48,32},{64,80},{80,64},{96,112},{112,96},{1... | collective-permute-start | bytes 1769480 | tf_op jit(solution)/shard_map/grad/ppermute | solution.py:280
  14.5 9.8 %collective-permute-start.1 = (f32[576,128]{1,0:T(8,128)S(1)}, f32[576,128]{1,0:T(8,128)S(1)}, u32[]{:S(2)}, u32[]{:S(2)}) collective-permute-start(f32[576,128]{1,0:T(8,128)S(1)} %get-tuple-element.25), channel_id=1, source_target_pairs={{0,32},{16,496},{32,0},{48,80},{64,96},{80,48},{96,64},{112,144},{... | collective-permute-start | bytes 884744 | tf_op jit(solution)/shard_map/factors/ppermute | solution.py:280
  20.3 8.7 %collective-permute-start.4 = (f32[576,128]{1,0:T(8,128)S(1)}, f32[576,128]{1,0:T(8,128)S(1)}, u32[]{:S(2)}, u32[]{:S(2)}) collective-permute-start(f32[576,128]{1,0:T(8,128)S(1)} %get-tuple-element.30), channel_id=1, source_target_pairs={{0,32},{16,496},{32,0},{48,80},{64,96},{80,48},{96,64},{112,144},{... | collective-permute-start | bytes 884744 | tf_op jit(solution)/shard_map/grad/ppermute | solution.py:280
  24.3 6.6 %collective-permute-start.3 = (f32[288,128]{1,0:T(8,128)S(1)}, f32[288,128]{1,0:T(8,128)S(1)}, u32[]{:S(2)}, u32[]{:S(2)}) collective-permute-start(f32[288,128]{1,0:T(8,128)S(1)} %get-tuple-element.29), channel_id=1, source_target_pairs={{0,480},{16,48},{32,64},{48,16},{64,32},{80,112},{96,128},{112,80}... | collective-permute-start | bytes 442376 | tf_op jit(solution)/shard_map/factors/ppermute | solution.py:280
  29.0 7.4 %collective-permute-start.6 = (f32[288,128]{1,0:T(8,128)S(1)}, f32[288,128]{1,0:T(8,128)S(1)}, u32[]{:S(2)}, u32[]{:S(2)}) collective-permute-start(f32[288,128]{1,0:T(8,128)S(1)} %get-tuple-element.34), channel_id=1, source_target_pairs={{0,480},{16,48},{32,64},{48,16},{64,32},{80,112},{96,128},{112,80}... | collective-permute-start | bytes 442376 | tf_op jit(solution)/shard_map/grad/ppermute | solution.py:280
  31.0 8.3 %collective-permute-start.5 = (f32[144,128]{1,0:T(8,128)S(1)}, f32[144,128]{1,0:T(8,128)S(1)}, u32[]{:S(2)}, u32[]{:S(2)}) collective-permute-start(f32[144,128]{1,0:T(8,128)S(1)} %get-tuple-element.33), channel_id=1, source_target_pairs={{0,96},{16,432},{32,448},{48,144},{64,160},{80,496},{96,0},{112,20... | collective-permute-start | bytes 221192 | tf_op jit(solution)/shard_map/factors/ppermute | solution.py:280
  36.5 8.1 %collective-permute-start.8 = (f32[144,128]{1,0:T(8,128)S(1)}, f32[144,128]{1,0:T(8,128)S(1)}, u32[]{:S(2)}, u32[]{:S(2)}) collective-permute-start(f32[144,128]{1,0:T(8,128)S(1)} %get-tuple-element.36), channel_id=1, source_target_pairs={{0,96},{16,432},{32,448},{48,144},{64,160},{80,496},{96,0},{112,20... | collective-permute-start | bytes 221192 | tf_op jit(solution)/shard_map/grad/ppermute | solution.py:280
  39.3 10.4 %collective-permute-start.7 = (f32[144,128]{1,0:T(8,128)S(1)}, f32[144,128]{1,0:T(8,128)S(1)}, u32[]{:S(2)}, u32[]{:S(2)}) collective-permute-start(f32[144,128]{1,0:T(8,128)S(1)} %shard_map.44.after.own), channel_id=1, source_target_pairs={{0,352},{16,176},{32,192},{48,400},{64,416},{80,240},{96,256},{112... | collective-permute-start | bytes 221192 | tf_op jit(solution)/shard_map/factors/ppermute | solution.py:280
  44.6 12.7 %collective-permute-start.10 = (f32[144,128]{1,0:T(8,128)S(1)}, f32[144,128]{1,0:T(8,128)S(1)}, u32[]{:S(2)}, u32[]{:S(2)}) collective-permute-start(f32[144,128]{1,0:T(8,128)S(1)} %shard_map.45.after.own), channel_id=1, source_target_pairs={{0,352},{16,176},{32,192},{48,400},{64,416},{80,240},{96,256},{112... | collective-permute-start | bytes 221192 | tf_op jit(solution)/shard_map/grad/ppermute | solution.py:280
  49.7 12.1 %collective-permute-start.9 = (f32[144,128]{1,0:T(8,128)S(1)}, f32[144,128]{1,0:T(8,128)S(1)}, u32[]{:S(2)}, u32[]{:S(2)}) collective-permute-start(f32[144,128]{1,0:T(8,128)S(1)} %shard_map.46.after.near), channel_id=1, source_target_pairs={{0,96},{16,432},{32,448},{48,144},{64,160},{80,496},{96,0},{112,20... | collective-permute-start | bytes 221192 | tf_op jit(solution)/shard_map/factors/ppermute | solution.py:280
  57.3 9.4 %collective-permute-start.12 = (f32[144,128]{1,0:T(8,128)S(1)}, f32[144,128]{1,0:T(8,128)S(1)}, u32[]{:S(2)}, u32[]{:S(2)}) collective-permute-start(f32[144,128]{1,0:T(8,128)S(1)} %shard_map.47.after.near), channel_id=1, source_target_pairs={{0,96},{16,432},{32,448},{48,144},{64,160},{80,496},{96,0},{112,20... | collective-permute-start | bytes 221192 | tf_op jit(solution)/shard_map/grad/ppermute | solution.py:280
  61.9 6.8 %collective-permute-start.11 = (f32[288,128]{1,0:T(8,128)S(1)}, f32[288,128]{1,0:T(8,128)S(1)}, u32[]{:S(2)}, u32[]{:S(2)}) collective-permute-start(f32[288,128]{1,0:T(8,128)S(1)} %shard_map.48.after.near), channel_id=1, source_target_pairs={{0,480},{16,48},{32,64},{48,16},{64,32},{80,112},{96,128},{112,80}... | collective-permute-start | bytes 442376 | tf_op jit(solution)/shard_map/factors/ppermute | solution.py:280
  66.7 6.2 %collective-permute-start.14 = (f32[288,128]{1,0:T(8,128)S(1)}, f32[288,128]{1,0:T(8,128)S(1)}, u32[]{:S(2)}, u32[]{:S(2)}) collective-permute-start(f32[288,128]{1,0:T(8,128)S(1)} %shard_map.49.after.near), channel_id=1, source_target_pairs={{0,480},{16,48},{32,64},{48,16},{64,32},{80,112},{96,128},{112,80}... | collective-permute-start | bytes 442376 | tf_op jit(solution)/shard_map/grad/ppermute | solution.py:280
  68.7 8.7 %collective-permute-start.13 = (f32[576,128]{1,0:T(8,128)S(1)}, f32[576,128]{1,0:T(8,128)S(1)}, u32[]{:S(2)}, u32[]{:S(2)}) collective-permute-start(f32[576,128]{1,0:T(8,128)S(1)} %shard_map.50.after.near), channel_id=1, source_target_pairs={{0,32},{16,496},{32,0},{48,80},{64,96},{80,48},{96,64},{112,144},{... | collective-permute-start | bytes 884744 | tf_op jit(solution)/shard_map/factors/ppermute | solution.py:280
  72.9 17.7 %collective-permute-start.15 = (f32[576,128]{1,0:T(8,128)S(1)}, f32[576,128]{1,0:T(8,128)S(1)}, u32[]{:S(2)}, u32[]{:S(2)}) collective-permute-start(f32[576,128]{1,0:T(8,128)S(1)} %shard_map.51.after.g_near), channel_id=1, source_target_pairs={{0,32},{16,496},{32,0},{48,80},{64,96},{80,48},{96,64},{112,144},{... | collective-permute-start | bytes 884744 | tf_op jit(solution)/shard_map/grad/ppermute | solution.py:280
  80.9 14.7 %copy-start = (s32[32]{0:T(128)S(1)}, s32[32]{0:T(128)}, u32[]{:S(2)}) copy-start(s32[32]{0:T(128)} %owner.1) | copy-start | bytes 388
  80.9 14.6 %collective-permute-start.18 = (f32[512,512]{1,0:T(8,128)S(1)}, f32[512,512]{1,0:T(8,128)S(1)}, u32[]{:S(2)}, u32[]{:S(2)}) collective-permute-start(f32[512,512]{1,0:T(8,128)S(1)} %shard_map.52.x), channel_id=1, source_target_pairs={{0,16},{16,0},{32,48},{48,32},{64,80},{80,64},{96,112},{112,96},{1... | collective-permute-start | bytes 3145736 | tf_op jit(solution)/shard_map/root/ppermute | solution.py:280
  88.7 4.4 %collective-permute-start.16 = (f32[576,128]{1,0:T(8,128)S(1)}, f32[576,128]{1,0:T(8,128)S(1)}, u32[]{:S(2)}, u32[]{:S(2)}) collective-permute-start(f32[576,128]{1,0:T(8,128)S(1)} %shard_map.51.after.g_near), channel_id=1, source_target_pairs={{0,16},{16,0},{32,48},{48,32},{64,80},{80,64},{96,112},{112,96},{1... | collective-permute-start | bytes 884744 | tf_op jit(solution)/shard_map/grad/ppermute | solution.py:280
  90.7 3.6 %collective-permute-start.17 = (f32[576,128]{1,0:T(8,128)S(1)}, f32[576,128]{1,0:T(8,128)S(1)}, u32[]{:S(2)}, u32[]{:S(2)}) collective-permute-start(f32[576,128]{1,0:T(8,128)S(1)} %collective-permute-done.15.g_far), channel_id=1, source_target_pairs={{0,16},{16,0},{32,48},{48,32},{64,80},{80,64},{96,112},{112,96},{1... | collective-permute-start | bytes 884744 | tf_op jit(solution)/shard_map/grad/ppermute | solution.py:280

commit v3 on v2

v3 whole, which is shorter than its diff:
```python
import functools

import jax
import jax.numpy as jnp
from jax import lax
from jax.experimental import pallas as pl
from jax.experimental.pallas import tpu as pltpu
from jax.sharding import PartitionSpec as P

Z = 16
W = 512
B = 128
ROWS = 136
OFF = ((0, 1), (0, 2), (0, 3), (1, 2), (1, 3), (2, 3))
F_FINE = True
G_FINE = True
JOIN_FLOPS = 4_000_000_000
ADD_FLOPS = 0
ROOT_FLOPS = 0

MIX_FLOPS = 5_000_000_000
TOKENS = 512
FRONT_LIMIT = 51 * 1024 * 1024
VMEM_LIMIT = 40 * 1024 * 1024


def partner1(v):
    return v ^ 1


def partner2(v):
    return (((v + 1) % Z) ^ 1) - 1 if ((v + 1) % Z) ^ 1 else Z - 1


def partner3(v):
    return v + 3 if v % 4 == 0 else v - 3 if v % 4 == 3 else (v + 3) % Z if v % 4 == 2 else (v - 3) % Z


def partner4(v):
    return (v + 5) % Z if v % 2 else (v - 5) % Z


EIGHTH = {3: 0, 8: 0, 0: 1, 11: 1, 7: 2, 12: 2, 4: 3, 15: 3, 9: 4, 14: 4, 1: 5, 6: 5, 5: 6, 10: 6, 2: 7, 13: 7}


def holders(v, partners):
    if not partners:
        return [v]
    return holders(v, partners[:-1]) + holders(partners[-1](v), partners[:-1])


def local_order(v, fine):
    order = [EIGHTH[u] for u in holders(v, (partner3, partner2, partner1) if fine else (partner2, partner1))]
    if not fine:
        order = [e for own in order for e in (own & 6, own | 1)]
    assert sorted(order) == list(range(8))
    return order


def position(z, core):
    return z if core == 0 else (-z) % Z


def order_code(v, fine):
    order = local_order(v, fine)
    return sum(order.index(e) << (3 * e) for e in range(8))


def places(own, fine):
    dp = lax.axis_index("dp")
    z, core = dp // 2, dp % 2
    v = jnp.where((core == 0) == own, z, (Z - z) % Z)
    code = jnp.int32(order_code(0, fine))
    for u in range(1, Z):
        code = jnp.where(v == u, order_code(u, fine), code)
    return [(code >> (3 * e)) & 7 for e in range(8)]


def ring_pairs(partner):
    pairs = []
    for z in range(Z):
        for core in range(2):
            pairs.append((2 * z + core, 2 * position(partner(position(z, core)), core) + core))
    return pairs


CORE_PAIRS = [(i, i ^ 1) for i in range(2 * Z)]
PAIRS = [ring_pairs(p) for p in (partner1, partner2, partner3, partner4)]


def split(x):
    high = x.astype(jnp.bfloat16)
    low = (x - high.astype(jnp.float32)).astype(jnp.bfloat16)
    return high, low


def dot(a, b, dims=((1,), (0,))):
    return lax.dot_general(a, b, (dims, ((), ())), preferred_element_type=jnp.float32)


def product(a, b):
    (ah, al), (bh, bl) = a, b
    return dot(ah, bh) + (dot(ah, bl) + dot(al, bh))


def rows_of(index, size):
    return pl.ds(pl.multiple_of(index * ROWS, 8), size)


def put_gradient(grad, dst, half, place):
    for e in range(8):
        r, c = half * 256 + (e // 4) * B, (e % 4) * B
        dst[rows_of(place[e], B), :] = grad[r : r + B, c : c + B]
        dst[pl.ds(pl.multiple_of(place[e] * ROWS + B, 8), ROWS - B), :] = jnp.zeros((ROWS - B, B), jnp.float32)


def block_iota():
    return (lax.broadcasted_iota(jnp.int32, (B, B), n) for n in range(2))


def put_factor(src, dst, place):
    row, col = block_iota()
    for e in range(8):
        base = place[e] * ROWS
        extra = jnp.zeros((ROWS - B, B), jnp.float32)
        if e < 6:
            i, j = OFF[e]
            block = src[i * B : (i + 1) * B, j * B : (j + 1) * B]
        else:
            i = 2 * e - 12
            first = src[i * B : (i + 1) * B, i * B : (i + 1) * B]
            second = src[(i + 1) * B : (i + 2) * B, (i + 1) * B : (i + 2) * B]
            block = jnp.where(row <= col, first, second)
            extra = extra + jnp.sum(jnp.where(row == col, second, 0.0), axis=0, keepdims=True)
        dst[pl.ds(pl.multiple_of(base, 8), B), :] = block
        dst[pl.ds(pl.multiple_of(base + B, 8), ROWS - B), :] = extra


def take_factor(packed, factor, place):
    row, col = block_iota()
    for e in range(8):
        base = place[e] * ROWS
        block = packed[pl.ds(pl.multiple_of(base, 8), B), :]
        turned = block.T
        if e < 6:
            i, j = OFF[e]
            factor[i * B : (i + 1) * B, j * B : (j + 1) * B] = block
            factor[j * B : (j + 1) * B, i * B : (i + 1) * B] = turned
        else:
            i = 2 * e - 12
            diagonal = packed[pl.ds(pl.multiple_of(base + B, 8), ROWS - B), :][:1, :]
            factor[i * B : (i + 1) * B, i * B : (i + 1) * B] = jnp.where(row <= col, block, turned)
            factor[(i + 1) * B : (i + 2) * B, (i + 1) * B : (i + 2) * B] = jnp.where(
                row > col, block, jnp.where(row < col, turned, diagonal)
            )


def front(acts, grads_out, f_own, f_send, g_own, g_send, a_vmem, g_vmem, grad, left, right, sems):
    copies = []
    for i in range(acts.shape[0] // TOKENS):
        rows = pl.ds(i * TOKENS, TOKENS)
        pair = [
            pltpu.make_async_copy(src.at[rows], dst.at[rows], sems.at[i, n])
            for n, (src, dst) in enumerate(((acts, a_vmem), (grads_out, g_vmem)))
        ]
        for copy in pair:
            copy.start()
        copies.append(pair)
    f_place, f_other = places(True, F_FINE), places(False, F_FINE)
    g_place, g_other = places(True, G_FINE), places(False, G_FINE)
    core = lax.axis_index("dp") % 2
    for i, pair in enumerate(copies):
        for copy in pair:
            copy.wait()
        rows = slice(i * TOKENS, (i + 1) * TOKENS)
        part = dot(a_vmem[rows, :], g_vmem[rows, :], ((0,), (0,)))
        grad[...] = part if i == 0 else grad[...] + part
    low = grad[...].astype(jnp.bfloat16)
    left[...] = dot(low, low, ((1,), (1,)))
    right[...] = dot(low, low, ((0,), (0,)))

    @pl.when(core == 0)
    def _():
        put_factor(left, f_own, f_place)
        put_factor(right, f_send, f_other)
        put_gradient(grad, g_own, 0, g_place)
        put_gradient(grad, g_send, 1, g_other)

    @pl.when(core == 1)
    def _():
        put_factor(right, f_own, f_place)
        put_factor(left, f_send, f_other)
        put_gradient(grad, g_own, 1, g_place)
        put_gradient(grad, g_send, 0, g_other)


def root(near, far, after, out, packed, factor):
    packed[: 4 * ROWS, :] = near[...]
    packed[4 * ROWS :, :] = far[...]
    take_factor(packed, factor, places(True, F_FINE))
    f = factor[...]
    norm = jnp.sqrt(jnp.sum(f * f, keepdims=True) + 1e-06)
    m1 = f / norm
    s1 = split(m1)
    m2 = product(s1, s1)
    s2 = split(m2)
    m3 = product(s2, s1)
    c = 1.0 / 4096.0
    high = (250.0 * c) * m1 - (25.0 * c) * m2 + c * m3
    low = (-5.0 / 16.0 - 3125.0 * c) * m1 + (3125.0 * c) * m2 - (1250.0 * c) * m3
    diagonal = lax.broadcasted_iota(jnp.int32, (W, W), 0) == lax.broadcasted_iota(jnp.int32, (W, W), 1)
    low = low + jnp.where(diagonal, 25.0 / 16.0, 0.0)
    x = low + product(split(m3), split(high))
    out[...] = x * lax.rsqrt(jnp.sqrt(norm))


def mix(x, own, other, high, low, grad):
    core = lax.axis_index("dp") % 2

    def take(src, half, place):
        for e in range(8):
            r, c = half * 256 + (e // 4) * B, (e % 4) * B
            grad[r : r + B, c : c + B] = src[rows_of(place[e], B), :]

    def put(value):
        high[...], low[...] = split(value)

    @pl.when(core == 0)
    def _():
        take(own, 0, places(True, G_FINE))
        take(other, 1, places(False, G_FINE))
        put(product(split(x[...]), split(grad[...])))

    @pl.when(core == 1)
    def _():
        take(own, 1, places(True, G_FINE))
        take(other, 0, places(False, G_FINE))
        put(product(split(grad[...]), split(x[...])))


def finish(owner, high, low, x, out, precond):
    dp = lax.axis_index("dp")

    @pl.when(dp % 2 == 0)
    def _():
        precond[...] = product((high[...], low[...]), split(x[...]))

    @pl.when(dp % 2 == 1)
    def _():
        precond[...] = product(split(x[...]), (high[...], low[...]))

    value = precond[...]
    scale = jnp.sqrt(jnp.sum(value * value, keepdims=True) / (W * W) + 1e-06)
    panel = precond[pl.ds(pl.multiple_of(owner[dp] * 16, 16), 16), :] / scale
    lane = lax.broadcasted_iota(jnp.int32, (8, B), 1)
    for m in range(16):
        tile = panel[:, (m // 4) * B : (m // 4 + 1) * B]
        shift = -32 * (m % 4) % B
        upper = pltpu.roll(tile[:8], shift, 1) if shift else tile[:8]
        lower = pltpu.roll(tile[8:], (shift + 32) % B, 1) if (shift + 32) % B else tile[8:]
        out[m] = jnp.where(lane < 32, upper, jnp.where(lane < 64, lower, 0.0))


def unfold(tiles, out):
    out[:, :8, :] = tiles[:, :, :32]
    out[:, 8:, :] = tiles[:, :, 32:64]


def call(kernel, outs, scratch, *args, cost=None, dtype=jnp.float32):
    places = {tuple: pltpu.SMEM, list: pl.ANY}
    estimate = {} if cost is None else dict(cost_estimate=pl.CostEstimate(flops=cost, transcendentals=0, bytes_accessed=1))
    return pl.pallas_call(
        kernel,
        out_shape=[jax.ShapeDtypeStruct(s, dtype) for s in outs],
        in_specs=[pl.BlockSpec(memory_space=places.get(type(a), pltpu.VMEM)) for a in args],
        out_specs=[pl.BlockSpec(memory_space=pltpu.VMEM) for _ in outs],
        scratch_shapes=[pltpu.VMEM(s, jnp.float32) for s in scratch],
        compiler_params=pltpu.CompilerParams(vmem_limit_bytes=VMEM_LIMIT),
        **estimate,
    )(*[a[0] if type(a) in places else a for a in args])


def move(x, step):
    return lax.ppermute(x, "dp", CORE_PAIRS if step == 0 else PAIRS[step - 1])


def halve(own, received, after):
    half = own.shape[0] // 2

    def kernel(own, received, after, keep, give):
        give[...] = own[half:, :] + received[half:, :]
        keep[...] = own[:half, :] + received[:half, :]

    return call(kernel, [(half, B)] * 2, [], own, received, [after], cost=ADD_FLOPS)


def add(own, received, after):
    def kernel(own, received, after, out):
        out[...] = own[...] + received[...]

    return call(kernel, [own.shape], [], own, received, [after], cost=ADD_FLOPS)[0]


def join(near, far, after):
    half = near.shape[0]

    def kernel(near, far, after, out):
        out[:half, :] = near[...]
        out[half:, :] = far[...]

    return call(kernel, [(2 * half, B)], [], near, far, [after], cost=JOIN_FLOPS)[0]


FINE = ((halve, 1), (halve, 2), (halve, 3), (add, 4), (add, 3), (join, 2), (join, 1))
COARSE = ((halve, 1), (halve, 2), (add, 3), (add, 4), (add, 2), (join, 1))
WAYS = {True: FINE, False: COARSE}


def totals(first, second):
    (a, a_send), (b, b_send) = first, second
    def move_a(x, step):
        with jax.named_scope("factors"):
            return move(x, step)

    def move_b(x, step):
        with jax.named_scope("grad"):
            return move(x, step)

    def advance(own, received, after, way, move):
        combine, step = way
        if combine is halve:
            own, give = halve(own, received, after)
            return own, move(give, step)
        own = combine(own, received, after)
        return own, move(own, step)

    a_in, b_in = move_a(a_send, 0), move_b(b_send, 0)
    a_way, b_way = WAYS[F_FINE], WAYS[G_FINE]
    for i in range(max(len(a_way), len(b_way))):
        if i < len(a_way):
            a, a_in = advance(a, a_in, b, a_way[i], move_a)
        if i < len(b_way):
            b, b_in = advance(b, b_in, a, b_way[i], move_b)
    return (a, a_in), (b, b_in)


def per_device(acts, grads_out, panel_owner):
    whole = (8 * ROWS, B)
    f_own, f_send, g_own, g_send = pl.pallas_call(
        front,
        out_shape=[jax.ShapeDtypeStruct(whole, jnp.float32)] * 4,
        in_specs=[pl.BlockSpec(memory_space=pltpu.HBM)] * 2,
        out_specs=[pl.BlockSpec(memory_space=pltpu.VMEM)] * 4,
        scratch_shapes=[pltpu.VMEM(acts.shape, acts.dtype)] * 2
        + [pltpu.VMEM((W, W), jnp.float32)] * 3
        + [pltpu.SemaphoreType.DMA((acts.shape[0] // TOKENS, 2))],
        compiler_params=pltpu.CompilerParams(vmem_limit_bytes=FRONT_LIMIT),
    )(acts, grads_out)
    (f_near, f_far), (g_near, g_far) = totals((f_own, f_send), (g_own, g_send))
    g_sum = join(g_near, g_far, f_near)
    with jax.named_scope("grad"):
        g_other = move(g_sum, 0)
    (x_own,) = call(root, [(W, W)], [whole, (W, W)], f_near, f_far, [g_near], cost=ROOT_FLOPS)
    with jax.named_scope("root"):
        x_other = move(x_own, 0)
    high, low = call(mix, [(W, W)] * 2, [(W, W)], x_own, g_sum, g_other, cost=MIX_FLOPS, dtype=jnp.bfloat16)
    (tiles,) = call(finish, [(16, 8, B)], [(W, W)], (panel_owner,), high, low, x_other)
    tiles = lax.all_to_all(tiles, "mp", split_axis=0, concat_axis=0, tiled=True)
    return call(unfold, [(16, 16, 32)], [], tiles)[0]


def solution(mesh):
    return jax.shard_map(
        per_device,
        mesh=mesh,
        in_specs=(P("dp", "mp"), P("dp", "mp"), P()),
        out_specs=P(None, "dp", "mp"),
        check_vma=False,
    )
```

time: 112 us -> 110 us (0.982)
  starting transfers between devices: 74.3 us -> 72.7 us
    ppermute x19 -> x18, starting transfers between devices: 74.3 us -> 72.7 us  [move(): return lax.ppermute(x, 'dp', CORE_PAIRS if step == 0 else PAIRS[step - 1])]
    ppermute x19 -> x18, waiting for transfers between devices: 12.2 us -> 11.4 us  [move(): return lax.ppermute(x, 'dp', CORE_PAIRS if step == 0 else PAIRS[step - 1])]
    pallas_call x18 -> x19, Pallas kernels: 7.82 us -> 7.71 us  [call(): pl.pallas_call(kernel, out_shape=[jax.ShapeDtypeStruct(s, dtype) for s in...]
  transfers between devices with their start and end apart: 19 -> 18, of which waited for: 7 -> 8; matrix products, arithmetic and copies ran while one was open for 0% -> 0% of each run, Pallas kernels for 5% -> 5%
where the time goes in v3:
time: 110 us; the launch traced here: 109 us
  starting transfers between devices  72.7 us (66%)
  blocking collectives  13.2 us (12%)
  waiting for transfers between devices  11.4 us (10%)
  Pallas kernels  11.3 us (10%)
    ppermute x18, starting transfers between devices, move(): return lax.ppermute(x, 'dp', CORE_PAIRS if step == 0 else PAIRS[step - 1])  72.7 us
    all_to_all x1, blocking collectives, per_device(): tiles = lax.all_to_all(tiles, 'mp', split_axis=0, concat_axis=0, tiled=True)  13.2 us
    ppermute x18, waiting for transfers between devices, move(): return lax.ppermute(x, 'dp', CORE_PAIRS if step == 0 else PAIRS[step - 1])  11.4 us
    pallas_call x19, Pallas kernels, call(): pl.pallas_call(kernel, out_shape=[jax.ShapeDtypeStruct(s, dtype) for s in...  7.71 us
    pallas_call x1, Pallas kernels, per_device(): pl.pallas_call(front, out_shape=[jax.ShapeDtypeStruct(whole, jnp.float32)...  3.64 us
  transfers between devices with their start and end apart: 18, of which 8 were waited for; matrix products, arithmetic and copies ran while one was open for 0% of the time, Pallas kernels for 5%

profile of v3, /device:TPU:1, one launch (start us, length us, event | category | flops | bytes accessed | tf_op | source)
XLA Modules:
  0.0 109.0 jit_solution(8226747435121668792)
XLA Ops:
  0.0 3.6 %shard_map.37 = (f32[1088,128]{1,0:T(8,128)S(1)}, f32[1088,128]{1,0:T(8,128)S(1)}, f32[1088,128]{1,0:T(8,128)S(1)}, f32[1088,128]{1,0:T(8,128)S(1)}) custom-call(bf16[2048,512]{1,0:T(8,128)(2,1)} %acts.1, bf16[2048,512]{1,0:T(8,128)(2,1)} %grads_out.1), custom_call_target="tpu_custom_call" | custom-call | tf_op jit(solution)/shard_map/pallas_call | solution.py:349
  3.6 8.8 %collective-permute-start = (f32[1088,128]{1,0:T(8,128)S(1)}, f32[1088,128]{1,0:T(8,128)S(1)}, u32[]{:S(2)}, u32[]{:S(2)}) collective-permute-start(f32[1088,128]{1,0:T(8,128)S(1)} %get-tuple-element.24), channel_id=1, source_target_pairs={{0,16},{16,0},{32,48},{48,32},{64,80},{80,64},{96,112},{112,96},{1... | collective-permute-start | bytes 1671176 | tf_op jit(solution)/shard_map/factors/ppermute | solution.py:284
  12.4 1.9 %collective-permute-start.2 = (f32[1088,128]{1,0:T(8,128)S(1)}, f32[1088,128]{1,0:T(8,128)S(1)}, u32[]{:S(2)}, u32[]{:S(2)}) collective-permute-start(f32[1088,128]{1,0:T(8,128)S(1)} %get-tuple-element.28), channel_id=1, source_target_pairs={{0,16},{16,0},{32,48},{48,32},{64,80},{80,64},{96,112},{112,96},{1... | collective-permute-start | bytes 1671176 | tf_op jit(solution)/shard_map/grad/ppermute | solution.py:284
  14.4 0.0 collective-permute-done.received
  14.4 0.1 shard_map.38
  14.5 5.7 %collective-permute-start.1 = (f32[544,128]{1,0:T(8,128)S(1)}, f32[544,128]{1,0:T(8,128)S(1)}, u32[]{:S(2)}, u32[]{:S(2)}) collective-permute-start(f32[544,128]{1,0:T(8,128)S(1)} %get-tuple-element.27), channel_id=1, source_target_pairs={{0,32},{16,496},{32,0},{48,80},{64,96},{80,48},{96,64},{112,144},{... | collective-permute-start | bytes 835592 | tf_op jit(solution)/shard_map/factors/ppermute | solution.py:284
  20.2 0.0 collective-permute-done.2.received
  20.2 0.1 shard_map.39
  20.3 1.9 %collective-permute-start.4 = (f32[544,128]{1,0:T(8,128)S(1)}, f32[544,128]{1,0:T(8,128)S(1)}, u32[]{:S(2)}, u32[]{:S(2)}) collective-permute-start(f32[544,128]{1,0:T(8,128)S(1)} %get-tuple-element.32), channel_id=1, source_target_pairs={{0,32},{16,496},{32,0},{48,80},{64,96},{80,48},{96,64},{112,144},{... | collective-permute-start | bytes 835592 | tf_op jit(solution)/shard_map/grad/ppermute | solution.py:284
  22.2 1.9 %collective-permute-done.1.received = f32[544,128]{1,0:T(8,128)S(1)} collective-permute-done((f32[544,128]{1,0:T(8,128)S(1)}, f32[544,128]{1,0:T(8,128)S(1)}, u32[]{:S(2)}, u32[]{:S(2)}) %collective-permute-start.1) | collective-permute-done | bytes 278560 | tf_op jit(solution)/shard_map/factors/ppermute | solution.py:284
  24.1 1.9 %collective-permute-start.3 = (f32[272,128]{1,0:T(8,128)S(1)}, f32[272,128]{1,0:T(8,128)S(1)}, u32[]{:S(2)}, u32[]{:S(2)}) collective-permute-start(f32[272,128]{1,0:T(8,128)S(1)} %get-tuple-element.31), channel_id=1, source_target_pairs={{0,480},{16,48},{32,64},{48,16},{64,32},{80,112},{96,128},{112,80}... | collective-permute-start | bytes 417800 | tf_op jit(solution)/shard_map/factors/ppermute | solution.py:284
  26.1 2.7 %collective-permute-done.4.received = f32[544,128]{1,0:T(8,128)S(1)} collective-permute-done((f32[544,128]{1,0:T(8,128)S(1)}, f32[544,128]{1,0:T(8,128)S(1)}, u32[]{:S(2)}, u32[]{:S(2)}) %collective-permute-start.4) | collective-permute-done | bytes 278560 | tf_op jit(solution)/shard_map/grad/ppermute | solution.py:284
  28.8 1.9 %collective-permute-start.6 = (f32[272,128]{1,0:T(8,128)S(1)}, f32[272,128]{1,0:T(8,128)S(1)}, u32[]{:S(2)}, u32[]{:S(2)}) collective-permute-start(f32[272,128]{1,0:T(8,128)S(1)} %get-tuple-element.36), channel_id=1, source_target_pairs={{0,480},{16,48},{32,64},{48,16},{64,32},{80,112},{96,128},{112,80}... | collective-permute-start | bytes 417800 | tf_op jit(solution)/shard_map/grad/ppermute | solution.py:284
  30.7 0.0 collective-permute-done.3.received
  30.8 5.5 %collective-permute-start.5 = (f32[136,128]{1,0:T(8,128)S(1)}, f32[136,128]{1,0:T(8,128)S(1)}, u32[]{:S(2)}, u32[]{:S(2)}) collective-permute-start(f32[136,128]{1,0:T(8,128)S(1)} %get-tuple-element.35), channel_id=1, source_target_pairs={{0,96},{16,432},{32,448},{48,144},{64,160},{80,496},{96,0},{112,20... | collective-permute-start | bytes 208904 | tf_op jit(solution)/shard_map/factors/ppermute | solution.py:284
  36.2 0.0 collective-permute-done.6.received
  36.3 2.8 %collective-permute-start.8 = (f32[136,128]{1,0:T(8,128)S(1)}, f32[136,128]{1,0:T(8,128)S(1)}, u32[]{:S(2)}, u32[]{:S(2)}) collective-permute-start(f32[136,128]{1,0:T(8,128)S(1)} %get-tuple-element.38), channel_id=1, source_target_pairs={{0,96},{16,432},{32,448},{48,144},{64,160},{80,496},{96,0},{112,20... | collective-permute-start | bytes 208904 | tf_op jit(solution)/shard_map/grad/ppermute | solution.py:284
  39.1 0.0 collective-permute-done.5.received
  39.1 4.9 %collective-permute-start.7 = (f32[136,128]{1,0:T(8,128)S(1)}, f32[136,128]{1,0:T(8,128)S(1)}, u32[]{:S(2)}, u32[]{:S(2)}) collective-permute-start(f32[136,128]{1,0:T(8,128)S(1)} %shard_map.44.after.own), channel_id=1, source_target_pairs={{0,352},{16,176},{32,192},{48,400},{64,416},{80,240},{96,256},{112... | collective-permute-start | bytes 208904 | tf_op jit(solution)/shard_map/factors/ppermute | solution.py:284
  44.1 0.2 collective-permute-done.8.received
  44.4 4.9 %collective-permute-start.10 = (f32[136,128]{1,0:T(8,128)S(1)}, f32[136,128]{1,0:T(8,128)S(1)}, u32[]{:S(2)}, u32[]{:S(2)}) collective-permute-start(f32[136,128]{1,0:T(8,128)S(1)} %shard_map.45.after.own), channel_id=1, source_target_pairs={{0,352},{16,176},{32,192},{48,400},{64,416},{80,240},{96,256},{112... | collective-permute-start | bytes 208904 | tf_op jit(solution)/shard_map/grad/ppermute | solution.py:284
  49.3 0.4 collective-permute-done.7.received
  49.7 7.2 %collective-permute-start.9 = (f32[136,128]{1,0:T(8,128)S(1)}, f32[136,128]{1,0:T(8,128)S(1)}, u32[]{:S(2)}, u32[]{:S(2)}) collective-permute-start(f32[136,128]{1,0:T(8,128)S(1)} %shard_map.46.after.near), channel_id=1, source_target_pairs={{0,96},{16,432},{32,448},{48,144},{64,160},{80,496},{96,0},{112,20... | collective-permute-start | bytes 208904 | tf_op jit(solution)/shard_map/factors/ppermute | solution.py:284
  56.9 0.0 collective-permute-done.10.received
  56.9 4.7 %collective-permute-start.12 = (f32[136,128]{1,0:T(8,128)S(1)}, f32[136,128]{1,0:T(8,128)S(1)}, u32[]{:S(2)}, u32[]{:S(2)}) collective-permute-start(f32[136,128]{1,0:T(8,128)S(1)} %shard_map.47.after.near), channel_id=1, source_target_pairs={{0,96},{16,432},{32,448},{48,144},{64,160},{80,496},{96,0},{112,20... | collective-permute-start | bytes 208904 | tf_op jit(solution)/shard_map/grad/ppermute | solution.py:284
  61.7 0.0 collective-permute-done.9.far
  61.7 1.9 %collective-permute-start.11 = (f32[272,128]{1,0:T(8,128)S(1)}, f32[272,128]{1,0:T(8,128)S(1)}, u32[]{:S(2)}, u32[]{:S(2)}) collective-permute-start(f32[272,128]{1,0:T(8,128)S(1)} %shard_map.48.after.near), channel_id=1, source_target_pairs={{0,480},{16,48},{32,64},{48,16},{64,32},{80,112},{96,128},{112,80}... | collective-permute-start | bytes 417800 | tf_op jit(solution)/shard_map/factors/ppermute | solution.py:284
  63.6 2.1 %collective-permute-done.12.far = f32[136,128]{1,0:T(8,128)S(1)} collective-permute-done((f32[136,128]{1,0:T(8,128)S(1)}, f32[136,128]{1,0:T(8,128)S(1)}, u32[]{:S(2)}, u32[]{:S(2)}) %collective-permute-start.12) | collective-permute-done | bytes 69664 | tf_op jit(solution)/shard_map/grad/ppermute | solution.py:284
  65.7 1.9 %collective-permute-start.14 = (f32[272,128]{1,0:T(8,128)S(1)}, f32[272,128]{1,0:T(8,128)S(1)}, u32[]{:S(2)}, u32[]{:S(2)}) collective-permute-start(f32[272,128]{1,0:T(8,128)S(1)} %shard_map.49.after.near), channel_id=1, source_target_pairs={{0,480},{16,48},{32,64},{48,16},{64,32},{80,112},{96,128},{112,80}... | collective-permute-start | bytes 417800 | tf_op jit(solution)/shard_map/grad/ppermute | solution.py:284
  67.7 0.0 collective-permute-done.11.far
  67.7 3.7 %collective-permute-start.13 = (f32[544,128]{1,0:T(8,128)S(1)}, f32[544,128]{1,0:T(8,128)S(1)}, u32[]{:S(2)}, u32[]{:S(2)}) collective-permute-start(f32[544,128]{1,0:T(8,128)S(1)} %shard_map.50.after.near), channel_id=1, source_target_pairs={{0,32},{16,496},{32,0},{48,80},{64,96},{80,48},{96,64},{112,144},{... | collective-permute-start | bytes 835592 | tf_op jit(solution)/shard_map/factors/ppermute | solution.py:284
  71.4 0.5 collective-permute-done.14.far
  71.9 2.3 %collective-permute-start.15 = (f32[544,128]{1,0:T(8,128)S(1)}, f32[544,128]{1,0:T(8,128)S(1)}, u32[]{:S(2)}, u32[]{:S(2)}) collective-permute-start(f32[544,128]{1,0:T(8,128)S(1)} %shard_map.51.after.near), channel_id=1, source_target_pairs={{0,32},{16,496},{32,0},{48,80},{64,96},{80,48},{96,64},{112,144},{... | collective-permute-start | bytes 835592 | tf_op jit(solution)/shard_map/grad/ppermute | solution.py:284
  74.3 2.0 %collective-permute-done.13.far = f32[544,128]{1,0:T(8,128)S(1)} collective-permute-done((f32[544,128]{1,0:T(8,128)S(1)}, f32[544,128]{1,0:T(8,128)S(1)}, u32[]{:S(2)}, u32[]{:S(2)}) %collective-permute-start.13) | collective-permute-done | bytes 278560 | tf_op jit(solution)/shard_map/factors/ppermute | solution.py:284
  76.2 3.5 %shard_map.52.x = f32[512,512]{1,0:T(8,128)S(1)} custom-call(f32[544,128]{1,0:T(8,128)S(1)} %shard_map.50.after.near, f32[544,128]{1,0:T(8,128)S(1)} %collective-permute-done.13.far, f32[544,128]{1,0:T(8,128)S(1)} %shard_map.51.after.near), custom_call_target="tpu_custom_call" | custom-call | bytes 1 | tf_op jit(solution)/shard_map/pallas_call | solution.py:272
  79.7 7.9 %collective-permute-start.17 = (f32[512,512]{1,0:T(8,128)S(1)}, f32[512,512]{1,0:T(8,128)S(1)}, u32[]{:S(2)}, u32[]{:S(2)}) collective-permute-start(f32[512,512]{1,0:T(8,128)S(1)} %shard_map.52.x), channel_id=1, source_target_pairs={{0,16},{16,0},{32,48},{48,32},{64,80},{80,64},{96,112},{112,96},{1... | collective-permute-start | bytes 3145736 | tf_op jit(solution)/shard_map/root/ppermute | solution.py:284
  87.6 0.0 collective-permute-done.15.far
  87.7 0.0 copy-start
  87.7 2.7 %collective-permute-start.16 = (f32[1088,128]{1,0:T(8,128)S(1)}, f32[1088,128]{1,0:T(8,128)S(1)}, u32[]{:S(2)}, u32[]{:S(2)}) collective-permute-start(f32[1088,128]{1,0:T(8,128)S(1)} %shard_map.53.own), channel_id=1, source_target_pairs={{0,16},{16,0},{32,48},{48,32},{64,80},{80,64},{96,112},{112,96},{1... | collective-permute-start | bytes 1671176 | tf_op jit(solution)/shard_map/grad/ppermute | solution.py:284
  90.4 1.6 %collective-permute-done.16.other = f32[1088,128]{1,0:T(8,128)S(1)} collective-permute-done((f32[1088,128]{1,0:T(8,128)S(1)}, f32[1088,128]{1,0:T(8,128)S(1)}, u32[]{:S(2)}, u32[]{:S(2)}) %collective-permute-start.16) | collective-permute-done | bytes 557088 | tf_op jit(solution)/shard_map/grad/ppermute | solution.py:284
  92.0 1.0 shard_map.54
  93.0 0.0 collective-permute-done.17.x
  93.0 0.0 copy-done
  93.0 2.0 %shard_map.55 = f32[16,8,128]{2,1,0:T(8,128)S(1)} custom-call(s32[32]{0:T(128)S(1)} %copy-done, bf16[512,512]{1,0:T(8,128)(2,1)S(1)} %get-tuple-element.39.high, bf16[512,512]{1,0:T(8,128)(2,1)S(1)} %get-tuple-element.40.low, f32[512,512]{1,0:T(8,128)S(1)} %collective-permute-done.17.x), custom_call_target="tpu_custom_call" | custom-call | tf_op jit(solution)/shard_map/pallas_call | solution.py:272
  95.1 13.2 %all_to_all.5.tiles = f32[16,8,128]{2,1,0:T(8,128)S(1)} all-to-all(f32[16,8,128]{2,1,0:T(8,128)S(1)} %shard_map.55), channel_id=1, replica_groups=mesh['dp'=32,'mp'=16] {'mp'}, dimensions={0} | all-to-all | bytes 131072 | tf_op jit(solution)/shard_map/all_to_all | solution.py:368
  108.3 0.7 shard_map.56
  (13 shorter events, 0.2 us)
Async XLA Ops:
  3.6 10.7 %collective-permute-start = (f32[1088,128]{1,0:T(8,128)S(1)}, f32[1088,128]{1,0:T(8,128)S(1)}, u32[]{:S(2)}, u32[]{:S(2)}) collective-permute-start(f32[1088,128]{1,0:T(8,128)S(1)} %get-tuple-element.24), channel_id=1, source_target_pairs={{0,16},{16,0},{32,48},{48,32},{64,80},{80,64},{96,112},{112,96},{1... | collective-permute-start | bytes 1671176 | tf_op jit(solution)/shard_map/factors/ppermute | solution.py:284
  12.4 7.8 %collective-permute-start.2 = (f32[1088,128]{1,0:T(8,128)S(1)}, f32[1088,128]{1,0:T(8,128)S(1)}, u32[]{:S(2)}, u32[]{:S(2)}) collective-permute-start(f32[1088,128]{1,0:T(8,128)S(1)} %get-tuple-element.28), channel_id=1, source_target_pairs={{0,16},{16,0},{32,48},{48,32},{64,80},{80,64},{96,112},{112,96},{1... | collective-permute-start | bytes 1671176 | tf_op jit(solution)/shard_map/grad/ppermute | solution.py:284
  14.5 9.7 %collective-permute-start.1 = (f32[544,128]{1,0:T(8,128)S(1)}, f32[544,128]{1,0:T(8,128)S(1)}, u32[]{:S(2)}, u32[]{:S(2)}) collective-permute-start(f32[544,128]{1,0:T(8,128)S(1)} %get-tuple-element.27), channel_id=1, source_target_pairs={{0,32},{16,496},{32,0},{48,80},{64,96},{80,48},{96,64},{112,144},{... | collective-permute-start | bytes 835592 | tf_op jit(solution)/shard_map/factors/ppermute | solution.py:284
  20.3 8.5 %collective-permute-start.4 = (f32[544,128]{1,0:T(8,128)S(1)}, f32[544,128]{1,0:T(8,128)S(1)}, u32[]{:S(2)}, u32[]{:S(2)}) collective-permute-start(f32[544,128]{1,0:T(8,128)S(1)} %get-tuple-element.32), channel_id=1, source_target_pairs={{0,32},{16,496},{32,0},{48,80},{64,96},{80,48},{96,64},{112,144},{... | collective-permute-start | bytes 835592 | tf_op jit(solution)/shard_map/grad/ppermute | solution.py:284
  24.1 6.6 %collective-permute-start.3 = (f32[272,128]{1,0:T(8,128)S(1)}, f32[272,128]{1,0:T(8,128)S(1)}, u32[]{:S(2)}, u32[]{:S(2)}) collective-permute-start(f32[272,128]{1,0:T(8,128)S(1)} %get-tuple-element.31), channel_id=1, source_target_pairs={{0,480},{16,48},{32,64},{48,16},{64,32},{80,112},{96,128},{112,80}... | collective-permute-start | bytes 417800 | tf_op jit(solution)/shard_map/factors/ppermute | solution.py:284
  28.8 7.4 %collective-permute-start.6 = (f32[272,128]{1,0:T(8,128)S(1)}, f32[272,128]{1,0:T(8,128)S(1)}, u32[]{:S(2)}, u32[]{:S(2)}) collective-permute-start(f32[272,128]{1,0:T(8,128)S(1)} %get-tuple-element.36), channel_id=1, source_target_pairs={{0,480},{16,48},{32,64},{48,16},{64,32},{80,112},{96,128},{112,80}... | collective-permute-start | bytes 417800 | tf_op jit(solution)/shard_map/grad/ppermute | solution.py:284
  30.8 8.3 %collective-permute-start.5 = (f32[136,128]{1,0:T(8,128)S(1)}, f32[136,128]{1,0:T(8,128)S(1)}, u32[]{:S(2)}, u32[]{:S(2)}) collective-permute-start(f32[136,128]{1,0:T(8,128)S(1)} %get-tuple-element.35), channel_id=1, source_target_pairs={{0,96},{16,432},{32,448},{48,144},{64,160},{80,496},{96,0},{112,20... | collective-permute-start | bytes 208904 | tf_op jit(solution)/shard_map/factors/ppermute | solution.py:284
  36.3 8.1 %collective-permute-start.8 = (f32[136,128]{1,0:T(8,128)S(1)}, f32[136,128]{1,0:T(8,128)S(1)}, u32[]{:S(2)}, u32[]{:S(2)}) collective-permute-start(f32[136,128]{1,0:T(8,128)S(1)} %get-tuple-element.38), channel_id=1, source_target_pairs={{0,96},{16,432},{32,448},{48,144},{64,160},{80,496},{96,0},{112,20... | collective-permute-start | bytes 208904 | tf_op jit(solution)/shard_map/grad/ppermute | solution.py:284
  39.1 10.5 %collective-permute-start.7 = (f32[136,128]{1,0:T(8,128)S(1)}, f32[136,128]{1,0:T(8,128)S(1)}, u32[]{:S(2)}, u32[]{:S(2)}) collective-permute-start(f32[136,128]{1,0:T(8,128)S(1)} %shard_map.44.after.own), channel_id=1, source_target_pairs={{0,352},{16,176},{32,192},{48,400},{64,416},{80,240},{96,256},{112... | collective-permute-start | bytes 208904 | tf_op jit(solution)/shard_map/factors/ppermute | solution.py:284
  44.4 12.5 %collective-permute-start.10 = (f32[136,128]{1,0:T(8,128)S(1)}, f32[136,128]{1,0:T(8,128)S(1)}, u32[]{:S(2)}, u32[]{:S(2)}) collective-permute-start(f32[136,128]{1,0:T(8,128)S(1)} %shard_map.45.after.own), channel_id=1, source_target_pairs={{0,352},{16,176},{32,192},{48,400},{64,416},{80,240},{96,256},{112... | collective-permute-start | bytes 208904 | tf_op jit(solution)/shard_map/grad/ppermute | solution.py:284
  49.7 12.0 %collective-permute-start.9 = (f32[136,128]{1,0:T(8,128)S(1)}, f32[136,128]{1,0:T(8,128)S(1)}, u32[]{:S(2)}, u32[]{:S(2)}) collective-permute-start(f32[136,128]{1,0:T(8,128)S(1)} %shard_map.46.after.near), channel_id=1, source_target_pairs={{0,96},{16,432},{32,448},{48,144},{64,160},{80,496},{96,0},{112,20... | collective-permute-start | bytes 208904 | tf_op jit(solution)/shard_map/factors/ppermute | solution.py:284
  56.9 8.8 %collective-permute-start.12 = (f32[136,128]{1,0:T(8,128)S(1)}, f32[136,128]{1,0:T(8,128)S(1)}, u32[]{:S(2)}, u32[]{:S(2)}) collective-permute-start(f32[136,128]{1,0:T(8,128)S(1)} %shard_map.47.after.near), channel_id=1, source_target_pairs={{0,96},{16,432},{32,448},{48,144},{64,160},{80,496},{96,0},{112,20... | collective-permute-start | bytes 208904 | tf_op jit(solution)/shard_map/grad/ppermute | solution.py:284
  61.7 6.0 %collective-permute-start.11 = (f32[272,128]{1,0:T(8,128)S(1)}, f32[272,128]{1,0:T(8,128)S(1)}, u32[]{:S(2)}, u32[]{:S(2)}) collective-permute-start(f32[272,128]{1,0:T(8,128)S(1)} %shard_map.48.after.near), channel_id=1, source_target_pairs={{0,480},{16,48},{32,64},{48,16},{64,32},{80,112},{96,128},{112,80}... | collective-permute-start | bytes 417800 | tf_op jit(solution)/shard_map/factors/ppermute | solution.py:284
  65.7 6.1 %collective-permute-start.14 = (f32[272,128]{1,0:T(8,128)S(1)}, f32[272,128]{1,0:T(8,128)S(1)}, u32[]{:S(2)}, u32[]{:S(2)}) collective-permute-start(f32[272,128]{1,0:T(8,128)S(1)} %shard_map.49.after.near), channel_id=1, source_target_pairs={{0,480},{16,48},{32,64},{48,16},{64,32},{80,112},{96,128},{112,80}... | collective-permute-start | bytes 417800 | tf_op jit(solution)/shard_map/grad/ppermute | solution.py:284
  67.7 8.5 %collective-permute-start.13 = (f32[544,128]{1,0:T(8,128)S(1)}, f32[544,128]{1,0:T(8,128)S(1)}, u32[]{:S(2)}, u32[]{:S(2)}) collective-permute-start(f32[544,128]{1,0:T(8,128)S(1)} %shard_map.50.after.near), channel_id=1, source_target_pairs={{0,32},{16,496},{32,0},{48,80},{64,96},{80,48},{96,64},{112,144},{... | collective-permute-start | bytes 835592 | tf_op jit(solution)/shard_map/factors/ppermute | solution.py:284
  71.9 15.7 %collective-permute-start.15 = (f32[544,128]{1,0:T(8,128)S(1)}, f32[544,128]{1,0:T(8,128)S(1)}, u32[]{:S(2)}, u32[]{:S(2)}) collective-permute-start(f32[544,128]{1,0:T(8,128)S(1)} %shard_map.51.after.near), channel_id=1, source_target_pairs={{0,32},{16,496},{32,0},{48,80},{64,96},{80,48},{96,64},{112,144},{... | collective-permute-start | bytes 835592 | tf_op jit(solution)/shard_map/grad/ppermute | solution.py:284
  79.7 13.3 %collective-permute-start.17 = (f32[512,512]{1,0:T(8,128)S(1)}, f32[512,512]{1,0:T(8,128)S(1)}, u32[]{:S(2)}, u32[]{:S(2)}) collective-permute-start(f32[512,512]{1,0:T(8,128)S(1)} %shard_map.52.x), channel_id=1, source_target_pairs={{0,16},{16,0},{32,48},{48,32},{64,80},{80,64},{96,112},{112,96},{1... | collective-permute-start | bytes 3145736 | tf_op jit(solution)/shard_map/root/ppermute | solution.py:284
  87.7 5.3 %copy-start = (s32[32]{0:T(128)S(1)}, s32[32]{0:T(128)}, u32[]{:S(2)}) copy-start(s32[32]{0:T(128)} %owner.1) | copy-start | bytes 388
  87.7 4.3 %collective-permute-start.16 = (f32[1088,128]{1,0:T(8,128)S(1)}, f32[1088,128]{1,0:T(8,128)S(1)}, u32[]{:S(2)}, u32[]{:S(2)}) collective-permute-start(f32[1088,128]{1,0:T(8,128)S(1)} %shard_map.53.own), channel_id=1, source_target_pairs={{0,16},{16,0},{32,48},{48,32},{64,80},{80,64},{96,112},{112,96},{1... | collective-permute-start | bytes 1671176 | tf_op jit(solution)/shard_map/grad/ppermute | solution.py:284

commit v4 on v3

--- a/solution.py
+++ b/solution.py
@@ -12,12 +12,11 @@
 B = 128
 ROWS = 136
 OFF = ((0, 1), (0, 2), (0, 3), (1, 2), (1, 3), (2, 3))
-F_FINE = True
-G_FINE = True
 JOIN_FLOPS = 4_000_000_000
 ADD_FLOPS = 0
 ROOT_FLOPS = 0
 
+BEGIN_FLOPS = 0
 MIX_FLOPS = 5_000_000_000
 TOKENS = 512
 FRONT_LIMIT = 51 * 1024 * 1024
@@ -49,43 +48,44 @@
     return holders(v, partners[:-1]) + holders(partners[-1](v), partners[:-1])
 
 
-def local_order(v, fine):
-    order = [EIGHTH[u] for u in holders(v, (partner3, partner2, partner1) if fine else (partner2, partner1))]
-    if not fine:
-        order = [e for own in order for e in (own & 6, own | 1)]
+def order_code(v):
+    order = [EIGHTH[u] for u in holders(v, (partner3, partner2, partner1))]
     assert sorted(order) == list(range(8))
-    return order
-
-
-def position(z, core):
-    return z if core == 0 else (-z) % Z
-
-
-def order_code(v, fine):
-    order = local_order(v, fine)
     return sum(order.index(e) << (3 * e) for e in range(8))
 
 
-def places(own, fine):
+def position(z, side):
+    return -z % Z if side else z
+
+
+def role():
     dp = lax.axis_index("dp")
-    z, core = dp // 2, dp % 2
-    v = jnp.where((core == 0) == own, z, (Z - z) % Z)
-    code = jnp.int32(order_code(0, fine))
+    return (dp // 2 + dp) % 2
+
+
+def places(own):
+    z = lax.axis_index("dp") // 2
+    v = jnp.where((role() == 0) == own, z, (Z - z) % Z)
+    code = jnp.int32(order_code(0))
     for u in range(1, Z):
-        code = jnp.where(v == u, order_code(u, fine), code)
+        code = jnp.where(v == u, order_code(u), code)
     return [(code >> (3 * e)) & 7 for e in range(8)]
+
+
+def device(z, side):
+    return 2 * z + (z + side) % 2
 
 
 def ring_pairs(partner):
     pairs = []
     for z in range(Z):
-        for core in range(2):
-            pairs.append((2 * z + core, 2 * position(partner(position(z, core)), core) + core))
+        for side in range(2):
+            pairs.append((device(z, side), device(position(partner(position(z, side)), side), side)))
     return pairs
 
 
 CORE_PAIRS = [(i, i ^ 1) for i in range(2 * Z)]
-PAIRS = [ring_pairs(p) for p in (partner1, partner2, partner3, partner4)]
+PAIRS = [CORE_PAIRS] + [ring_pairs(p) for p in (partner1, partner2, partner3, partner4)]
 
 
 def split(x):
@@ -166,9 +166,8 @@
         for copy in pair:
             copy.start()
         copies.append(pair)
-    f_place, f_other = places(True, F_FINE), places(False, F_FINE)
-    g_place, g_other = places(True, G_FINE), places(False, G_FINE)
-    core = lax.axis_index("dp") % 2
+    place, other = places(True), places(False)
+    mine = role()
     for i, pair in enumerate(copies):
         for copy in pair:
             copy.wait()
@@ -179,25 +178,25 @@
     left[...] = dot(low, low, ((1,), (1,)))
     right[...] = dot(low, low, ((0,), (0,)))
 
-    @pl.when(core == 0)
-    def _():
-        put_factor(left, f_own, f_place)
-        put_factor(right, f_send, f_other)
-        put_gradient(grad, g_own, 0, g_place)
-        put_gradient(grad, g_send, 1, g_other)
-
-    @pl.when(core == 1)
-    def _():
-        put_factor(right, f_own, f_place)
-        put_factor(left, f_send, f_other)
-        put_gradient(grad, g_own, 1, g_place)
-        put_gradient(grad, g_send, 0, g_other)
+    @pl.when(mine == 0)
+    def _():
+        put_factor(left, f_own, place)
+        put_factor(right, f_send, other)
+        put_gradient(grad, g_own, 0, place)
+        put_gradient(grad, g_send, 1, other)
+
+    @pl.when(mine == 1)
+    def _():
+        put_factor(right, f_own, place)
+        put_factor(left, f_send, other)
+        put_gradient(grad, g_own, 1, place)
+        put_gradient(grad, g_send, 0, other)
 
 
 def root(near, far, after, out, packed, factor):
     packed[: 4 * ROWS, :] = near[...]
     packed[4 * ROWS :, :] = far[...]
-    take_factor(packed, factor, places(True, F_FINE))
+    take_factor(packed, factor, places(True))
     f = factor[...]
     norm = jnp.sqrt(jnp.sum(f * f, keepdims=True) + 1e-06)
     m1 = f / norm
@@ -214,44 +213,55 @@
     out[...] = x * lax.rsqrt(jnp.sqrt(norm))
 
 
-def mix(x, own, other, high, low, grad):
-    core = lax.axis_index("dp") % 2
-
-    def take(src, half, place):
-        for e in range(8):
-            r, c = half * 256 + (e // 4) * B, (e % 4) * B
-            grad[r : r + B, c : c + B] = src[rows_of(place[e], B), :]
-
-    def put(value):
-        high[...], low[...] = split(value)
-
-    @pl.when(core == 0)
-    def _():
-        take(own, 0, places(True, G_FINE))
-        take(other, 1, places(False, G_FINE))
-        put(product(split(x[...]), split(grad[...])))
-
-    @pl.when(core == 1)
-    def _():
-        take(own, 1, places(True, G_FINE))
-        take(other, 0, places(False, G_FINE))
-        put(product(split(grad[...]), split(x[...])))
+def take_gradient(src, half, place):
+    for e in range(8):
+        r, c = (e // 4) * B, (e % 4) * B
+        half[r : r + B, c : c + B] = src[rows_of(place[e], B), :]
+    return split(half[...])
+
+
+def begin(x, own, out, half):
+    mine = role()
+    rows = take_gradient(own, half, places(True))
+
+    @pl.when(mine == 0)
+    def _():
+        out[...] = product(split(x[:, : W // 2]), rows)
+
+    @pl.when(mine == 1)
+    def _():
+        out[W // 2 :, :] = product(rows, split(x[...]))
+        out[: W // 2, :] = jnp.zeros((W // 2, W), jnp.float32)
+
+
+def mix(x, begun, other, high, low, half):
+    mine = role()
+    rows = take_gradient(other, half, places(False))
+
+    @pl.when(mine == 0)
+    def _():
+        high[...], low[...] = split(begun[...] + product(split(x[:, W // 2 :]), rows))
+
+    @pl.when(mine == 1)
+    def _():
+        high[: W // 2, :], low[: W // 2, :] = split(product(rows, split(x[...])))
+        high[W // 2 :, :], low[W // 2 :, :] = split(begun[W // 2 :, :])
 
 
 def finish(owner, high, low, x, out, precond):
-    dp = lax.axis_index("dp")
-
-    @pl.when(dp % 2 == 0)
+    mine = role()
+
+    @pl.when(mine == 0)
     def _():
         precond[...] = product((high[...], low[...]), split(x[...]))
 
-    @pl.when(dp % 2 == 1)
+    @pl.when(mine == 1)
     def _():
         precond[...] = product(split(x[...]), (high[...], low[...]))
 
     value = precond[...]
     scale = jnp.sqrt(jnp.sum(value * value, keepdims=True) / (W * W) + 1e-06)
-    panel = precond[pl.ds(pl.multiple_of(owner[dp] * 16, 16), 16), :] / scale
+    panel = precond[pl.ds(pl.multiple_of(owner[lax.axis_index("dp")] * 16, 16), 16), :] / scale
     lane = lax.broadcasted_iota(jnp.int32, (8, B), 1)
     for m in range(16):
         tile = panel[:, (m // 4) * B : (m // 4 + 1) * B]
@@ -281,7 +291,7 @@
 
 
 def move(x, step):
-    return lax.ppermute(x, "dp", CORE_PAIRS if step == 0 else PAIRS[step - 1])
+    return lax.ppermute(x, "dp", PAIRS[step])
 
 
 def halve(own, received, after):
@@ -311,13 +321,10 @@
     return call(kernel, [(2 * half, B)], [], near, far, [after], cost=JOIN_FLOPS)[0]
 
 
-FINE = ((halve, 1), (halve, 2), (halve, 3), (add, 4), (add, 3), (join, 2), (join, 1))
-COARSE = ((halve, 1), (halve, 2), (add, 3), (add, 4), (add, 2), (join, 1))
-WAYS = {True: FINE, False: COARSE}
+WAY = ((halve, 1), (halve, 2), (halve, 3), (add, 4), (add, 3), (join, 2), (join, 1))
 
 
 def totals(first, second):
-    (a, a_send), (b, b_send) = first, second
     def move_a(x, step):
         with jax.named_scope("factors"):
             return move(x, step)
@@ -326,21 +333,18 @@
         with jax.named_scope("grad"):
             return move(x, step)
 
-    def advance(own, received, after, way, move):
-        combine, step = way
+    def advance(own, received, after, combine, step, move):
         if combine is halve:
             own, give = halve(own, received, after)
             return own, move(give, step)
         own = combine(own, received, after)
         return own, move(own, step)
 
+    (a, a_send), (b, b_send) = first, second
     a_in, b_in = move_a(a_send, 0), move_b(b_send, 0)
-    a_way, b_way = WAYS[F_FINE], WAYS[G_FINE]
-    for i in range(max(len(a_way), len(b_way))):
-        if i < len(a_way):
-            a, a_in = advance(a, a_in, b, a_way[i], move_a)
-        if i < len(b_way):
-            b, b_in = advance(b, b_in, a, b_way[i], move_b)
+    for combine, step in WAY:
+        a, a_in = advance(a, a_in, b, combine, step, move_a)
+        b, b_in = advance(b, b_in, a, combine, step, move_b)
     return (a, a_in), (b, b_in)
 
 
@@ -363,7 +367,8 @@
     (x_own,) = call(root, [(W, W)], [whole, (W, W)], f_near, f_far, [g_near], cost=ROOT_FLOPS)
     with jax.named_scope("root"):
         x_other = move(x_own, 0)
-    high, low = call(mix, [(W, W)] * 2, [(W, W)], x_own, g_sum, g_other, cost=MIX_FLOPS, dtype=jnp.bfloat16)
+    (begun,) = call(begin, [(W, W)], [(W // 2, W)], x_own, g_sum, cost=BEGIN_FLOPS)
+    high, low = call(mix, [(W, W)] * 2, [(W // 2, W)], x_own, begun, g_other, cost=MIX_FLOPS, dtype=jnp.bfloat16)
     (tiles,) = call(finish, [(16, 8, B)], [(W, W)], (panel_owner,), high, low, x_other)
     tiles = lax.all_to_all(tiles, "mp", split_axis=0, concat_axis=0, tiled=True)
     return call(unfold, [(16, 16, 32)], [], tiles)[0]

time: 110 us -> 108 us (0.982)
  starting transfers between devices: 72.7 us -> 70.1 us
    ppermute x18, starting transfers between devices: 72.7 us -> 70.1 us  [move(): return lax.ppermute(x, 'dp', PAIRS[step])]
    pallas_call x19 -> x20, Pallas kernels: 7.71 us -> 8.21 us  [call(): pl.pallas_call(kernel, out_shape=[jax.ShapeDtypeStruct(s, dtype) for s in...]
  transfers between devices with their start and end apart: 18 -> 18, of which waited for: 8 -> 9; matrix products, arithmetic and copies ran while one was open for 0% -> 0% of each run, Pallas kernels for 5% -> 5%
where the time goes in v4:
time: 108 us; the launch traced here: 107 us
  starting transfers between devices  70.1 us (65%)
  blocking collectives  13.1 us (12%)
  Pallas kernels  11.9 us (11%)
  waiting for transfers between devices  11.6 us (11%)
    ppermute x18, starting transfers between devices, move(): return lax.ppermute(x, 'dp', PAIRS[step])  70.1 us
    all_to_all x1, blocking collectives, per_device(): tiles = lax.all_to_all(tiles, 'mp', split_axis=0, concat_axis=0, tiled=True)  13.1 us
    ppermute x18, waiting for transfers between devices, move(): return lax.ppermute(x, 'dp', PAIRS[step])  11.6 us
    pallas_call x20, Pallas kernels, call(): pl.pallas_call(kernel, out_shape=[jax.ShapeDtypeStruct(s, dtype) for s in...  8.21 us
    pallas_call x1, Pallas kernels, per_device(): pl.pallas_call(front, out_shape=[jax.ShapeDtypeStruct(whole, jnp.float32)...  3.64 us
  transfers between devices with their start and end apart: 18, of which 9 were waited for; matrix products, arithmetic and copies ran while one was open for 0% of the time, Pallas kernels for 5%

profile of v4, /device:TPU:1, one launch (start us, length us, event | category | flops | bytes accessed | tf_op | source)
XLA Modules:
  0.0 107.0 jit_solution(15269667473019700801)
XLA Ops:
  0.0 3.6 %shard_map.37 = (f32[1088,128]{1,0:T(8,128)S(1)}, f32[1088,128]{1,0:T(8,128)S(1)}, f32[1088,128]{1,0:T(8,128)S(1)}, f32[1088,128]{1,0:T(8,128)S(1)}) custom-call(bf16[2048,512]{1,0:T(8,128)(2,1)} %acts.1, bf16[2048,512]{1,0:T(8,128)(2,1)} %grads_out.1), custom_call_target="tpu_custom_call" | custom-call | tf_op jit(solution)/shard_map/pallas_call | solution.py:353
  3.6 8.8 %collective-permute-start = (f32[1088,128]{1,0:T(8,128)S(1)}, f32[1088,128]{1,0:T(8,128)S(1)}, u32[]{:S(2)}, u32[]{:S(2)}) collective-permute-start(f32[1088,128]{1,0:T(8,128)S(1)} %get-tuple-element.24), channel_id=1, source_target_pairs={{0,16},{16,0},{32,48},{48,32},{64,80},{80,64},{96,112},{112,96},{1... | collective-permute-start | bytes 1671176 | tf_op jit(solution)/shard_map/factors/ppermute | solution.py:294
  12.4 1.9 %collective-permute-start.2 = (f32[1088,128]{1,0:T(8,128)S(1)}, f32[1088,128]{1,0:T(8,128)S(1)}, u32[]{:S(2)}, u32[]{:S(2)}) collective-permute-start(f32[1088,128]{1,0:T(8,128)S(1)} %get-tuple-element.28), channel_id=1, source_target_pairs={{0,16},{16,0},{32,48},{48,32},{64,80},{80,64},{96,112},{112,96},{1... | collective-permute-start | bytes 1671176 | tf_op jit(solution)/shard_map/grad/ppermute | solution.py:294
  14.4 0.0 collective-permute-done.received
  14.4 0.1 shard_map.38
  14.5 6.1 %collective-permute-start.1 = (f32[544,128]{1,0:T(8,128)S(1)}, f32[544,128]{1,0:T(8,128)S(1)}, u32[]{:S(2)}, u32[]{:S(2)}) collective-permute-start(f32[544,128]{1,0:T(8,128)S(1)} %get-tuple-element.27), channel_id=1, source_target_pairs={{0,48},{16,480},{48,0},{32,80},{64,112},{80,32},{112,64},{96,144},... | collective-permute-start | bytes 835592 | tf_op jit(solution)/shard_map/factors/ppermute | solution.py:294
  20.6 0.0 collective-permute-done.2.received
  20.6 0.1 shard_map.39
  20.7 1.9 %collective-permute-start.4 = (f32[544,128]{1,0:T(8,128)S(1)}, f32[544,128]{1,0:T(8,128)S(1)}, u32[]{:S(2)}, u32[]{:S(2)}) collective-permute-start(f32[544,128]{1,0:T(8,128)S(1)} %get-tuple-element.32), channel_id=1, source_target_pairs={{0,48},{16,480},{48,0},{32,80},{64,112},{80,32},{112,64},{96,144},... | collective-permute-start | bytes 835592 | tf_op jit(solution)/shard_map/grad/ppermute | solution.py:294
  22.6 2.2 %collective-permute-done.1.received = f32[544,128]{1,0:T(8,128)S(1)} collective-permute-done((f32[544,128]{1,0:T(8,128)S(1)}, f32[544,128]{1,0:T(8,128)S(1)}, u32[]{:S(2)}, u32[]{:S(2)}) %collective-permute-start.1) | collective-permute-done | bytes 278560 | tf_op jit(solution)/shard_map/factors/ppermute | solution.py:294
  24.8 1.9 %collective-permute-start.3 = (f32[272,128]{1,0:T(8,128)S(1)}, f32[272,128]{1,0:T(8,128)S(1)}, u32[]{:S(2)}, u32[]{:S(2)}) collective-permute-start(f32[272,128]{1,0:T(8,128)S(1)} %get-tuple-element.31), channel_id=1, source_target_pairs={{0,496},{16,32},{48,64},{32,16},{64,48},{80,96},{112,128},{96,80},... | collective-permute-start | bytes 417800 | tf_op jit(solution)/shard_map/factors/ppermute | solution.py:294
  26.8 3.6 %collective-permute-done.4.received = f32[544,128]{1,0:T(8,128)S(1)} collective-permute-done((f32[544,128]{1,0:T(8,128)S(1)}, f32[544,128]{1,0:T(8,128)S(1)}, u32[]{:S(2)}, u32[]{:S(2)}) %collective-permute-start.4) | collective-permute-done | bytes 278560 | tf_op jit(solution)/shard_map/grad/ppermute | solution.py:294
  30.4 1.9 %collective-permute-start.6 = (f32[272,128]{1,0:T(8,128)S(1)}, f32[272,128]{1,0:T(8,128)S(1)}, u32[]{:S(2)}, u32[]{:S(2)}) collective-permute-start(f32[272,128]{1,0:T(8,128)S(1)} %get-tuple-element.36), channel_id=1, source_target_pairs={{0,496},{16,32},{48,64},{32,16},{64,48},{80,96},{112,128},{96,80},... | collective-permute-start | bytes 417800 | tf_op jit(solution)/shard_map/grad/ppermute | solution.py:294
  32.3 0.0 collective-permute-done.3.received
  32.4 5.1 %collective-permute-start.5 = (f32[136,128]{1,0:T(8,128)S(1)}, f32[136,128]{1,0:T(8,128)S(1)}, u32[]{:S(2)}, u32[]{:S(2)}) collective-permute-start(f32[136,128]{1,0:T(8,128)S(1)} %get-tuple-element.35), channel_id=1, source_target_pairs={{0,112},{16,416},{48,448},{32,144},{64,176},{80,480},{112,0},{96,2... | collective-permute-start | bytes 208904 | tf_op jit(solution)/shard_map/factors/ppermute | solution.py:294
  37.5 0.0 collective-permute-done.6.received
  37.5 3.5 %collective-permute-start.8 = (f32[136,128]{1,0:T(8,128)S(1)}, f32[136,128]{1,0:T(8,128)S(1)}, u32[]{:S(2)}, u32[]{:S(2)}) collective-permute-start(f32[136,128]{1,0:T(8,128)S(1)} %get-tuple-element.38), channel_id=1, source_target_pairs={{0,112},{16,416},{48,448},{32,144},{64,176},{80,480},{112,0},{96,2... | collective-permute-start | bytes 208904 | tf_op jit(solution)/shard_map/grad/ppermute | solution.py:294
  41.0 0.8 collective-permute-done.5.received
  41.8 4.0 %collective-permute-start.7 = (f32[136,128]{1,0:T(8,128)S(1)}, f32[136,128]{1,0:T(8,128)S(1)}, u32[]{:S(2)}, u32[]{:S(2)}) collective-permute-start(f32[136,128]{1,0:T(8,128)S(1)} %shard_map.44.after.own), channel_id=1, source_target_pairs={{0,368},{16,160},{48,192},{32,400},{64,432},{80,224},{112,256},{96... | collective-permute-start | bytes 208904 | tf_op jit(solution)/shard_map/factors/ppermute | solution.py:294
  45.8 1.1 collective-permute-done.8.received
  46.8 5.4 %collective-permute-start.10 = (f32[136,128]{1,0:T(8,128)S(1)}, f32[136,128]{1,0:T(8,128)S(1)}, u32[]{:S(2)}, u32[]{:S(2)}) collective-permute-start(f32[136,128]{1,0:T(8,128)S(1)} %shard_map.45.after.own), channel_id=1, source_target_pairs={{0,368},{16,160},{48,192},{32,400},{64,432},{80,224},{112,256},{96... | collective-permute-start | bytes 208904 | tf_op jit(solution)/shard_map/grad/ppermute | solution.py:294
  52.2 0.1 collective-permute-done.7.received
  52.3 7.0 %collective-permute-start.9 = (f32[136,128]{1,0:T(8,128)S(1)}, f32[136,128]{1,0:T(8,128)S(1)}, u32[]{:S(2)}, u32[]{:S(2)}) collective-permute-start(f32[136,128]{1,0:T(8,128)S(1)} %shard_map.46.after.near), channel_id=1, source_target_pairs={{0,112},{16,416},{48,448},{32,144},{64,176},{80,480},{112,0},{96,2... | collective-permute-start | bytes 208904 | tf_op jit(solution)/shard_map/factors/ppermute | solution.py:294
  59.3 0.0 collective-permute-done.10.received
  59.3 5.9 %collective-permute-start.12 = (f32[136,128]{1,0:T(8,128)S(1)}, f32[136,128]{1,0:T(8,128)S(1)}, u32[]{:S(2)}, u32[]{:S(2)}) collective-permute-start(f32[136,128]{1,0:T(8,128)S(1)} %shard_map.47.after.near), channel_id=1, source_target_pairs={{0,112},{16,416},{48,448},{32,144},{64,176},{80,480},{112,0},{96,2... | collective-permute-start | bytes 208904 | tf_op jit(solution)/shard_map/grad/ppermute | solution.py:294
  65.3 0.0 collective-permute-done.9.far
  65.3 1.9 %collective-permute-start.11 = (f32[272,128]{1,0:T(8,128)S(1)}, f32[272,128]{1,0:T(8,128)S(1)}, u32[]{:S(2)}, u32[]{:S(2)}) collective-permute-start(f32[272,128]{1,0:T(8,128)S(1)} %shard_map.48.after.near), channel_id=1, source_target_pairs={{0,496},{16,32},{48,64},{32,16},{64,48},{80,96},{112,128},{96,80},... | collective-permute-start | bytes 417800 | tf_op jit(solution)/shard_map/factors/ppermute | solution.py:294
  67.3 1.4 %collective-permute-done.12.far = f32[136,128]{1,0:T(8,128)S(1)} collective-permute-done((f32[136,128]{1,0:T(8,128)S(1)}, f32[136,128]{1,0:T(8,128)S(1)}, u32[]{:S(2)}, u32[]{:S(2)}) %collective-permute-start.12) | collective-permute-done | bytes 69664 | tf_op jit(solution)/shard_map/grad/ppermute | solution.py:294
  68.7 2.2 %collective-permute-start.14 = (f32[272,128]{1,0:T(8,128)S(1)}, f32[272,128]{1,0:T(8,128)S(1)}, u32[]{:S(2)}, u32[]{:S(2)}) collective-permute-start(f32[272,128]{1,0:T(8,128)S(1)} %shard_map.49.after.near), channel_id=1, source_target_pairs={{0,496},{16,32},{48,64},{32,16},{64,48},{80,96},{112,128},{96,80},... | collective-permute-start | bytes 417800 | tf_op jit(solution)/shard_map/grad/ppermute | solution.py:294
  70.9 0.8 collective-permute-done.11.far
  71.7 4.4 %collective-permute-start.13 = (f32[544,128]{1,0:T(8,128)S(1)}, f32[544,128]{1,0:T(8,128)S(1)}, u32[]{:S(2)}, u32[]{:S(2)}) collective-permute-start(f32[544,128]{1,0:T(8,128)S(1)} %shard_map.50.after.near), channel_id=1, source_target_pairs={{0,48},{16,480},{48,0},{32,80},{64,112},{80,32},{112,64},{96,144},... | collective-permute-start | bytes 835592 | tf_op jit(solution)/shard_map/factors/ppermute | solution.py:294
  76.1 0.0 collective-permute-done.14.far
  76.2 3.8 %collective-permute-start.15 = (f32[544,128]{1,0:T(8,128)S(1)}, f32[544,128]{1,0:T(8,128)S(1)}, u32[]{:S(2)}, u32[]{:S(2)}) collective-permute-start(f32[544,128]{1,0:T(8,128)S(1)} %shard_map.51.after.near), channel_id=1, source_target_pairs={{0,48},{16,480},{48,0},{32,80},{64,112},{80,32},{112,64},{96,144},... | collective-permute-start | bytes 835592 | tf_op jit(solution)/shard_map/grad/ppermute | solution.py:294
  80.0 0.8 collective-permute-done.13.far
  80.8 3.5 %shard_map.52.x = f32[512,512]{1,0:T(8,128)S(1)} custom-call(f32[544,128]{1,0:T(8,128)S(1)} %shard_map.50.after.near, f32[544,128]{1,0:T(8,128)S(1)} %collective-permute-done.13.far, f32[544,128]{1,0:T(8,128)S(1)} %shard_map.51.after.near), custom_call_target="tpu_custom_call" | custom-call | bytes 1 | tf_op jit(solution)/shard_map/pallas_call | solution.py:282
  84.3 1.9 %collective-permute-start.17 = (f32[512,512]{1,0:T(8,128)S(1)}, f32[512,512]{1,0:T(8,128)S(1)}, u32[]{:S(2)}, u32[]{:S(2)}) collective-permute-start(f32[512,512]{1,0:T(8,128)S(1)} %shard_map.52.x), channel_id=1, source_target_pairs={{0,16},{16,0},{32,48},{48,32},{64,80},{80,64},{96,112},{112,96},{1... | collective-permute-start | bytes 3145736 | tf_op jit(solution)/shard_map/root/ppermute | solution.py:294
  86.3 0.0 collective-permute-done.15.far
  86.3 2.4 %collective-permute-start.16 = (f32[1088,128]{1,0:T(8,128)S(1)}, f32[1088,128]{1,0:T(8,128)S(1)}, u32[]{:S(2)}, u32[]{:S(2)}) collective-permute-start(f32[1088,128]{1,0:T(8,128)S(1)} %shard_map.53.own), channel_id=1, source_target_pairs={{0,16},{16,0},{32,48},{48,32},{64,80},{80,64},{96,112},{112,96},{1... | collective-permute-start | bytes 1671176 | tf_op jit(solution)/shard_map/grad/ppermute | solution.py:294
  88.7 0.7 shard_map.54.begun
  89.5 0.0 copy-start
  89.5 0.8 collective-permute-done.16.other
  90.3 0.8 shard_map.55
  91.1 0.0 collective-permute-done.17.x
  91.1 0.0 copy-done
  91.1 2.0 %shard_map.56 = f32[16,8,128]{2,1,0:T(8,128)S(1)} custom-call(s32[32]{0:T(128)S(1)} %copy-done, bf16[512,512]{1,0:T(8,128)(2,1)S(1)} %get-tuple-element.39.high, bf16[512,512]{1,0:T(8,128)(2,1)S(1)} %get-tuple-element.40.low, f32[512,512]{1,0:T(8,128)S(1)} %collective-permute-done.17.x), custom_call_target="tpu_custom_call" | custom-call | tf_op jit(solution)/shard_map/pallas_call | solution.py:282
  93.2 13.1 %all_to_all.5.tiles = f32[16,8,128]{2,1,0:T(8,128)S(1)} all-to-all(f32[16,8,128]{2,1,0:T(8,128)S(1)} %shard_map.56), channel_id=1, replica_groups=mesh['dp'=32,'mp'=16] {'mp'}, dimensions={0} | all-to-all | bytes 131072 | tf_op jit(solution)/shard_map/all_to_all | solution.py:373
  106.3 0.7 shard_map.57
  (13 shorter events, 0.2 us)
Async XLA Ops:
  3.6 10.7 %collective-permute-start = (f32[1088,128]{1,0:T(8,128)S(1)}, f32[1088,128]{1,0:T(8,128)S(1)}, u32[]{:S(2)}, u32[]{:S(2)}) collective-permute-start(f32[1088,128]{1,0:T(8,128)S(1)} %get-tuple-element.24), channel_id=1, source_target_pairs={{0,16},{16,0},{32,48},{48,32},{64,80},{80,64},{96,112},{112,96},{1... | collective-permute-start | bytes 1671176 | tf_op jit(solution)/shard_map/factors/ppermute | solution.py:294
  12.4 8.1 %collective-permute-start.2 = (f32[1088,128]{1,0:T(8,128)S(1)}, f32[1088,128]{1,0:T(8,128)S(1)}, u32[]{:S(2)}, u32[]{:S(2)}) collective-permute-start(f32[1088,128]{1,0:T(8,128)S(1)} %get-tuple-element.28), channel_id=1, source_target_pairs={{0,16},{16,0},{32,48},{48,32},{64,80},{80,64},{96,112},{112,96},{1... | collective-permute-start | bytes 1671176 | tf_op jit(solution)/shard_map/grad/ppermute | solution.py:294
  14.5 10.3 %collective-permute-start.1 = (f32[544,128]{1,0:T(8,128)S(1)}, f32[544,128]{1,0:T(8,128)S(1)}, u32[]{:S(2)}, u32[]{:S(2)}) collective-permute-start(f32[544,128]{1,0:T(8,128)S(1)} %get-tuple-element.27), channel_id=1, source_target_pairs={{0,48},{16,480},{48,0},{32,80},{64,112},{80,32},{112,64},{96,144},... | collective-permute-start | bytes 835592 | tf_op jit(solution)/shard_map/factors/ppermute | solution.py:294
  20.7 9.7 %collective-permute-start.4 = (f32[544,128]{1,0:T(8,128)S(1)}, f32[544,128]{1,0:T(8,128)S(1)}, u32[]{:S(2)}, u32[]{:S(2)}) collective-permute-start(f32[544,128]{1,0:T(8,128)S(1)} %get-tuple-element.32), channel_id=1, source_target_pairs={{0,48},{16,480},{48,0},{32,80},{64,112},{80,32},{112,64},{96,144},... | collective-permute-start | bytes 835592 | tf_op jit(solution)/shard_map/grad/ppermute | solution.py:294
  24.8 7.5 %collective-permute-start.3 = (f32[272,128]{1,0:T(8,128)S(1)}, f32[272,128]{1,0:T(8,128)S(1)}, u32[]{:S(2)}, u32[]{:S(2)}) collective-permute-start(f32[272,128]{1,0:T(8,128)S(1)} %get-tuple-element.31), channel_id=1, source_target_pairs={{0,496},{16,32},{48,64},{32,16},{64,48},{80,96},{112,128},{96,80},... | collective-permute-start | bytes 417800 | tf_op jit(solution)/shard_map/factors/ppermute | solution.py:294
  30.4 7.1 %collective-permute-start.6 = (f32[272,128]{1,0:T(8,128)S(1)}, f32[272,128]{1,0:T(8,128)S(1)}, u32[]{:S(2)}, u32[]{:S(2)}) collective-permute-start(f32[272,128]{1,0:T(8,128)S(1)} %get-tuple-element.36), channel_id=1, source_target_pairs={{0,496},{16,32},{48,64},{32,16},{64,48},{80,96},{112,128},{96,80},... | collective-permute-start | bytes 417800 | tf_op jit(solution)/shard_map/grad/ppermute | solution.py:294
  32.4 9.4 %collective-permute-start.5 = (f32[136,128]{1,0:T(8,128)S(1)}, f32[136,128]{1,0:T(8,128)S(1)}, u32[]{:S(2)}, u32[]{:S(2)}) collective-permute-start(f32[136,128]{1,0:T(8,128)S(1)} %get-tuple-element.35), channel_id=1, source_target_pairs={{0,112},{16,416},{48,448},{32,144},{64,176},{80,480},{112,0},{96,2... | collective-permute-start | bytes 208904 | tf_op jit(solution)/shard_map/factors/ppermute | solution.py:294
  37.5 9.3 %collective-permute-start.8 = (f32[136,128]{1,0:T(8,128)S(1)}, f32[136,128]{1,0:T(8,128)S(1)}, u32[]{:S(2)}, u32[]{:S(2)}) collective-permute-start(f32[136,128]{1,0:T(8,128)S(1)} %get-tuple-element.38), channel_id=1, source_target_pairs={{0,112},{16,416},{48,448},{32,144},{64,176},{80,480},{112,0},{96,2... | collective-permute-start | bytes 208904 | tf_op jit(solution)/shard_map/grad/ppermute | solution.py:294
  41.8 10.5 %collective-permute-start.7 = (f32[136,128]{1,0:T(8,128)S(1)}, f32[136,128]{1,0:T(8,128)S(1)}, u32[]{:S(2)}, u32[]{:S(2)}) collective-permute-start(f32[136,128]{1,0:T(8,128)S(1)} %shard_map.44.after.own), channel_id=1, source_target_pairs={{0,368},{16,160},{48,192},{32,400},{64,432},{80,224},{112,256},{96... | collective-permute-start | bytes 208904 | tf_op jit(solution)/shard_map/factors/ppermute | solution.py:294
  46.8 12.5 %collective-permute-start.10 = (f32[136,128]{1,0:T(8,128)S(1)}, f32[136,128]{1,0:T(8,128)S(1)}, u32[]{:S(2)}, u32[]{:S(2)}) collective-permute-start(f32[136,128]{1,0:T(8,128)S(1)} %shard_map.45.after.own), channel_id=1, source_target_pairs={{0,368},{16,160},{48,192},{32,400},{64,432},{80,224},{112,256},{96... | collective-permute-start | bytes 208904 | tf_op jit(solution)/shard_map/grad/ppermute | solution.py:294
  52.3 13.0 %collective-permute-start.9 = (f32[136,128]{1,0:T(8,128)S(1)}, f32[136,128]{1,0:T(8,128)S(1)}, u32[]{:S(2)}, u32[]{:S(2)}) collective-permute-start(f32[136,128]{1,0:T(8,128)S(1)} %shard_map.46.after.near), channel_id=1, source_target_pairs={{0,112},{16,416},{48,448},{32,144},{64,176},{80,480},{112,0},{96,2... | collective-permute-start | bytes 208904 | tf_op jit(solution)/shard_map/factors/ppermute | solution.py:294
  59.3 9.3 %collective-permute-start.12 = (f32[136,128]{1,0:T(8,128)S(1)}, f32[136,128]{1,0:T(8,128)S(1)}, u32[]{:S(2)}, u32[]{:S(2)}) collective-permute-start(f32[136,128]{1,0:T(8,128)S(1)} %shard_map.47.after.near), channel_id=1, source_target_pairs={{0,112},{16,416},{48,448},{32,144},{64,176},{80,480},{112,0},{96,2... | collective-permute-start | bytes 208904 | tf_op jit(solution)/shard_map/grad/ppermute | solution.py:294
  65.3 6.4 %collective-permute-start.11 = (f32[272,128]{1,0:T(8,128)S(1)}, f32[272,128]{1,0:T(8,128)S(1)}, u32[]{:S(2)}, u32[]{:S(2)}) collective-permute-start(f32[272,128]{1,0:T(8,128)S(1)} %shard_map.48.after.near), channel_id=1, source_target_pairs={{0,496},{16,32},{48,64},{32,16},{64,48},{80,96},{112,128},{96,80},... | collective-permute-start | bytes 417800 | tf_op jit(solution)/shard_map/factors/ppermute | solution.py:294
  68.7 7.5 %collective-permute-start.14 = (f32[272,128]{1,0:T(8,128)S(1)}, f32[272,128]{1,0:T(8,128)S(1)}, u32[]{:S(2)}, u32[]{:S(2)}) collective-permute-start(f32[272,128]{1,0:T(8,128)S(1)} %shard_map.49.after.near), channel_id=1, source_target_pairs={{0,496},{16,32},{48,64},{32,16},{64,48},{80,96},{112,128},{96,80},... | collective-permute-start | bytes 417800 | tf_op jit(solution)/shard_map/grad/ppermute | solution.py:294
  71.7 9.1 %collective-permute-start.13 = (f32[544,128]{1,0:T(8,128)S(1)}, f32[544,128]{1,0:T(8,128)S(1)}, u32[]{:S(2)}, u32[]{:S(2)}) collective-permute-start(f32[544,128]{1,0:T(8,128)S(1)} %shard_map.50.after.near), channel_id=1, source_target_pairs={{0,48},{16,480},{48,0},{32,80},{64,112},{80,32},{112,64},{96,144},... | collective-permute-start | bytes 835592 | tf_op jit(solution)/shard_map/factors/ppermute | solution.py:294
  76.2 10.1 %collective-permute-start.15 = (f32[544,128]{1,0:T(8,128)S(1)}, f32[544,128]{1,0:T(8,128)S(1)}, u32[]{:S(2)}, u32[]{:S(2)}) collective-permute-start(f32[544,128]{1,0:T(8,128)S(1)} %shard_map.51.after.near), channel_id=1, source_target_pairs={{0,48},{16,480},{48,0},{32,80},{64,112},{80,32},{112,64},{96,144},... | collective-permute-start | bytes 835592 | tf_op jit(solution)/shard_map/grad/ppermute | solution.py:294
  84.3 6.8 %collective-permute-start.17 = (f32[512,512]{1,0:T(8,128)S(1)}, f32[512,512]{1,0:T(8,128)S(1)}, u32[]{:S(2)}, u32[]{:S(2)}) collective-permute-start(f32[512,512]{1,0:T(8,128)S(1)} %shard_map.52.x), channel_id=1, source_target_pairs={{0,16},{16,0},{32,48},{48,32},{64,80},{80,64},{96,112},{112,96},{1... | collective-permute-start | bytes 3145736 | tf_op jit(solution)/shard_map/root/ppermute | solution.py:294
  86.3 4.0 %collective-permute-start.16 = (f32[1088,128]{1,0:T(8,128)S(1)}, f32[1088,128]{1,0:T(8,128)S(1)}, u32[]{:S(2)}, u32[]{:S(2)}) collective-permute-start(f32[1088,128]{1,0:T(8,128)S(1)} %shard_map.53.own), channel_id=1, source_target_pairs={{0,16},{16,0},{32,48},{48,32},{64,80},{80,64},{96,112},{112,96},{1... | collective-permute-start | bytes 1671176 | tf_op jit(solution)/shard_map/grad/ppermute | solution.py:294
  89.5 1.7 %copy-start = (s32[32]{0:T(128)S(1)}, s32[32]{0:T(128)}, u32[]{:S(2)}) copy-start(s32[32]{0:T(128)} %owner.1) | copy-start | bytes 388

commit v5 on v4

--- a/solution.py
+++ b/solution.py
@@ -39,7 +39,7 @@
     return (v + 5) % Z if v % 2 else (v - 5) % Z
 
 
-EIGHTH = {3: 0, 8: 0, 0: 1, 11: 1, 7: 2, 12: 2, 4: 3, 15: 3, 9: 4, 14: 4, 1: 5, 6: 5, 5: 6, 10: 6, 2: 7, 13: 7}
+QUARTER = {0: 0, 3: 0, 8: 0, 11: 0, 4: 1, 7: 1, 12: 1, 15: 1, 1: 2, 6: 2, 9: 2, 14: 2, 2: 3, 5: 3, 10: 3, 13: 3}
 
 
 def holders(v, partners):
@@ -49,7 +49,7 @@
 
 
 def order_code(v):
-    order = [EIGHTH[u] for u in holders(v, (partner3, partner2, partner1))]
+    order = [2 * QUARTER[u] + n for u in holders(v, (partner2, partner1)) for n in range(2)]
     assert sorted(order) == list(range(8))
     return sum(order.index(e) << (3 * e) for e in range(8))
 
@@ -321,7 +321,7 @@
     return call(kernel, [(2 * half, B)], [], near, far, [after], cost=JOIN_FLOPS)[0]
 
 
-WAY = ((halve, 1), (halve, 2), (halve, 3), (add, 4), (add, 3), (join, 2), (join, 1))
+WAY = ((halve, 1), (halve, 2), (add, 3), (add, 4), (add, 2), (join, 1))
 
 
 def totals(first, second):

time: 108 us -> 108 us (level)
  starting transfers between devices: 70.1 us -> 59.6 us
  waiting for transfers between devices: 11.6 us -> 20.6 us
  blocking collectives: 13.1 us -> 15.3 us
    ppermute x18 -> x16, starting transfers between devices: 70.1 us -> 59.6 us  [move(): return lax.ppermute(x, 'dp', PAIRS[step])]
    ppermute x18 -> x16, waiting for transfers between devices: 11.6 us -> 20.6 us  [move(): return lax.ppermute(x, 'dp', PAIRS[step])]
    all_to_all x1, blocking collectives: 13.1 us -> 15.3 us  [per_device(): tiles = lax.all_to_all(tiles, 'mp', split_axis=0, concat_axis=0, tiled=True)]
    pallas_call x20 -> x18, Pallas kernels: 8.21 us -> 8.21 us  [call(): pl.pallas_call(kernel, out_shape=[jax.ShapeDtypeStruct(s, dtype) for s in...]
  transfers between devices with their start and end apart: 18 -> 16, of which waited for: 9 -> 8; matrix products, arithmetic and copies ran while one was open for 0% -> 0% of each run, Pallas kernels for 5% -> 5%
where the time goes in v5:
time: 108 us
  starting transfers between devices  59.6 us (55%)
  waiting for transfers between devices  20.6 us (19%)
  blocking collectives  15.3 us (14%)
  Pallas kernels  11.8 us (11%)
    ppermute x16, starting transfers between devices, move(): return lax.ppermute(x, 'dp', PAIRS[step])  59.6 us
    ppermute x16, waiting for transfers between devices, move(): return lax.ppermute(x, 'dp', PAIRS[step])  20.6 us
    all_to_all x1, blocking collectives, per_device(): tiles = lax.all_to_all(tiles, 'mp', split_axis=0, concat_axis=0, tiled=True)  15.3 us
    pallas_call x18, Pallas kernels, call(): pl.pallas_call(kernel, out_shape=[jax.ShapeDtypeStruct(s, dtype) for s in...  8.21 us
    pallas_call x1, Pallas kernels, per_device(): pl.pallas_call(front, out_shape=[jax.ShapeDtypeStruct(whole, jnp.float32)...  3.63 us
  transfers between devices with their start and end apart: 16, of which 8 were waited for; matrix products, arithmetic and copies ran while one was open for 0% of the time, Pallas kernels for 5%

profile of v5, /device:TPU:1, one launch (start us, length us, event | category | flops | bytes accessed | tf_op | source)
XLA Modules:
  0.0 107.7 jit_solution(1614426680970642446)
XLA Ops:
  0.0 3.6 %shard_map.37 = (f32[1088,128]{1,0:T(8,128)S(1)}, f32[1088,128]{1,0:T(8,128)S(1)}, f32[1088,128]{1,0:T(8,128)S(1)}, f32[1088,128]{1,0:T(8,128)S(1)}) custom-call(bf16[2048,512]{1,0:T(8,128)(2,1)} %acts.1, bf16[2048,512]{1,0:T(8,128)(2,1)} %grads_out.1), custom_call_target="tpu_custom_call" | custom-call | tf_op jit(solution)/shard_map/pallas_call | solution.py:353
  3.6 8.8 %collective-permute-start = (f32[1088,128]{1,0:T(8,128)S(1)}, f32[1088,128]{1,0:T(8,128)S(1)}, u32[]{:S(2)}, u32[]{:S(2)}) collective-permute-start(f32[1088,128]{1,0:T(8,128)S(1)} %get-tuple-element.20), channel_id=1, source_target_pairs={{0,16},{16,0},{32,48},{48,32},{64,80},{80,64},{96,112},{112,96},{1... | collective-permute-start | bytes 1671176 | tf_op jit(solution)/shard_map/factors/ppermute | solution.py:294
  12.4 1.9 %collective-permute-start.2 = (f32[1088,128]{1,0:T(8,128)S(1)}, f32[1088,128]{1,0:T(8,128)S(1)}, u32[]{:S(2)}, u32[]{:S(2)}) collective-permute-start(f32[1088,128]{1,0:T(8,128)S(1)} %get-tuple-element.24), channel_id=1, source_target_pairs={{0,16},{16,0},{32,48},{48,32},{64,80},{80,64},{96,112},{112,96},{1... | collective-permute-start | bytes 1671176 | tf_op jit(solution)/shard_map/grad/ppermute | solution.py:294
  14.4 0.0 collective-permute-done.received
  14.4 0.1 shard_map.38
  14.4 6.1 %collective-permute-start.1 = (f32[544,128]{1,0:T(8,128)S(1)}, f32[544,128]{1,0:T(8,128)S(1)}, u32[]{:S(2)}, u32[]{:S(2)}) collective-permute-start(f32[544,128]{1,0:T(8,128)S(1)} %get-tuple-element.23), channel_id=1, source_target_pairs={{0,48},{16,480},{48,0},{32,80},{64,112},{80,32},{112,64},{96,144},... | collective-permute-start | bytes 835592 | tf_op jit(solution)/shard_map/factors/ppermute | solution.py:294
  20.6 0.0 collective-permute-done.2.received
  20.6 0.1 shard_map.39
  20.6 1.9 %collective-permute-start.4 = (f32[544,128]{1,0:T(8,128)S(1)}, f32[544,128]{1,0:T(8,128)S(1)}, u32[]{:S(2)}, u32[]{:S(2)}) collective-permute-start(f32[544,128]{1,0:T(8,128)S(1)} %get-tuple-element.28), channel_id=1, source_target_pairs={{0,48},{16,480},{48,0},{32,80},{64,112},{80,32},{112,64},{96,144},... | collective-permute-start | bytes 835592 | tf_op jit(solution)/shard_map/grad/ppermute | solution.py:294
  22.6 2.2 %collective-permute-done.1.received = f32[544,128]{1,0:T(8,128)S(1)} collective-permute-done((f32[544,128]{1,0:T(8,128)S(1)}, f32[544,128]{1,0:T(8,128)S(1)}, u32[]{:S(2)}, u32[]{:S(2)}) %collective-permute-start.1) | collective-permute-done | bytes 278560 | tf_op jit(solution)/shard_map/factors/ppermute | solution.py:294
  24.8 1.9 %collective-permute-start.3 = (f32[272,128]{1,0:T(8,128)S(1)}, f32[272,128]{1,0:T(8,128)S(1)}, u32[]{:S(2)}, u32[]{:S(2)}) collective-permute-start(f32[272,128]{1,0:T(8,128)S(1)} %get-tuple-element.27), channel_id=1, source_target_pairs={{0,496},{16,32},{48,64},{32,16},{64,48},{80,96},{112,128},{96,80},... | collective-permute-start | bytes 417800 | tf_op jit(solution)/shard_map/factors/ppermute | solution.py:294
  26.7 3.6 %collective-permute-done.4.received = f32[544,128]{1,0:T(8,128)S(1)} collective-permute-done((f32[544,128]{1,0:T(8,128)S(1)}, f32[544,128]{1,0:T(8,128)S(1)}, u32[]{:S(2)}, u32[]{:S(2)}) %collective-permute-start.4) | collective-permute-done | bytes 278560 | tf_op jit(solution)/shard_map/grad/ppermute | solution.py:294
  30.4 1.9 %collective-permute-start.6 = (f32[272,128]{1,0:T(8,128)S(1)}, f32[272,128]{1,0:T(8,128)S(1)}, u32[]{:S(2)}, u32[]{:S(2)}) collective-permute-start(f32[272,128]{1,0:T(8,128)S(1)} %get-tuple-element.30), channel_id=1, source_target_pairs={{0,496},{16,32},{48,64},{32,16},{64,48},{80,96},{112,128},{96,80},... | collective-permute-start | bytes 417800 | tf_op jit(solution)/shard_map/grad/ppermute | solution.py:294
  32.3 0.0 collective-permute-done.3.received
  32.4 5.1 %collective-permute-start.5 = (f32[272,128]{1,0:T(8,128)S(1)}, f32[272,128]{1,0:T(8,128)S(1)}, u32[]{:S(2)}, u32[]{:S(2)}) collective-permute-start(f32[272,128]{1,0:T(8,128)S(1)} %shard_map.42.after.own), channel_id=1, source_target_pairs={{0,112},{16,416},{48,448},{32,144},{64,176},{80,480},{112,0},{96,2... | collective-permute-start | bytes 417800 | tf_op jit(solution)/shard_map/factors/ppermute | solution.py:294
  37.5 0.0 collective-permute-done.6.received
  37.5 3.5 %collective-permute-start.8 = (f32[272,128]{1,0:T(8,128)S(1)}, f32[272,128]{1,0:T(8,128)S(1)}, u32[]{:S(2)}, u32[]{:S(2)}) collective-permute-start(f32[272,128]{1,0:T(8,128)S(1)} %shard_map.43.after.own), channel_id=1, source_target_pairs={{0,112},{16,416},{48,448},{32,144},{64,176},{80,480},{112,0},{96,2... | collective-permute-start | bytes 417800 | tf_op jit(solution)/shard_map/grad/ppermute | solution.py:294
  41.0 3.6 %collective-permute-done.5.received = f32[272,128]{1,0:T(8,128)S(1)} collective-permute-done((f32[272,128]{1,0:T(8,128)S(1)}, f32[272,128]{1,0:T(8,128)S(1)}, u32[]{:S(2)}, u32[]{:S(2)}) %collective-permute-start.5) | collective-permute-done | bytes 139296 | tf_op jit(solution)/shard_map/factors/ppermute | solution.py:294
  44.6 3.1 %collective-permute-start.7 = (f32[272,128]{1,0:T(8,128)S(1)}, f32[272,128]{1,0:T(8,128)S(1)}, u32[]{:S(2)}, u32[]{:S(2)}) collective-permute-start(f32[272,128]{1,0:T(8,128)S(1)} %shard_map.44.after.own), channel_id=1, source_target_pairs={{0,368},{16,160},{48,192},{32,400},{64,432},{80,224},{112,256},{96... | collective-permute-start | bytes 417800 | tf_op jit(solution)/shard_map/factors/ppermute | solution.py:294
  47.8 2.7 %collective-permute-done.8.received = f32[272,128]{1,0:T(8,128)S(1)} collective-permute-done((f32[272,128]{1,0:T(8,128)S(1)}, f32[272,128]{1,0:T(8,128)S(1)}, u32[]{:S(2)}, u32[]{:S(2)}) %collective-permute-start.8) | collective-permute-done | bytes 139296 | tf_op jit(solution)/shard_map/grad/ppermute | solution.py:294
  50.5 4.6 %collective-permute-start.10 = (f32[272,128]{1,0:T(8,128)S(1)}, f32[272,128]{1,0:T(8,128)S(1)}, u32[]{:S(2)}, u32[]{:S(2)}) collective-permute-start(f32[272,128]{1,0:T(8,128)S(1)} %shard_map.45.after.own), channel_id=1, source_target_pairs={{0,368},{16,160},{48,192},{32,400},{64,432},{80,224},{112,256},{96... | collective-permute-start | bytes 417800 | tf_op jit(solution)/shard_map/grad/ppermute | solution.py:294
  55.0 2.4 %collective-permute-done.7.received = f32[272,128]{1,0:T(8,128)S(1)} collective-permute-done((f32[272,128]{1,0:T(8,128)S(1)}, f32[272,128]{1,0:T(8,128)S(1)}, u32[]{:S(2)}, u32[]{:S(2)}) %collective-permute-start.7) | collective-permute-done | bytes 139296 | tf_op jit(solution)/shard_map/factors/ppermute | solution.py:294
  57.4 3.7 %collective-permute-start.9 = (f32[272,128]{1,0:T(8,128)S(1)}, f32[272,128]{1,0:T(8,128)S(1)}, u32[]{:S(2)}, u32[]{:S(2)}) collective-permute-start(f32[272,128]{1,0:T(8,128)S(1)} %shard_map.46.after.near), channel_id=1, source_target_pairs={{0,496},{16,32},{48,64},{32,16},{64,48},{80,96},{112,128},{96,80},... | collective-permute-start | bytes 417800 | tf_op jit(solution)/shard_map/factors/ppermute | solution.py:294
  61.1 4.4 %collective-permute-done.10.received = f32[272,128]{1,0:T(8,128)S(1)} collective-permute-done((f32[272,128]{1,0:T(8,128)S(1)}, f32[272,128]{1,0:T(8,128)S(1)}, u32[]{:S(2)}, u32[]{:S(2)}) %collective-permute-start.10) | collective-permute-done | bytes 139296 | tf_op jit(solution)/shard_map/grad/ppermute | solution.py:294
  65.5 4.6 %collective-permute-start.12 = (f32[272,128]{1,0:T(8,128)S(1)}, f32[272,128]{1,0:T(8,128)S(1)}, u32[]{:S(2)}, u32[]{:S(2)}) collective-permute-start(f32[272,128]{1,0:T(8,128)S(1)} %shard_map.47.after.near), channel_id=1, source_target_pairs={{0,496},{16,32},{48,64},{32,16},{64,48},{80,96},{112,128},{96,80},... | collective-permute-start | bytes 417800 | tf_op jit(solution)/shard_map/grad/ppermute | solution.py:294
  70.1 0.0 collective-permute-done.9.far
  70.2 4.1 %collective-permute-start.11 = (f32[544,128]{1,0:T(8,128)S(1)}, f32[544,128]{1,0:T(8,128)S(1)}, u32[]{:S(2)}, u32[]{:S(2)}) collective-permute-start(f32[544,128]{1,0:T(8,128)S(1)} %shard_map.48.after.near), channel_id=1, source_target_pairs={{0,48},{16,480},{48,0},{32,80},{64,112},{80,32},{112,64},{96,144},... | collective-permute-start | bytes 835592 | tf_op jit(solution)/shard_map/factors/ppermute | solution.py:294
  74.3 0.0 collective-permute-done.12.far
  74.3 4.1 %collective-permute-start.13 = (f32[544,128]{1,0:T(8,128)S(1)}, f32[544,128]{1,0:T(8,128)S(1)}, u32[]{:S(2)}, u32[]{:S(2)}) collective-permute-start(f32[544,128]{1,0:T(8,128)S(1)} %shard_map.49.after.near), channel_id=1, source_target_pairs={{0,48},{16,480},{48,0},{32,80},{64,112},{80,32},{112,64},{96,144},... | collective-permute-start | bytes 835592 | tf_op jit(solution)/shard_map/grad/ppermute | solution.py:294
  78.4 0.9 collective-permute-done.11.far
  79.2 3.5 %shard_map.50.x = f32[512,512]{1,0:T(8,128)S(1)} custom-call(f32[544,128]{1,0:T(8,128)S(1)} %shard_map.48.after.near, f32[544,128]{1,0:T(8,128)S(1)} %collective-permute-done.11.far, f32[544,128]{1,0:T(8,128)S(1)} %shard_map.49.after.near), custom_call_target="tpu_custom_call" | custom-call | bytes 1 | tf_op jit(solution)/shard_map/pallas_call | solution.py:282
  82.8 1.9 %collective-permute-start.15 = (f32[512,512]{1,0:T(8,128)S(1)}, f32[512,512]{1,0:T(8,128)S(1)}, u32[]{:S(2)}, u32[]{:S(2)}) collective-permute-start(f32[512,512]{1,0:T(8,128)S(1)} %shard_map.50.x), channel_id=1, source_target_pairs={{0,16},{16,0},{32,48},{48,32},{64,80},{80,64},{96,112},{112,96},{1... | collective-permute-start | bytes 3145736 | tf_op jit(solution)/shard_map/root/ppermute | solution.py:294
  84.7 0.0 collective-permute-done.13.far
  84.7 2.4 %collective-permute-start.14 = (f32[1088,128]{1,0:T(8,128)S(1)}, f32[1088,128]{1,0:T(8,128)S(1)}, u32[]{:S(2)}, u32[]{:S(2)}) collective-permute-start(f32[1088,128]{1,0:T(8,128)S(1)} %shard_map.51.own), channel_id=1, source_target_pairs={{0,16},{16,0},{32,48},{48,32},{64,80},{80,64},{96,112},{112,96},{1... | collective-permute-start | bytes 1671176 | tf_op jit(solution)/shard_map/grad/ppermute | solution.py:294
  87.2 0.7 shard_map.52.begun
  87.9 0.0 copy-start
  87.9 0.8 collective-permute-done.14.other
  88.7 0.8 shard_map.53
  89.5 0.0 collective-permute-done.15.x
  89.6 0.0 copy-done
  89.6 2.0 %shard_map.54 = f32[16,8,128]{2,1,0:T(8,128)S(1)} custom-call(s32[32]{0:T(128)S(1)} %copy-done, bf16[512,512]{1,0:T(8,128)(2,1)S(1)} %get-tuple-element.31.high, bf16[512,512]{1,0:T(8,128)(2,1)S(1)} %get-tuple-element.32.low, f32[512,512]{1,0:T(8,128)S(1)} %collective-permute-done.15.x), custom_call_target="tpu_custom_call" | custom-call | tf_op jit(solution)/shard_map/pallas_call | solution.py:282
  91.6 15.3 %all_to_all.5.tiles = f32[16,8,128]{2,1,0:T(8,128)S(1)} all-to-all(f32[16,8,128]{2,1,0:T(8,128)S(1)} %shard_map.54), channel_id=1, replica_groups=mesh['dp'=32,'mp'=16] {'mp'}, dimensions={0} | all-to-all | bytes 131072 | tf_op jit(solution)/shard_map/all_to_all | solution.py:373
  106.9 0.7 shard_map.55
  (11 shorter events, 0.2 us)
Async XLA Ops:
  3.6 10.7 %collective-permute-start = (f32[1088,128]{1,0:T(8,128)S(1)}, f32[1088,128]{1,0:T(8,128)S(1)}, u32[]{:S(2)}, u32[]{:S(2)}) collective-permute-start(f32[1088,128]{1,0:T(8,128)S(1)} %get-tuple-element.20), channel_id=1, source_target_pairs={{0,16},{16,0},{32,48},{48,32},{64,80},{80,64},{96,112},{112,96},{1... | collective-permute-start | bytes 1671176 | tf_op jit(solution)/shard_map/factors/ppermute | solution.py:294
  12.4 8.1 %collective-permute-start.2 = (f32[1088,128]{1,0:T(8,128)S(1)}, f32[1088,128]{1,0:T(8,128)S(1)}, u32[]{:S(2)}, u32[]{:S(2)}) collective-permute-start(f32[1088,128]{1,0:T(8,128)S(1)} %get-tuple-element.24), channel_id=1, source_target_pairs={{0,16},{16,0},{32,48},{48,32},{64,80},{80,64},{96,112},{112,96},{1... | collective-permute-start | bytes 1671176 | tf_op jit(solution)/shard_map/grad/ppermute | solution.py:294
  14.4 10.3 %collective-permute-start.1 = (f32[544,128]{1,0:T(8,128)S(1)}, f32[544,128]{1,0:T(8,128)S(1)}, u32[]{:S(2)}, u32[]{:S(2)}) collective-permute-start(f32[544,128]{1,0:T(8,128)S(1)} %get-tuple-element.23), channel_id=1, source_target_pairs={{0,48},{16,480},{48,0},{32,80},{64,112},{80,32},{112,64},{96,144},... | collective-permute-start | bytes 835592 | tf_op jit(solution)/shard_map/factors/ppermute | solution.py:294
  20.6 9.7 %collective-permute-start.4 = (f32[544,128]{1,0:T(8,128)S(1)}, f32[544,128]{1,0:T(8,128)S(1)}, u32[]{:S(2)}, u32[]{:S(2)}) collective-permute-start(f32[544,128]{1,0:T(8,128)S(1)} %get-tuple-element.28), channel_id=1, source_target_pairs={{0,48},{16,480},{48,0},{32,80},{64,112},{80,32},{112,64},{96,144},... | collective-permute-start | bytes 835592 | tf_op jit(solution)/shard_map/grad/ppermute | solution.py:294
  24.8 7.5 %collective-permute-start.3 = (f32[272,128]{1,0:T(8,128)S(1)}, f32[272,128]{1,0:T(8,128)S(1)}, u32[]{:S(2)}, u32[]{:S(2)}) collective-permute-start(f32[272,128]{1,0:T(8,128)S(1)} %get-tuple-element.27), channel_id=1, source_target_pairs={{0,496},{16,32},{48,64},{32,16},{64,48},{80,96},{112,128},{96,80},... | collective-permute-start | bytes 417800 | tf_op jit(solution)/shard_map/factors/ppermute | solution.py:294
  30.4 7.1 %collective-permute-start.6 = (f32[272,128]{1,0:T(8,128)S(1)}, f32[272,128]{1,0:T(8,128)S(1)}, u32[]{:S(2)}, u32[]{:S(2)}) collective-permute-start(f32[272,128]{1,0:T(8,128)S(1)} %get-tuple-element.30), channel_id=1, source_target_pairs={{0,496},{16,32},{48,64},{32,16},{64,48},{80,96},{112,128},{96,80},... | collective-permute-start | bytes 417800 | tf_op jit(solution)/shard_map/grad/ppermute | solution.py:294
  32.4 12.3 %collective-permute-start.5 = (f32[272,128]{1,0:T(8,128)S(1)}, f32[272,128]{1,0:T(8,128)S(1)}, u32[]{:S(2)}, u32[]{:S(2)}) collective-permute-start(f32[272,128]{1,0:T(8,128)S(1)} %shard_map.42.after.own), channel_id=1, source_target_pairs={{0,112},{16,416},{48,448},{32,144},{64,176},{80,480},{112,0},{96,2... | collective-permute-start | bytes 417800 | tf_op jit(solution)/shard_map/factors/ppermute | solution.py:294
  37.5 12.9 %collective-permute-start.8 = (f32[272,128]{1,0:T(8,128)S(1)}, f32[272,128]{1,0:T(8,128)S(1)}, u32[]{:S(2)}, u32[]{:S(2)}) collective-permute-start(f32[272,128]{1,0:T(8,128)S(1)} %shard_map.43.after.own), channel_id=1, source_target_pairs={{0,112},{16,416},{48,448},{32,144},{64,176},{80,480},{112,0},{96,2... | collective-permute-start | bytes 417800 | tf_op jit(solution)/shard_map/grad/ppermute | solution.py:294
  44.6 12.8 %collective-permute-start.7 = (f32[272,128]{1,0:T(8,128)S(1)}, f32[272,128]{1,0:T(8,128)S(1)}, u32[]{:S(2)}, u32[]{:S(2)}) collective-permute-start(f32[272,128]{1,0:T(8,128)S(1)} %shard_map.44.after.own), channel_id=1, source_target_pairs={{0,368},{16,160},{48,192},{32,400},{64,432},{80,224},{112,256},{96... | collective-permute-start | bytes 417800 | tf_op jit(solution)/shard_map/factors/ppermute | solution.py:294
  50.5 15.0 %collective-permute-start.10 = (f32[272,128]{1,0:T(8,128)S(1)}, f32[272,128]{1,0:T(8,128)S(1)}, u32[]{:S(2)}, u32[]{:S(2)}) collective-permute-start(f32[272,128]{1,0:T(8,128)S(1)} %shard_map.45.after.own), channel_id=1, source_target_pairs={{0,368},{16,160},{48,192},{32,400},{64,432},{80,224},{112,256},{96... | collective-permute-start | bytes 417800 | tf_op jit(solution)/shard_map/grad/ppermute | solution.py:294
  57.4 12.7 %collective-permute-start.9 = (f32[272,128]{1,0:T(8,128)S(1)}, f32[272,128]{1,0:T(8,128)S(1)}, u32[]{:S(2)}, u32[]{:S(2)}) collective-permute-start(f32[272,128]{1,0:T(8,128)S(1)} %shard_map.46.after.near), channel_id=1, source_target_pairs={{0,496},{16,32},{48,64},{32,16},{64,48},{80,96},{112,128},{96,80},... | collective-permute-start | bytes 417800 | tf_op jit(solution)/shard_map/factors/ppermute | solution.py:294
  65.5 8.8 %collective-permute-start.12 = (f32[272,128]{1,0:T(8,128)S(1)}, f32[272,128]{1,0:T(8,128)S(1)}, u32[]{:S(2)}, u32[]{:S(2)}) collective-permute-start(f32[272,128]{1,0:T(8,128)S(1)} %shard_map.47.after.near), channel_id=1, source_target_pairs={{0,496},{16,32},{48,64},{32,16},{64,48},{80,96},{112,128},{96,80},... | collective-permute-start | bytes 417800 | tf_op jit(solution)/shard_map/grad/ppermute | solution.py:294
  70.2 9.1 %collective-permute-start.11 = (f32[544,128]{1,0:T(8,128)S(1)}, f32[544,128]{1,0:T(8,128)S(1)}, u32[]{:S(2)}, u32[]{:S(2)}) collective-permute-start(f32[544,128]{1,0:T(8,128)S(1)} %shard_map.48.after.near), channel_id=1, source_target_pairs={{0,48},{16,480},{48,0},{32,80},{64,112},{80,32},{112,64},{96,144},... | collective-permute-start | bytes 835592 | tf_op jit(solution)/shard_map/factors/ppermute | solution.py:294
  74.3 10.4 %collective-permute-start.13 = (f32[544,128]{1,0:T(8,128)S(1)}, f32[544,128]{1,0:T(8,128)S(1)}, u32[]{:S(2)}, u32[]{:S(2)}) collective-permute-start(f32[544,128]{1,0:T(8,128)S(1)} %shard_map.49.after.near), channel_id=1, source_target_pairs={{0,48},{16,480},{48,0},{32,80},{64,112},{80,32},{112,64},{96,144},... | collective-permute-start | bytes 835592 | tf_op jit(solution)/shard_map/grad/ppermute | solution.py:294
  82.8 6.8 %collective-permute-start.15 = (f32[512,512]{1,0:T(8,128)S(1)}, f32[512,512]{1,0:T(8,128)S(1)}, u32[]{:S(2)}, u32[]{:S(2)}) collective-permute-start(f32[512,512]{1,0:T(8,128)S(1)} %shard_map.50.x), channel_id=1, source_target_pairs={{0,16},{16,0},{32,48},{48,32},{64,80},{80,64},{96,112},{112,96},{1... | collective-permute-start | bytes 3145736 | tf_op jit(solution)/shard_map/root/ppermute | solution.py:294
  84.7 4.0 %collective-permute-start.14 = (f32[1088,128]{1,0:T(8,128)S(1)}, f32[1088,128]{1,0:T(8,128)S(1)}, u32[]{:S(2)}, u32[]{:S(2)}) collective-permute-start(f32[1088,128]{1,0:T(8,128)S(1)} %shard_map.51.own), channel_id=1, source_target_pairs={{0,16},{16,0},{32,48},{48,32},{64,80},{80,64},{96,112},{112,96},{1... | collective-permute-start | bytes 1671176 | tf_op jit(solution)/shard_map/grad/ppermute | solution.py:294
  87.9 1.7 %copy-start = (s32[32]{0:T(128)S(1)}, s32[32]{0:T(128)}, u32[]{:S(2)}) copy-start(s32[32]{0:T(128)} %owner.1) | copy-start | bytes 388

commit v6 on v5

--- a/solution.py
+++ b/solution.py
@@ -55,7 +55,11 @@
 
 
 def position(z, side):
-    return -z % Z if side else z
+    return (1 - z) % Z if side else (z + 1) % Z
+
+
+def chip(v, side):
+    return (1 - v) % Z if side else (v - 1) % Z
 
 
 def role():
@@ -65,7 +69,7 @@
 
 def places(own):
     z = lax.axis_index("dp") // 2
-    v = jnp.where((role() == 0) == own, z, (Z - z) % Z)
+    v = jnp.where((role() == 0) == own, (z + 1) % Z, (Z + 1 - z) % Z)
     code = jnp.int32(order_code(0))
     for u in range(1, Z):
         code = jnp.where(v == u, order_code(u), code)
@@ -80,7 +84,7 @@
     pairs = []
     for z in range(Z):
         for side in range(2):
-            pairs.append((device(z, side), device(position(partner(position(z, side)), side), side)))
+            pairs.append((device(z, side), device(chip(partner(position(z, side)), side), side)))
     return pairs
 
 

time: 108 us -> 105 us (0.972)
  waiting for transfers between devices: 20.6 us -> 13.8 us
  starting transfers between devices: 59.6 us -> 66 us
  blocking collectives: 15.3 us -> 13 us
    ppermute x16, waiting for transfers between devices: 20.6 us -> 13.8 us  [move(): return lax.ppermute(x, 'dp', PAIRS[step])]
    ppermute x16, starting transfers between devices: 59.6 us -> 66 us  [move(): return lax.ppermute(x, 'dp', PAIRS[step])]
    all_to_all x1, blocking collectives: 15.3 us -> 13 us  [per_device(): tiles = lax.all_to_all(tiles, 'mp', split_axis=0, concat_axis=0, tiled=True)]
where the time goes in v6:
time: 105 us
  starting transfers between devices  66 us (63%)
  waiting for transfers between devices  13.8 us (13%)
  blocking collectives  13 us (12%)
  Pallas kernels  11.8 us (11%)
    ppermute x16, starting transfers between devices, move(): return lax.ppermute(x, 'dp', PAIRS[step])  66 us
    ppermute x16, waiting for transfers between devices, move(): return lax.ppermute(x, 'dp', PAIRS[step])  13.8 us
    all_to_all x1, blocking collectives, per_device(): tiles = lax.all_to_all(tiles, 'mp', split_axis=0, concat_axis=0, tiled=True)  13 us
    pallas_call x18, Pallas kernels, call(): pl.pallas_call(kernel, out_shape=[jax.ShapeDtypeStruct(s, dtype) for s in...  8.21 us
    pallas_call x1, Pallas kernels, per_device(): pl.pallas_call(front, out_shape=[jax.ShapeDtypeStruct(whole, jnp.float32)...  3.63 us
  transfers between devices with their start and end apart: 16, of which 8 were waited for; matrix products, arithmetic and copies ran while one was open for 0% of the time, Pallas kernels for 5%

profile of v6, /device:TPU:1, one launch (start us, length us, event | category | flops | bytes accessed | tf_op | source)
XLA Modules:
  0.0 104.9 jit_solution(4927956978364736034)
XLA Ops:
  0.0 3.6 %shard_map.37 = (f32[1088,128]{1,0:T(8,128)S(1)}, f32[1088,128]{1,0:T(8,128)S(1)}, f32[1088,128]{1,0:T(8,128)S(1)}, f32[1088,128]{1,0:T(8,128)S(1)}) custom-call(bf16[2048,512]{1,0:T(8,128)(2,1)} %acts.1, bf16[2048,512]{1,0:T(8,128)(2,1)} %grads_out.1), custom_call_target="tpu_custom_call" | custom-call | tf_op jit(solution)/shard_map/pallas_call | solution.py:357
  3.6 8.8 %collective-permute-start = (f32[1088,128]{1,0:T(8,128)S(1)}, f32[1088,128]{1,0:T(8,128)S(1)}, u32[]{:S(2)}, u32[]{:S(2)}) collective-permute-start(f32[1088,128]{1,0:T(8,128)S(1)} %get-tuple-element.20), channel_id=1, source_target_pairs={{0,16},{16,0},{32,48},{48,32},{64,80},{80,64},{96,112},{112,96},{1... | collective-permute-start | bytes 1671176 | tf_op jit(solution)/shard_map/factors/ppermute | solution.py:298
  12.4 1.9 %collective-permute-start.2 = (f32[1088,128]{1,0:T(8,128)S(1)}, f32[1088,128]{1,0:T(8,128)S(1)}, u32[]{:S(2)}, u32[]{:S(2)}) collective-permute-start(f32[1088,128]{1,0:T(8,128)S(1)} %get-tuple-element.24), channel_id=1, source_target_pairs={{0,16},{16,0},{32,48},{48,32},{64,80},{80,64},{96,112},{112,96},{1... | collective-permute-start | bytes 1671176 | tf_op jit(solution)/shard_map/grad/ppermute | solution.py:298
  14.4 0.0 collective-permute-done.received
  14.4 0.1 shard_map.38
  14.4 1.9 %collective-permute-start.1 = (f32[544,128]{1,0:T(8,128)S(1)}, f32[544,128]{1,0:T(8,128)S(1)}, u32[]{:S(2)}, u32[]{:S(2)}) collective-permute-start(f32[544,128]{1,0:T(8,128)S(1)} %get-tuple-element.23), channel_id=1, source_target_pairs={{0,496},{16,32},{48,64},{32,16},{64,48},{80,96},{112,128},{96,80},... | collective-permute-start | bytes 835592 | tf_op jit(solution)/shard_map/factors/ppermute | solution.py:298
  16.4 0.0 collective-permute-done.2.received
  16.4 0.1 shard_map.39
  16.5 3.6 %collective-permute-start.4 = (f32[544,128]{1,0:T(8,128)S(1)}, f32[544,128]{1,0:T(8,128)S(1)}, u32[]{:S(2)}, u32[]{:S(2)}) collective-permute-start(f32[544,128]{1,0:T(8,128)S(1)} %get-tuple-element.28), channel_id=1, source_target_pairs={{0,496},{16,32},{48,64},{32,16},{64,48},{80,96},{112,128},{96,80},... | collective-permute-start | bytes 835592 | tf_op jit(solution)/shard_map/grad/ppermute | solution.py:298
  20.1 2.5 %collective-permute-done.1.received = f32[544,128]{1,0:T(8,128)S(1)} collective-permute-done((f32[544,128]{1,0:T(8,128)S(1)}, f32[544,128]{1,0:T(8,128)S(1)}, u32[]{:S(2)}, u32[]{:S(2)}) %collective-permute-start.1) | collective-permute-done | bytes 278560 | tf_op jit(solution)/shard_map/factors/ppermute | solution.py:298
  22.6 5.8 %collective-permute-start.3 = (f32[272,128]{1,0:T(8,128)S(1)}, f32[272,128]{1,0:T(8,128)S(1)}, u32[]{:S(2)}, u32[]{:S(2)}) collective-permute-start(f32[272,128]{1,0:T(8,128)S(1)} %get-tuple-element.27), channel_id=1, source_target_pairs={{0,48},{16,480},{48,0},{32,80},{64,112},{80,32},{112,64},{96,144},... | collective-permute-start | bytes 417800 | tf_op jit(solution)/shard_map/factors/ppermute | solution.py:298
  28.5 0.0 collective-permute-done.4.received
  28.5 2.9 %collective-permute-start.6 = (f32[272,128]{1,0:T(8,128)S(1)}, f32[272,128]{1,0:T(8,128)S(1)}, u32[]{:S(2)}, u32[]{:S(2)}) collective-permute-start(f32[272,128]{1,0:T(8,128)S(1)} %get-tuple-element.30), channel_id=1, source_target_pairs={{0,48},{16,480},{48,0},{32,80},{64,112},{80,32},{112,64},{96,144},... | collective-permute-start | bytes 417800 | tf_op jit(solution)/shard_map/grad/ppermute | solution.py:298
  31.5 0.0 collective-permute-done.3.received
  31.5 1.9 %collective-permute-start.5 = (f32[272,128]{1,0:T(8,128)S(1)}, f32[272,128]{1,0:T(8,128)S(1)}, u32[]{:S(2)}, u32[]{:S(2)}) collective-permute-start(f32[272,128]{1,0:T(8,128)S(1)} %shard_map.42.after.own), channel_id=1, source_target_pairs={{0,432},{16,96},{48,128},{32,464},{64,496},{80,160},{112,192},{96,... | collective-permute-start | bytes 417800 | tf_op jit(solution)/shard_map/factors/ppermute | solution.py:298
  33.4 2.7 %collective-permute-done.6.received = f32[272,128]{1,0:T(8,128)S(1)} collective-permute-done((f32[272,128]{1,0:T(8,128)S(1)}, f32[272,128]{1,0:T(8,128)S(1)}, u32[]{:S(2)}, u32[]{:S(2)}) %collective-permute-start.6) | collective-permute-done | bytes 139296 | tf_op jit(solution)/shard_map/grad/ppermute | solution.py:298
  36.1 2.8 %collective-permute-start.8 = (f32[272,128]{1,0:T(8,128)S(1)}, f32[272,128]{1,0:T(8,128)S(1)}, u32[]{:S(2)}, u32[]{:S(2)}) collective-permute-start(f32[272,128]{1,0:T(8,128)S(1)} %shard_map.43.after.own), channel_id=1, source_target_pairs={{0,432},{16,96},{48,128},{32,464},{64,496},{80,160},{112,192},{96,... | collective-permute-start | bytes 417800 | tf_op jit(solution)/shard_map/grad/ppermute | solution.py:298
  38.9 1.2 %collective-permute-done.5.received = f32[272,128]{1,0:T(8,128)S(1)} collective-permute-done((f32[272,128]{1,0:T(8,128)S(1)}, f32[272,128]{1,0:T(8,128)S(1)}, u32[]{:S(2)}, u32[]{:S(2)}) %collective-permute-start.5) | collective-permute-done | bytes 139296 | tf_op jit(solution)/shard_map/factors/ppermute | solution.py:298
  40.1 9.3 %collective-permute-start.7 = (f32[272,128]{1,0:T(8,128)S(1)}, f32[272,128]{1,0:T(8,128)S(1)}, u32[]{:S(2)}, u32[]{:S(2)}) collective-permute-start(f32[272,128]{1,0:T(8,128)S(1)} %shard_map.44.after.own), channel_id=1, source_target_pairs={{0,176},{16,352},{48,384},{32,208},{64,240},{80,416},{112,448},{96... | collective-permute-start | bytes 417800 | tf_op jit(solution)/shard_map/factors/ppermute | solution.py:298
  49.4 0.0 collective-permute-done.8.received
  49.5 2.9 %collective-permute-start.10 = (f32[272,128]{1,0:T(8,128)S(1)}, f32[272,128]{1,0:T(8,128)S(1)}, u32[]{:S(2)}, u32[]{:S(2)}) collective-permute-start(f32[272,128]{1,0:T(8,128)S(1)} %shard_map.45.after.own), channel_id=1, source_target_pairs={{0,176},{16,352},{48,384},{32,208},{64,240},{80,416},{112,448},{96... | collective-permute-start | bytes 417800 | tf_op jit(solution)/shard_map/grad/ppermute | solution.py:298
  52.4 0.5 collective-permute-done.7.received
  52.9 10.2 %collective-permute-start.9 = (f32[272,128]{1,0:T(8,128)S(1)}, f32[272,128]{1,0:T(8,128)S(1)}, u32[]{:S(2)}, u32[]{:S(2)}) collective-permute-start(f32[272,128]{1,0:T(8,128)S(1)} %shard_map.46.after.near), channel_id=1, source_target_pairs={{0,48},{16,480},{48,0},{32,80},{64,112},{80,32},{112,64},{96,144},... | collective-permute-start | bytes 417800 | tf_op jit(solution)/shard_map/factors/ppermute | solution.py:298
  63.1 1.5 %collective-permute-done.10.received = f32[272,128]{1,0:T(8,128)S(1)} collective-permute-done((f32[272,128]{1,0:T(8,128)S(1)}, f32[272,128]{1,0:T(8,128)S(1)}, u32[]{:S(2)}, u32[]{:S(2)}) %collective-permute-start.10) | collective-permute-done | bytes 139296 | tf_op jit(solution)/shard_map/grad/ppermute | solution.py:298
  64.5 3.8 %collective-permute-start.12 = (f32[272,128]{1,0:T(8,128)S(1)}, f32[272,128]{1,0:T(8,128)S(1)}, u32[]{:S(2)}, u32[]{:S(2)}) collective-permute-start(f32[272,128]{1,0:T(8,128)S(1)} %shard_map.47.after.near), channel_id=1, source_target_pairs={{0,48},{16,480},{48,0},{32,80},{64,112},{80,32},{112,64},{96,144},... | collective-permute-start | bytes 417800 | tf_op jit(solution)/shard_map/grad/ppermute | solution.py:298
  68.3 0.0 collective-permute-done.9.far
  68.4 2.0 %collective-permute-start.11 = (f32[544,128]{1,0:T(8,128)S(1)}, f32[544,128]{1,0:T(8,128)S(1)}, u32[]{:S(2)}, u32[]{:S(2)}) collective-permute-start(f32[544,128]{1,0:T(8,128)S(1)} %shard_map.48.after.near), channel_id=1, source_target_pairs={{0,496},{16,32},{48,64},{32,16},{64,48},{80,96},{112,128},{96,80},... | collective-permute-start | bytes 835592 | tf_op jit(solution)/shard_map/factors/ppermute | solution.py:298
  70.4 1.7 %collective-permute-done.12.far = f32[272,128]{1,0:T(8,128)S(1)} collective-permute-done((f32[272,128]{1,0:T(8,128)S(1)}, f32[272,128]{1,0:T(8,128)S(1)}, u32[]{:S(2)}, u32[]{:S(2)}) %collective-permute-start.12) | collective-permute-done | bytes 139296 | tf_op jit(solution)/shard_map/grad/ppermute | solution.py:298
  72.2 1.9 %collective-permute-start.13 = (f32[544,128]{1,0:T(8,128)S(1)}, f32[544,128]{1,0:T(8,128)S(1)}, u32[]{:S(2)}, u32[]{:S(2)}) collective-permute-start(f32[544,128]{1,0:T(8,128)S(1)} %shard_map.49.after.near), channel_id=1, source_target_pairs={{0,496},{16,32},{48,64},{32,16},{64,48},{80,96},{112,128},{96,80},... | collective-permute-start | bytes 835592 | tf_op jit(solution)/shard_map/grad/ppermute | solution.py:298
  74.1 2.5 %collective-permute-done.11.far = f32[544,128]{1,0:T(8,128)S(1)} collective-permute-done((f32[544,128]{1,0:T(8,128)S(1)}, f32[544,128]{1,0:T(8,128)S(1)}, u32[]{:S(2)}, u32[]{:S(2)}) %collective-permute-start.11) | collective-permute-done | bytes 278560 | tf_op jit(solution)/shard_map/factors/ppermute | solution.py:298
  76.5 3.5 %shard_map.50.x = f32[512,512]{1,0:T(8,128)S(1)} custom-call(f32[544,128]{1,0:T(8,128)S(1)} %shard_map.48.after.near, f32[544,128]{1,0:T(8,128)S(1)} %collective-permute-done.11.far, f32[544,128]{1,0:T(8,128)S(1)} %shard_map.49.after.near), custom_call_target="tpu_custom_call" | custom-call | bytes 1 | tf_op jit(solution)/shard_map/pallas_call | solution.py:286
  80.1 4.3 %collective-permute-start.15 = (f32[512,512]{1,0:T(8,128)S(1)}, f32[512,512]{1,0:T(8,128)S(1)}, u32[]{:S(2)}, u32[]{:S(2)}) collective-permute-start(f32[512,512]{1,0:T(8,128)S(1)} %shard_map.50.x), channel_id=1, source_target_pairs={{0,16},{16,0},{32,48},{48,32},{64,80},{80,64},{96,112},{112,96},{1... | collective-permute-start | bytes 3145736 | tf_op jit(solution)/shard_map/root/ppermute | solution.py:298
  84.4 0.0 collective-permute-done.13.far
  84.4 1.9 %collective-permute-start.14 = (f32[1088,128]{1,0:T(8,128)S(1)}, f32[1088,128]{1,0:T(8,128)S(1)}, u32[]{:S(2)}, u32[]{:S(2)}) collective-permute-start(f32[1088,128]{1,0:T(8,128)S(1)} %shard_map.51.own), channel_id=1, source_target_pairs={{0,16},{16,0},{32,48},{48,32},{64,80},{80,64},{96,112},{112,96},{1... | collective-permute-start | bytes 1671176 | tf_op jit(solution)/shard_map/grad/ppermute | solution.py:298
  86.4 0.7 shard_map.52.begun
  87.1 0.0 copy-start
  87.1 1.2 %collective-permute-done.14.other = f32[1088,128]{1,0:T(8,128)S(1)} collective-permute-done((f32[1088,128]{1,0:T(8,128)S(1)}, f32[1088,128]{1,0:T(8,128)S(1)}, u32[]{:S(2)}, u32[]{:S(2)}) %collective-permute-start.14) | collective-permute-done | bytes 557088 | tf_op jit(solution)/shard_map/grad/ppermute | solution.py:298
  88.3 0.8 shard_map.53
  89.1 0.0 collective-permute-done.15.x
  89.1 0.0 copy-done
  89.1 2.0 %shard_map.54 = f32[16,8,128]{2,1,0:T(8,128)S(1)} custom-call(s32[32]{0:T(128)S(1)} %copy-done, bf16[512,512]{1,0:T(8,128)(2,1)S(1)} %get-tuple-element.31.high, bf16[512,512]{1,0:T(8,128)(2,1)S(1)} %get-tuple-element.32.low, f32[512,512]{1,0:T(8,128)S(1)} %collective-permute-done.15.x), custom_call_target="tpu_custom_call" | custom-call | tf_op jit(solution)/shard_map/pallas_call | solution.py:286
  91.2 13.0 %all_to_all.5.tiles = f32[16,8,128]{2,1,0:T(8,128)S(1)} all-to-all(f32[16,8,128]{2,1,0:T(8,128)S(1)} %shard_map.54), channel_id=1, replica_groups=mesh['dp'=32,'mp'=16] {'mp'}, dimensions={0} | all-to-all | bytes 131072 | tf_op jit(solution)/shard_map/all_to_all | solution.py:377
  104.2 0.7 shard_map.55
  (11 shorter events, 0.2 us)
Async XLA Ops:
  3.6 10.7 %collective-permute-start = (f32[1088,128]{1,0:T(8,128)S(1)}, f32[1088,128]{1,0:T(8,128)S(1)}, u32[]{:S(2)}, u32[]{:S(2)}) collective-permute-start(f32[1088,128]{1,0:T(8,128)S(1)} %get-tuple-element.20), channel_id=1, source_target_pairs={{0,16},{16,0},{32,48},{48,32},{64,80},{80,64},{96,112},{112,96},{1... | collective-permute-start | bytes 1671176 | tf_op jit(solution)/shard_map/factors/ppermute | solution.py:298
  12.4 3.9 %collective-permute-start.2 = (f32[1088,128]{1,0:T(8,128)S(1)}, f32[1088,128]{1,0:T(8,128)S(1)}, u32[]{:S(2)}, u32[]{:S(2)}) collective-permute-start(f32[1088,128]{1,0:T(8,128)S(1)} %get-tuple-element.24), channel_id=1, source_target_pairs={{0,16},{16,0},{32,48},{48,32},{64,80},{80,64},{96,112},{112,96},{1... | collective-permute-start | bytes 1671176 | tf_op jit(solution)/shard_map/grad/ppermute | solution.py:298
  14.4 8.2 %collective-permute-start.1 = (f32[544,128]{1,0:T(8,128)S(1)}, f32[544,128]{1,0:T(8,128)S(1)}, u32[]{:S(2)}, u32[]{:S(2)}) collective-permute-start(f32[544,128]{1,0:T(8,128)S(1)} %get-tuple-element.23), channel_id=1, source_target_pairs={{0,496},{16,32},{48,64},{32,16},{64,48},{80,96},{112,128},{96,80},... | collective-permute-start | bytes 835592 | tf_op jit(solution)/shard_map/factors/ppermute | solution.py:298
  16.5 12.0 %collective-permute-start.4 = (f32[544,128]{1,0:T(8,128)S(1)}, f32[544,128]{1,0:T(8,128)S(1)}, u32[]{:S(2)}, u32[]{:S(2)}) collective-permute-start(f32[544,128]{1,0:T(8,128)S(1)} %get-tuple-element.28), channel_id=1, source_target_pairs={{0,496},{16,32},{48,64},{32,16},{64,48},{80,96},{112,128},{96,80},... | collective-permute-start | bytes 835592 | tf_op jit(solution)/shard_map/grad/ppermute | solution.py:298
  22.6 8.8 %collective-permute-start.3 = (f32[272,128]{1,0:T(8,128)S(1)}, f32[272,128]{1,0:T(8,128)S(1)}, u32[]{:S(2)}, u32[]{:S(2)}) collective-permute-start(f32[272,128]{1,0:T(8,128)S(1)} %get-tuple-element.27), channel_id=1, source_target_pairs={{0,48},{16,480},{48,0},{32,80},{64,112},{80,32},{112,64},{96,144},... | collective-permute-start | bytes 417800 | tf_op jit(solution)/shard_map/factors/ppermute | solution.py:298
  28.5 7.6 %collective-permute-start.6 = (f32[272,128]{1,0:T(8,128)S(1)}, f32[272,128]{1,0:T(8,128)S(1)}, u32[]{:S(2)}, u32[]{:S(2)}) collective-permute-start(f32[272,128]{1,0:T(8,128)S(1)} %get-tuple-element.30), channel_id=1, source_target_pairs={{0,48},{16,480},{48,0},{32,80},{64,112},{80,32},{112,64},{96,144},... | collective-permute-start | bytes 417800 | tf_op jit(solution)/shard_map/grad/ppermute | solution.py:298
  31.5 8.6 %collective-permute-start.5 = (f32[272,128]{1,0:T(8,128)S(1)}, f32[272,128]{1,0:T(8,128)S(1)}, u32[]{:S(2)}, u32[]{:S(2)}) collective-permute-start(f32[272,128]{1,0:T(8,128)S(1)} %shard_map.42.after.own), channel_id=1, source_target_pairs={{0,432},{16,96},{48,128},{32,464},{64,496},{80,160},{112,192},{96,... | collective-permute-start | bytes 417800 | tf_op jit(solution)/shard_map/factors/ppermute | solution.py:298
  36.1 13.3 %collective-permute-start.8 = (f32[272,128]{1,0:T(8,128)S(1)}, f32[272,128]{1,0:T(8,128)S(1)}, u32[]{:S(2)}, u32[]{:S(2)}) collective-permute-start(f32[272,128]{1,0:T(8,128)S(1)} %shard_map.43.after.own), channel_id=1, source_target_pairs={{0,432},{16,96},{48,128},{32,464},{64,496},{80,160},{112,192},{96,... | collective-permute-start | bytes 417800 | tf_op jit(solution)/shard_map/grad/ppermute | solution.py:298
  40.1 12.7 %collective-permute-start.7 = (f32[272,128]{1,0:T(8,128)S(1)}, f32[272,128]{1,0:T(8,128)S(1)}, u32[]{:S(2)}, u32[]{:S(2)}) collective-permute-start(f32[272,128]{1,0:T(8,128)S(1)} %shard_map.44.after.own), channel_id=1, source_target_pairs={{0,176},{16,352},{48,384},{32,208},{64,240},{80,416},{112,448},{96... | collective-permute-start | bytes 417800 | tf_op jit(solution)/shard_map/factors/ppermute | solution.py:298
  49.5 15.0 %collective-permute-start.10 = (f32[272,128]{1,0:T(8,128)S(1)}, f32[272,128]{1,0:T(8,128)S(1)}, u32[]{:S(2)}, u32[]{:S(2)}) collective-permute-start(f32[272,128]{1,0:T(8,128)S(1)} %shard_map.45.after.own), channel_id=1, source_target_pairs={{0,176},{16,352},{48,384},{32,208},{64,240},{80,416},{112,448},{96... | collective-permute-start | bytes 417800 | tf_op jit(solution)/shard_map/grad/ppermute | solution.py:298
  52.9 15.5 %collective-permute-start.9 = (f32[272,128]{1,0:T(8,128)S(1)}, f32[272,128]{1,0:T(8,128)S(1)}, u32[]{:S(2)}, u32[]{:S(2)}) collective-permute-start(f32[272,128]{1,0:T(8,128)S(1)} %shard_map.46.after.near), channel_id=1, source_target_pairs={{0,48},{16,480},{48,0},{32,80},{64,112},{80,32},{112,64},{96,144},... | collective-permute-start | bytes 417800 | tf_op jit(solution)/shard_map/factors/ppermute | solution.py:298
  64.5 7.6 %collective-permute-start.12 = (f32[272,128]{1,0:T(8,128)S(1)}, f32[272,128]{1,0:T(8,128)S(1)}, u32[]{:S(2)}, u32[]{:S(2)}) collective-permute-start(f32[272,128]{1,0:T(8,128)S(1)} %shard_map.47.after.near), channel_id=1, source_target_pairs={{0,48},{16,480},{48,0},{32,80},{64,112},{80,32},{112,64},{96,144},... | collective-permute-start | bytes 417800 | tf_op jit(solution)/shard_map/grad/ppermute | solution.py:298
  68.4 8.2 %collective-permute-start.11 = (f32[544,128]{1,0:T(8,128)S(1)}, f32[544,128]{1,0:T(8,128)S(1)}, u32[]{:S(2)}, u32[]{:S(2)}) collective-permute-start(f32[544,128]{1,0:T(8,128)S(1)} %shard_map.48.after.near), channel_id=1, source_target_pairs={{0,496},{16,32},{48,64},{32,16},{64,48},{80,96},{112,128},{96,80},... | collective-permute-start | bytes 835592 | tf_op jit(solution)/shard_map/factors/ppermute | solution.py:298
  72.2 12.2 %collective-permute-start.13 = (f32[544,128]{1,0:T(8,128)S(1)}, f32[544,128]{1,0:T(8,128)S(1)}, u32[]{:S(2)}, u32[]{:S(2)}) collective-permute-start(f32[544,128]{1,0:T(8,128)S(1)} %shard_map.49.after.near), channel_id=1, source_target_pairs={{0,496},{16,32},{48,64},{32,16},{64,48},{80,96},{112,128},{96,80},... | collective-permute-start | bytes 835592 | tf_op jit(solution)/shard_map/grad/ppermute | solution.py:298
  80.1 9.0 %collective-permute-start.15 = (f32[512,512]{1,0:T(8,128)S(1)}, f32[512,512]{1,0:T(8,128)S(1)}, u32[]{:S(2)}, u32[]{:S(2)}) collective-permute-start(f32[512,512]{1,0:T(8,128)S(1)} %shard_map.50.x), channel_id=1, source_target_pairs={{0,16},{16,0},{32,48},{48,32},{64,80},{80,64},{96,112},{112,96},{1... | collective-permute-start | bytes 3145736 | tf_op jit(solution)/shard_map/root/ppermute | solution.py:298
  84.4 3.9 %collective-permute-start.14 = (f32[1088,128]{1,0:T(8,128)S(1)}, f32[1088,128]{1,0:T(8,128)S(1)}, u32[]{:S(2)}, u32[]{:S(2)}) collective-permute-start(f32[1088,128]{1,0:T(8,128)S(1)} %shard_map.51.own), channel_id=1, source_target_pairs={{0,16},{16,0},{32,48},{48,32},{64,80},{80,64},{96,112},{112,96},{1... | collective-permute-start | bytes 1671176 | tf_op jit(solution)/shard_map/grad/ppermute | solution.py:298
  87.1 2.0 %copy-start = (s32[32]{0:T(128)S(1)}, s32[32]{0:T(128)}, u32[]{:S(2)}) copy-start(s32[32]{0:T(128)} %owner.1) | copy-start | bytes 388

commit v7 on v6

--- a/solution.py
+++ b/solution.py
@@ -213,7 +213,9 @@
     low = (-5.0 / 16.0 - 3125.0 * c) * m1 + (3125.0 * c) * m2 - (1250.0 * c) * m3
     diagonal = lax.broadcasted_iota(jnp.int32, (W, W), 0) == lax.broadcasted_iota(jnp.int32, (W, W), 1)
     low = low + jnp.where(diagonal, 25.0 / 16.0, 0.0)
-    x = low + product(split(m3), split(high))
+    cubed, rest = split(m3)
+    short = high.astype(jnp.bfloat16)
+    x = low + (dot(cubed, short) + dot(rest, short))
     out[...] = x * lax.rsqrt(jnp.sqrt(norm))
 
 

time: 105 us -> 105 us (level)
  no operation moved by 1% of the time
where the time goes in v7:
time: 105 us
  starting transfers between devices  66 us (63%)
  waiting for transfers between devices  13.8 us (13%)
  blocking collectives  13 us (12%)
  Pallas kernels  11.5 us (11%)
    ppermute x16, starting transfers between devices, move(): return lax.ppermute(x, 'dp', PAIRS[step])  66 us
    ppermute x16, waiting for transfers between devices, move(): return lax.ppermute(x, 'dp', PAIRS[step])  13.8 us
    all_to_all x1, blocking collectives, per_device(): tiles = lax.all_to_all(tiles, 'mp', split_axis=0, concat_axis=0, tiled=True)  13 us
    pallas_call x18, Pallas kernels, call(): pl.pallas_call(kernel, out_shape=[jax.ShapeDtypeStruct(s, dtype) for s in...  7.89 us
    pallas_call x1, Pallas kernels, per_device(): pl.pallas_call(front, out_shape=[jax.ShapeDtypeStruct(whole, jnp.float32)...  3.63 us
  transfers between devices with their start and end apart: 16, of which 8 were waited for; matrix products, arithmetic and copies ran while one was open for 0% of the time, Pallas kernels for 5%

profile of v7, /device:TPU:1, one launch (start us, length us, event | category | flops | bytes accessed | tf_op | source)
XLA Modules:
  0.0 104.6 jit_solution(5603083587535101402)
XLA Ops:
  0.0 3.6 %shard_map.37 = (f32[1088,128]{1,0:T(8,128)S(1)}, f32[1088,128]{1,0:T(8,128)S(1)}, f32[1088,128]{1,0:T(8,128)S(1)}, f32[1088,128]{1,0:T(8,128)S(1)}) custom-call(bf16[2048,512]{1,0:T(8,128)(2,1)} %acts.1, bf16[2048,512]{1,0:T(8,128)(2,1)} %grads_out.1), custom_call_target="tpu_custom_call" | custom-call | tf_op jit(solution)/shard_map/pallas_call | solution.py:359
  3.6 8.8 %collective-permute-start = (f32[1088,128]{1,0:T(8,128)S(1)}, f32[1088,128]{1,0:T(8,128)S(1)}, u32[]{:S(2)}, u32[]{:S(2)}) collective-permute-start(f32[1088,128]{1,0:T(8,128)S(1)} %get-tuple-element.20), channel_id=1, source_target_pairs={{0,16},{16,0},{32,48},{48,32},{64,80},{80,64},{96,112},{112,96},{1... | collective-permute-start | bytes 1671176 | tf_op jit(solution)/shard_map/factors/ppermute | solution.py:300
  12.4 1.9 %collective-permute-start.2 = (f32[1088,128]{1,0:T(8,128)S(1)}, f32[1088,128]{1,0:T(8,128)S(1)}, u32[]{:S(2)}, u32[]{:S(2)}) collective-permute-start(f32[1088,128]{1,0:T(8,128)S(1)} %get-tuple-element.24), channel_id=1, source_target_pairs={{0,16},{16,0},{32,48},{48,32},{64,80},{80,64},{96,112},{112,96},{1... | collective-permute-start | bytes 1671176 | tf_op jit(solution)/shard_map/grad/ppermute | solution.py:300
  14.4 0.0 collective-permute-done.received
  14.4 0.1 shard_map.38
  14.4 1.9 %collective-permute-start.1 = (f32[544,128]{1,0:T(8,128)S(1)}, f32[544,128]{1,0:T(8,128)S(1)}, u32[]{:S(2)}, u32[]{:S(2)}) collective-permute-start(f32[544,128]{1,0:T(8,128)S(1)} %get-tuple-element.23), channel_id=1, source_target_pairs={{0,496},{16,32},{48,64},{32,16},{64,48},{80,96},{112,128},{96,80},... | collective-permute-start | bytes 835592 | tf_op jit(solution)/shard_map/factors/ppermute | solution.py:300
  16.4 0.0 collective-permute-done.2.received
  16.4 0.1 shard_map.39
  16.5 3.6 %collective-permute-start.4 = (f32[544,128]{1,0:T(8,128)S(1)}, f32[544,128]{1,0:T(8,128)S(1)}, u32[]{:S(2)}, u32[]{:S(2)}) collective-permute-start(f32[544,128]{1,0:T(8,128)S(1)} %get-tuple-element.28), channel_id=1, source_target_pairs={{0,496},{16,32},{48,64},{32,16},{64,48},{80,96},{112,128},{96,80},... | collective-permute-start | bytes 835592 | tf_op jit(solution)/shard_map/grad/ppermute | solution.py:300
  20.1 2.5 %collective-permute-done.1.received = f32[544,128]{1,0:T(8,128)S(1)} collective-permute-done((f32[544,128]{1,0:T(8,128)S(1)}, f32[544,128]{1,0:T(8,128)S(1)}, u32[]{:S(2)}, u32[]{:S(2)}) %collective-permute-start.1) | collective-permute-done | bytes 278560 | tf_op jit(solution)/shard_map/factors/ppermute | solution.py:300
  22.6 5.8 %collective-permute-start.3 = (f32[272,128]{1,0:T(8,128)S(1)}, f32[272,128]{1,0:T(8,128)S(1)}, u32[]{:S(2)}, u32[]{:S(2)}) collective-permute-start(f32[272,128]{1,0:T(8,128)S(1)} %get-tuple-element.27), channel_id=1, source_target_pairs={{0,48},{16,480},{48,0},{32,80},{64,112},{80,32},{112,64},{96,144},... | collective-permute-start | bytes 417800 | tf_op jit(solution)/shard_map/factors/ppermute | solution.py:300
  28.5 0.0 collective-permute-done.4.received
  28.5 2.9 %collective-permute-start.6 = (f32[272,128]{1,0:T(8,128)S(1)}, f32[272,128]{1,0:T(8,128)S(1)}, u32[]{:S(2)}, u32[]{:S(2)}) collective-permute-start(f32[272,128]{1,0:T(8,128)S(1)} %get-tuple-element.30), channel_id=1, source_target_pairs={{0,48},{16,480},{48,0},{32,80},{64,112},{80,32},{112,64},{96,144},... | collective-permute-start | bytes 417800 | tf_op jit(solution)/shard_map/grad/ppermute | solution.py:300
  31.5 0.0 collective-permute-done.3.received
  31.5 1.9 %collective-permute-start.5 = (f32[272,128]{1,0:T(8,128)S(1)}, f32[272,128]{1,0:T(8,128)S(1)}, u32[]{:S(2)}, u32[]{:S(2)}) collective-permute-start(f32[272,128]{1,0:T(8,128)S(1)} %shard_map.42.after.own), channel_id=1, source_target_pairs={{0,432},{16,96},{48,128},{32,464},{64,496},{80,160},{112,192},{96,... | collective-permute-start | bytes 417800 | tf_op jit(solution)/shard_map/factors/ppermute | solution.py:300
  33.4 2.7 %collective-permute-done.6.received = f32[272,128]{1,0:T(8,128)S(1)} collective-permute-done((f32[272,128]{1,0:T(8,128)S(1)}, f32[272,128]{1,0:T(8,128)S(1)}, u32[]{:S(2)}, u32[]{:S(2)}) %collective-permute-start.6) | collective-permute-done | bytes 139296 | tf_op jit(solution)/shard_map/grad/ppermute | solution.py:300
  36.1 2.8 %collective-permute-start.8 = (f32[272,128]{1,0:T(8,128)S(1)}, f32[272,128]{1,0:T(8,128)S(1)}, u32[]{:S(2)}, u32[]{:S(2)}) collective-permute-start(f32[272,128]{1,0:T(8,128)S(1)} %shard_map.43.after.own), channel_id=1, source_target_pairs={{0,432},{16,96},{48,128},{32,464},{64,496},{80,160},{112,192},{96,... | collective-permute-start | bytes 417800 | tf_op jit(solution)/shard_map/grad/ppermute | solution.py:300
  38.9 1.2 %collective-permute-done.5.received = f32[272,128]{1,0:T(8,128)S(1)} collective-permute-done((f32[272,128]{1,0:T(8,128)S(1)}, f32[272,128]{1,0:T(8,128)S(1)}, u32[]{:S(2)}, u32[]{:S(2)}) %collective-permute-start.5) | collective-permute-done | bytes 139296 | tf_op jit(solution)/shard_map/factors/ppermute | solution.py:300
  40.1 9.3 %collective-permute-start.7 = (f32[272,128]{1,0:T(8,128)S(1)}, f32[272,128]{1,0:T(8,128)S(1)}, u32[]{:S(2)}, u32[]{:S(2)}) collective-permute-start(f32[272,128]{1,0:T(8,128)S(1)} %shard_map.44.after.own), channel_id=1, source_target_pairs={{0,176},{16,352},{48,384},{32,208},{64,240},{80,416},{112,448},{96... | collective-permute-start | bytes 417800 | tf_op jit(solution)/shard_map/factors/ppermute | solution.py:300
  49.4 0.0 collective-permute-done.8.received
  49.5 2.9 %collective-permute-start.10 = (f32[272,128]{1,0:T(8,128)S(1)}, f32[272,128]{1,0:T(8,128)S(1)}, u32[]{:S(2)}, u32[]{:S(2)}) collective-permute-start(f32[272,128]{1,0:T(8,128)S(1)} %shard_map.45.after.own), channel_id=1, source_target_pairs={{0,176},{16,352},{48,384},{32,208},{64,240},{80,416},{112,448},{96... | collective-permute-start | bytes 417800 | tf_op jit(solution)/shard_map/grad/ppermute | solution.py:300
  52.4 0.5 collective-permute-done.7.received
  52.9 10.2 %collective-permute-start.9 = (f32[272,128]{1,0:T(8,128)S(1)}, f32[272,128]{1,0:T(8,128)S(1)}, u32[]{:S(2)}, u32[]{:S(2)}) collective-permute-start(f32[272,128]{1,0:T(8,128)S(1)} %shard_map.46.after.near), channel_id=1, source_target_pairs={{0,48},{16,480},{48,0},{32,80},{64,112},{80,32},{112,64},{96,144},... | collective-permute-start | bytes 417800 | tf_op jit(solution)/shard_map/factors/ppermute | solution.py:300
  63.1 1.5 %collective-permute-done.10.received = f32[272,128]{1,0:T(8,128)S(1)} collective-permute-done((f32[272,128]{1,0:T(8,128)S(1)}, f32[272,128]{1,0:T(8,128)S(1)}, u32[]{:S(2)}, u32[]{:S(2)}) %collective-permute-start.10) | collective-permute-done | bytes 139296 | tf_op jit(solution)/shard_map/grad/ppermute | solution.py:300
  64.5 3.8 %collective-permute-start.12 = (f32[272,128]{1,0:T(8,128)S(1)}, f32[272,128]{1,0:T(8,128)S(1)}, u32[]{:S(2)}, u32[]{:S(2)}) collective-permute-start(f32[272,128]{1,0:T(8,128)S(1)} %shard_map.47.after.near), channel_id=1, source_target_pairs={{0,48},{16,480},{48,0},{32,80},{64,112},{80,32},{112,64},{96,144},... | collective-permute-start | bytes 417800 | tf_op jit(solution)/shard_map/grad/ppermute | solution.py:300
  68.3 0.0 collective-permute-done.9.far
  68.4 2.0 %collective-permute-start.11 = (f32[544,128]{1,0:T(8,128)S(1)}, f32[544,128]{1,0:T(8,128)S(1)}, u32[]{:S(2)}, u32[]{:S(2)}) collective-permute-start(f32[544,128]{1,0:T(8,128)S(1)} %shard_map.48.after.near), channel_id=1, source_target_pairs={{0,496},{16,32},{48,64},{32,16},{64,48},{80,96},{112,128},{96,80},... | collective-permute-start | bytes 835592 | tf_op jit(solution)/shard_map/factors/ppermute | solution.py:300
  70.4 1.7 %collective-permute-done.12.far = f32[272,128]{1,0:T(8,128)S(1)} collective-permute-done((f32[272,128]{1,0:T(8,128)S(1)}, f32[272,128]{1,0:T(8,128)S(1)}, u32[]{:S(2)}, u32[]{:S(2)}) %collective-permute-start.12) | collective-permute-done | bytes 139296 | tf_op jit(solution)/shard_map/grad/ppermute | solution.py:300
  72.2 1.9 %collective-permute-start.13 = (f32[544,128]{1,0:T(8,128)S(1)}, f32[544,128]{1,0:T(8,128)S(1)}, u32[]{:S(2)}, u32[]{:S(2)}) collective-permute-start(f32[544,128]{1,0:T(8,128)S(1)} %shard_map.49.after.near), channel_id=1, source_target_pairs={{0,496},{16,32},{48,64},{32,16},{64,48},{80,96},{112,128},{96,80},... | collective-permute-start | bytes 835592 | tf_op jit(solution)/shard_map/grad/ppermute | solution.py:300
  74.1 2.5 %collective-permute-done.11.far = f32[544,128]{1,0:T(8,128)S(1)} collective-permute-done((f32[544,128]{1,0:T(8,128)S(1)}, f32[544,128]{1,0:T(8,128)S(1)}, u32[]{:S(2)}, u32[]{:S(2)}) %collective-permute-start.11) | collective-permute-done | bytes 278560 | tf_op jit(solution)/shard_map/factors/ppermute | solution.py:300
  76.5 3.2 %shard_map.50.x = f32[512,512]{1,0:T(8,128)S(1)} custom-call(f32[544,128]{1,0:T(8,128)S(1)} %shard_map.48.after.near, f32[544,128]{1,0:T(8,128)S(1)} %collective-permute-done.11.far, f32[544,128]{1,0:T(8,128)S(1)} %shard_map.49.after.near), custom_call_target="tpu_custom_call" | custom-call | bytes 1 | tf_op jit(solution)/shard_map/pallas_call | solution.py:288
  79.8 4.3 %collective-permute-start.15 = (f32[512,512]{1,0:T(8,128)S(1)}, f32[512,512]{1,0:T(8,128)S(1)}, u32[]{:S(2)}, u32[]{:S(2)}) collective-permute-start(f32[512,512]{1,0:T(8,128)S(1)} %shard_map.50.x), channel_id=1, source_target_pairs={{0,16},{16,0},{32,48},{48,32},{64,80},{80,64},{96,112},{112,96},{1... | collective-permute-start | bytes 3145736 | tf_op jit(solution)/shard_map/root/ppermute | solution.py:300
  84.1 0.0 collective-permute-done.13.far
  84.1 1.9 %collective-permute-start.14 = (f32[1088,128]{1,0:T(8,128)S(1)}, f32[1088,128]{1,0:T(8,128)S(1)}, u32[]{:S(2)}, u32[]{:S(2)}) collective-permute-start(f32[1088,128]{1,0:T(8,128)S(1)} %shard_map.51.own), channel_id=1, source_target_pairs={{0,16},{16,0},{32,48},{48,32},{64,80},{80,64},{96,112},{112,96},{1... | collective-permute-start | bytes 1671176 | tf_op jit(solution)/shard_map/grad/ppermute | solution.py:300
  86.0 0.7 shard_map.52.begun
  86.8 0.0 copy-start
  86.8 1.2 %collective-permute-done.14.other = f32[1088,128]{1,0:T(8,128)S(1)} collective-permute-done((f32[1088,128]{1,0:T(8,128)S(1)}, f32[1088,128]{1,0:T(8,128)S(1)}, u32[]{:S(2)}, u32[]{:S(2)}) %collective-permute-start.14) | collective-permute-done | bytes 557088 | tf_op jit(solution)/shard_map/grad/ppermute | solution.py:300
  88.0 0.8 shard_map.53
  88.8 0.0 collective-permute-done.15.x
  88.8 0.0 copy-done
  88.8 2.0 %shard_map.54 = f32[16,8,128]{2,1,0:T(8,128)S(1)} custom-call(s32[32]{0:T(128)S(1)} %copy-done, bf16[512,512]{1,0:T(8,128)(2,1)S(1)} %get-tuple-element.31.high, bf16[512,512]{1,0:T(8,128)(2,1)S(1)} %get-tuple-element.32.low, f32[512,512]{1,0:T(8,128)S(1)} %collective-permute-done.15.x), custom_call_target="tpu_custom_call" | custom-call | tf_op jit(solution)/shard_map/pallas_call | solution.py:288
  90.9 13.0 %all_to_all.5.tiles = f32[16,8,128]{2,1,0:T(8,128)S(1)} all-to-all(f32[16,8,128]{2,1,0:T(8,128)S(1)} %shard_map.54), channel_id=1, replica_groups=mesh['dp'=32,'mp'=16] {'mp'}, dimensions={0} | all-to-all | bytes 131072 | tf_op jit(solution)/shard_map/all_to_all | solution.py:379
  103.9 0.7 shard_map.55
  (11 shorter events, 0.2 us)
Async XLA Ops:
  3.6 10.7 %collective-permute-start = (f32[1088,128]{1,0:T(8,128)S(1)}, f32[1088,128]{1,0:T(8,128)S(1)}, u32[]{:S(2)}, u32[]{:S(2)}) collective-permute-start(f32[1088,128]{1,0:T(8,128)S(1)} %get-tuple-element.20), channel_id=1, source_target_pairs={{0,16},{16,0},{32,48},{48,32},{64,80},{80,64},{96,112},{112,96},{1... | collective-permute-start | bytes 1671176 | tf_op jit(solution)/shard_map/factors/ppermute | solution.py:300
  12.4 3.9 %collective-permute-start.2 = (f32[1088,128]{1,0:T(8,128)S(1)}, f32[1088,128]{1,0:T(8,128)S(1)}, u32[]{:S(2)}, u32[]{:S(2)}) collective-permute-start(f32[1088,128]{1,0:T(8,128)S(1)} %get-tuple-element.24), channel_id=1, source_target_pairs={{0,16},{16,0},{32,48},{48,32},{64,80},{80,64},{96,112},{112,96},{1... | collective-permute-start | bytes 1671176 | tf_op jit(solution)/shard_map/grad/ppermute | solution.py:300
  14.4 8.2 %collective-permute-start.1 = (f32[544,128]{1,0:T(8,128)S(1)}, f32[544,128]{1,0:T(8,128)S(1)}, u32[]{:S(2)}, u32[]{:S(2)}) collective-permute-start(f32[544,128]{1,0:T(8,128)S(1)} %get-tuple-element.23), channel_id=1, source_target_pairs={{0,496},{16,32},{48,64},{32,16},{64,48},{80,96},{112,128},{96,80},... | collective-permute-start | bytes 835592 | tf_op jit(solution)/shard_map/factors/ppermute | solution.py:300
  16.5 12.0 %collective-permute-start.4 = (f32[544,128]{1,0:T(8,128)S(1)}, f32[544,128]{1,0:T(8,128)S(1)}, u32[]{:S(2)}, u32[]{:S(2)}) collective-permute-start(f32[544,128]{1,0:T(8,128)S(1)} %get-tuple-element.28), channel_id=1, source_target_pairs={{0,496},{16,32},{48,64},{32,16},{64,48},{80,96},{112,128},{96,80},... | collective-permute-start | bytes 835592 | tf_op jit(solution)/shard_map/grad/ppermute | solution.py:300
  22.6 8.8 %collective-permute-start.3 = (f32[272,128]{1,0:T(8,128)S(1)}, f32[272,128]{1,0:T(8,128)S(1)}, u32[]{:S(2)}, u32[]{:S(2)}) collective-permute-start(f32[272,128]{1,0:T(8,128)S(1)} %get-tuple-element.27), channel_id=1, source_target_pairs={{0,48},{16,480},{48,0},{32,80},{64,112},{80,32},{112,64},{96,144},... | collective-permute-start | bytes 417800 | tf_op jit(solution)/shard_map/factors/ppermute | solution.py:300
  28.5 7.6 %collective-permute-start.6 = (f32[272,128]{1,0:T(8,128)S(1)}, f32[272,128]{1,0:T(8,128)S(1)}, u32[]{:S(2)}, u32[]{:S(2)}) collective-permute-start(f32[272,128]{1,0:T(8,128)S(1)} %get-tuple-element.30), channel_id=1, source_target_pairs={{0,48},{16,480},{48,0},{32,80},{64,112},{80,32},{112,64},{96,144},... | collective-permute-start | bytes 417800 | tf_op jit(solution)/shard_map/grad/ppermute | solution.py:300
  31.5 8.6 %collective-permute-start.5 = (f32[272,128]{1,0:T(8,128)S(1)}, f32[272,128]{1,0:T(8,128)S(1)}, u32[]{:S(2)}, u32[]{:S(2)}) collective-permute-start(f32[272,128]{1,0:T(8,128)S(1)} %shard_map.42.after.own), channel_id=1, source_target_pairs={{0,432},{16,96},{48,128},{32,464},{64,496},{80,160},{112,192},{96,... | collective-permute-start | bytes 417800 | tf_op jit(solution)/shard_map/factors/ppermute | solution.py:300
  36.1 13.3 %collective-permute-start.8 = (f32[272,128]{1,0:T(8,128)S(1)}, f32[272,128]{1,0:T(8,128)S(1)}, u32[]{:S(2)}, u32[]{:S(2)}) collective-permute-start(f32[272,128]{1,0:T(8,128)S(1)} %shard_map.43.after.own), channel_id=1, source_target_pairs={{0,432},{16,96},{48,128},{32,464},{64,496},{80,160},{112,192},{96,... | collective-permute-start | bytes 417800 | tf_op jit(solution)/shard_map/grad/ppermute | solution.py:300
  40.1 12.7 %collective-permute-start.7 = (f32[272,128]{1,0:T(8,128)S(1)}, f32[272,128]{1,0:T(8,128)S(1)}, u32[]{:S(2)}, u32[]{:S(2)}) collective-permute-start(f32[272,128]{1,0:T(8,128)S(1)} %shard_map.44.after.own), channel_id=1, source_target_pairs={{0,176},{16,352},{48,384},{32,208},{64,240},{80,416},{112,448},{96... | collective-permute-start | bytes 417800 | tf_op jit(solution)/shard_map/factors/ppermute | solution.py:300
  49.5 15.0 %collective-permute-start.10 = (f32[272,128]{1,0:T(8,128)S(1)}, f32[272,128]{1,0:T(8,128)S(1)}, u32[]{:S(2)}, u32[]{:S(2)}) collective-permute-start(f32[272,128]{1,0:T(8,128)S(1)} %shard_map.45.after.own), channel_id=1, source_target_pairs={{0,176},{16,352},{48,384},{32,208},{64,240},{80,416},{112,448},{96... | collective-permute-start | bytes 417800 | tf_op jit(solution)/shard_map/grad/ppermute | solution.py:300
  52.9 15.5 %collective-permute-start.9 = (f32[272,128]{1,0:T(8,128)S(1)}, f32[272,128]{1,0:T(8,128)S(1)}, u32[]{:S(2)}, u32[]{:S(2)}) collective-permute-start(f32[272,128]{1,0:T(8,128)S(1)} %shard_map.46.after.near), channel_id=1, source_target_pairs={{0,48},{16,480},{48,0},{32,80},{64,112},{80,32},{112,64},{96,144},... | collective-permute-start | bytes 417800 | tf_op jit(solution)/shard_map/factors/ppermute | solution.py:300
  64.5 7.6 %collective-permute-start.12 = (f32[272,128]{1,0:T(8,128)S(1)}, f32[272,128]{1,0:T(8,128)S(1)}, u32[]{:S(2)}, u32[]{:S(2)}) collective-permute-start(f32[272,128]{1,0:T(8,128)S(1)} %shard_map.47.after.near), channel_id=1, source_target_pairs={{0,48},{16,480},{48,0},{32,80},{64,112},{80,32},{112,64},{96,144},... | collective-permute-start | bytes 417800 | tf_op jit(solution)/shard_map/grad/ppermute | solution.py:300
  68.4 8.2 %collective-permute-start.11 = (f32[544,128]{1,0:T(8,128)S(1)}, f32[544,128]{1,0:T(8,128)S(1)}, u32[]{:S(2)}, u32[]{:S(2)}) collective-permute-start(f32[544,128]{1,0:T(8,128)S(1)} %shard_map.48.after.near), channel_id=1, source_target_pairs={{0,496},{16,32},{48,64},{32,16},{64,48},{80,96},{112,128},{96,80},... | collective-permute-start | bytes 835592 | tf_op jit(solution)/shard_map/factors/ppermute | solution.py:300
  72.2 11.9 %collective-permute-start.13 = (f32[544,128]{1,0:T(8,128)S(1)}, f32[544,128]{1,0:T(8,128)S(1)}, u32[]{:S(2)}, u32[]{:S(2)}) collective-permute-start(f32[544,128]{1,0:T(8,128)S(1)} %shard_map.49.after.near), channel_id=1, source_target_pairs={{0,496},{16,32},{48,64},{32,16},{64,48},{80,96},{112,128},{96,80},... | collective-permute-start | bytes 835592 | tf_op jit(solution)/shard_map/grad/ppermute | solution.py:300
  79.8 9.0 %collective-permute-start.15 = (f32[512,512]{1,0:T(8,128)S(1)}, f32[512,512]{1,0:T(8,128)S(1)}, u32[]{:S(2)}, u32[]{:S(2)}) collective-permute-start(f32[512,512]{1,0:T(8,128)S(1)} %shard_map.50.x), channel_id=1, source_target_pairs={{0,16},{16,0},{32,48},{48,32},{64,80},{80,64},{96,112},{112,96},{1... | collective-permute-start | bytes 3145736 | tf_op jit(solution)/shard_map/root/ppermute | solution.py:300
  84.1 3.9 %collective-permute-start.14 = (f32[1088,128]{1,0:T(8,128)S(1)}, f32[1088,128]{1,0:T(8,128)S(1)}, u32[]{:S(2)}, u32[]{:S(2)}) collective-permute-start(f32[1088,128]{1,0:T(8,128)S(1)} %shard_map.51.own), channel_id=1, source_target_pairs={{0,16},{16,0},{32,48},{48,32},{64,80},{80,64},{96,112},{112,96},{1... | collective-permute-start | bytes 1671176 | tf_op jit(solution)/shard_map/grad/ppermute | solution.py:300
  86.8 2.0 %copy-start = (s32[32]{0:T(128)S(1)}, s32[32]{0:T(128)}, u32[]{:S(2)}) copy-start(s32[32]{0:T(128)} %owner.1) | copy-start | bytes 388
